TPU v7x, 32 devices: a whole 2x2x4 slice. The times are simulated.
32 devices in a mesh: silo: 16 (over z, y, core), shard: 2 (over x).
Axes of the slice: x: 2, y: 2, z: 4, core: 2. Of those that a mesh axis runs over, the one named last changes fastest.
Arguments:
- activ: bfloat16 [32768, 1280], P(('silo', 'shard')), may hold values from -6 to 6
- cotangent: bfloat16 [32768, 640], P(('silo', 'shard')), may hold values from -6 to 6
- error_memory: float32 [16, 2, 3200, 256], P('silo', 'shard'), may hold values from -5 to 5
- params: float32 [16, 640, 1280], P('silo', 'shard'), may hold values from -6 to 6
- estimate: float32 [16, 640, 1280], P('silo', 'shard'), may hold values from -6 to 6
- mixed: float32 [16, 640, 1280], P('silo', 'shard'), may hold values from -6 to 6
- kept_blocks: int32 [16, 2, 2, 64], P('silo'), may hold values from 0 to 1599, as said below
- kept_counts: int32 [16, 2, 2], P('silo'), may hold values from 1 to 64, as said below
- gossip_blocks: int32 [16, 2, 128], P(None, 'shard'), may hold values from 0 to 1599, as said below
- gossip_counts: int32 [16, 2], P(None, 'shard'), may hold values from 1 to 128, as said below
Outputs:
- params_out: float32 [16, 640, 1280], P('silo', 'shard')
- estimate_out: float32 [16, 640, 1280], P('silo', 'shard')
- mixed_out: float32 [16, 640, 1280], P('silo', 'shard')
- error_out: float32 [16, 2, 3200, 256], P('silo', 'shard')
Inputs may be any that keep to these rules, and one draw needn't show every extreme that they name: `kept_blocks`: for each silo, sender and owner the 64 entries are distinct. In every silo some owner has kept_counts equal to 64 from every sender. `kept_counts`: in every silo one owner receives 64 from every device of the silo. `gossip_blocks`: for each silo and owner the 128 entries are distinct. `gossip_counts`: for every owner some silo gossips 128 blocks.
All inputs are finite; a program needn't handle non-finite values.
Results may differ from a plain program's by a relative error of at most 0.0003.
Values sent between devices are 32-bit elements; how exact they have to be, the bound alone decides.
No kernel may reach another device: no remote copies, remote signals or barrier semaphores. Data moves between devices by JAX's collectives and lax.ppermute only.
A program may use at most 64 MiB of HBM per device.

v0:
```python
import jax
import jax.numpy as jnp
from jax import lax
from jax.sharding import PartitionSpec as P

LEARN_RATE = 0.25
CONSENSUS = 0.5
MIX_WEIGHT = 1.0 / 3.0


def shifted(value, axis, steps):
    count = lax.axis_size(axis)
    pairs = [(source, (source + steps) % count) for source in range(count)]
    return lax.ppermute(value, axis, pairs)


def body(
    activ,
    cotangent,
    error_memory,
    params,
    estimate,
    mixed,
    kept_blocks,
    kept_counts,
    gossip_blocks,
    gossip_counts,
):
    shards = lax.axis_size("shard")
    my_shard = lax.axis_index("shard")
    my_silo = lax.axis_index("silo")
    width_in = activ.shape[1]
    block_len = error_memory.shape[3]
    nblocks = error_memory.shape[2]
    own_blocks = nblocks // shards
    slot_count = kept_blocks.shape[3]
    gossip_slots = gossip_blocks.shape[2]
    scale_in = width_in ** (-0.5)
    grad_local = (
        lax.dot_general(
            cotangent, activ, (((0,), (0,)), ((), ())), preferred_element_type=jnp.float32
        )
        * scale_in
    )
    pending = error_memory[0, 0] + grad_local.reshape(nblocks, block_len)
    my_lists = kept_blocks[0][my_shard]
    my_counts = kept_counts[0][my_shard]
    offsets = (jnp.arange(shards, dtype=jnp.int32) * own_blocks)[:, None]
    global_ids = my_lists + offsets
    filled = jnp.arange(slot_count, dtype=jnp.int32)[None, :] < my_counts[:, None]
    chosen = (
        jnp.zeros((nblocks,), jnp.int32)
        .at[global_ids.reshape(-1)]
        .max(filled.astype(jnp.int32).reshape(-1))
    )
    keep_mask = chosen[:, None] > 0
    error_new = jnp.where(keep_mask, jnp.float32(0.0), pending)
    slot_rows = jnp.where(filled[:, :, None], pending[global_ids], jnp.float32(0.0))
    arrived = lax.all_to_all(slot_rows, "shard", split_axis=0, concat_axis=0, tiled=True)
    source_lists = kept_blocks[0][:, my_shard]
    own_grad = (
        jnp.zeros((own_blocks, block_len), jnp.float32)
        .at[source_lists.reshape(-1)]
        .add(arrived.reshape(-1, block_len))
    )
    weights = params[0].reshape(own_blocks, block_len)
    half_step = weights - LEARN_RATE * own_grad
    old_estimate = estimate[0].reshape(own_blocks, block_len)
    drift = half_step - old_estimate
    silo_lists = gossip_blocks[:, 0]
    silo_counts = gossip_counts[:, 0]
    my_blocks = silo_lists[my_silo]
    gossip_filled = jnp.arange(gossip_slots, dtype=jnp.int32) < silo_counts[my_silo]
    delta_rows = jnp.where(gossip_filled[:, None], drift[my_blocks], jnp.float32(0.0))
    delta_dense = jnp.zeros_like(drift).at[my_blocks].set(delta_rows)
    estimate_new = old_estimate + delta_dense
    silo_count = lax.axis_size("silo")
    from_lower = shifted(delta_rows, "silo", 1)
    from_upper = shifted(delta_rows, "silo", -1)
    lower_silo = (my_silo - 1) % silo_count
    upper_silo = (my_silo + 1) % silo_count
    spread = (
        delta_dense.at[silo_lists[lower_silo]]
        .add(from_lower)
        .at[silo_lists[upper_silo]]
        .add(from_upper)
    )
    mixed_new = mixed[0].reshape(own_blocks, block_len) + MIX_WEIGHT * spread
    params_new = half_step + CONSENSUS * (mixed_new - estimate_new)
    return (
        params_new.reshape(params.shape),
        estimate_new.reshape(estimate.shape),
        mixed_new.reshape(mixed.shape),
        error_new.reshape(error_memory.shape),
    )


def solution(mesh):
    in_specs = (
        P(("silo", "shard"), None),
        P(("silo", "shard"), None),
        P("silo", "shard", None, None),
        P("silo", "shard", None),
        P("silo", "shard", None),
        P("silo", "shard", None),
        P("silo", None, None, None),
        P("silo", None, None),
        P(None, "shard", None),
        P(None, "shard"),
    )
    out_specs = (
        P("silo", "shard", None),
        P("silo", "shard", None),
        P("silo", "shard", None),
        P("silo", "shard", None, None),
    )
    return jax.shard_map(body, mesh=mesh, in_specs=in_specs, out_specs=out_specs, check_vma=False)
```

profile of v0, /device:TPU:0, one launch (start us, length us, event | category | flops | bytes accessed | tf_op | source)
XLA Modules:
  0.0 86.9 jit_solution(18286464634709459039)
XLA Ops:
  0.7 0.9 %compare_select_fusion = (s32[2,64,1]{1,0,2:T(2,128)S(1)}, s32[1,1,2,64]{3,2,1,0:T(2,128)S(1)}) fusion(s32[2]{0:T(128)S(1)} %iota_multiply_fusion, s32[1,2,2,64]{3,2,1,0:T(2,128)} %param.16, s32[]{:T(128)S(6)} %select_n.100), kind=kLoop, calls=%fused_computation.25 | loop fusion | flops 512 | bytes 1548 | tf_op jit(solution)/shard_map/select_n | solution.py:58
  2.4 4.9 %convolution_multiply_fusion = f32[640,1280]{1,0:T(8,128)} fusion(bf16[1024,640]{1,0:T(8,128)(2,1)} %param.11, bf16[1024,1280]{1,0:T(8,128)(2,1)S(1)} %copy-done), kind=kOutput, calls=%fused_computation.7 | convolution fusion | flops 1678540800 | bytes 7208960 | tf_op jit(solution)/shard_map/dot_general | solution.py:40
  7.3 4.9 %reshape.267 = f32[3200,256]{1,0:T(8,128)} reshape(f32[640,1280]{1,0:T(8,128)} %convolution_multiply_fusion) | data formatting | bytes 6553600 | tf_op jit(solution)/shard_map/reshape | solution.py:45
  12.3 5.0 %bitcast_add_fusion = f32[3200,256]{1,0:T(8,128)} fusion(f32[3200,256]{1,0:T(8,128)} %reshape.267, f32[1,1,3200,256]{3,2,1,0:T(8,128)} %param.12), kind=kLoop, calls=%fused_computation.8 | loop fusion | flops 819200 | bytes 9830400 | tf_op jit(solution)/shard_map/add | solution.py:45
  17.3 2.7 %gather_fusion = f32[128,256]{1,0:T(8,128)S(1)} fusion(f32[3200,256]{1,0:T(8,128)} %bitcast_add_fusion, s32[1024]{0:T(1024)S(1)} %pad_clamp_fusion.1), kind=kCustom, calls=%fused_computation | custom fusion | bytes 262656 | tf_op jit(solution)/shard_map/gather | solution.py:58
  20.7 4.2 %all-to-all-start = ((f32[2,64,256]{2,1,0:T(8,128)}), f32[2,64,256]{2,1,0:T(8,128)S(1)}, u32[]{:S(2)}, u32[]{:S(2)}) async-start(f32[2,64,256]{2,1,0:T(8,128)} %broadcast_select_fusion.1), calls=%async_computation | async-start | bytes 262144 | tf_op jit(solution)/shard_map/all_to_all | solution.py:59
  25.0 4.9 %reshape.272 = f32[1,1,3200,256]{3,2,1,0:T(8,128)} reshape(f32[640,1280]{1,0:T(8,128)} %convolution_multiply_fusion) | data formatting | bytes 6553600 | tf_op jit(solution)/shard_map/reshape | solution.py:45
  30.9 2.7 %reshape_squeeze.12 = f32[1600,256]{1,0:T(8,128)} reshape(f32[1,320,1280]{2,1,0:T(8,128)} %param.13) | data formatting | bytes 3276800 | tf_op jit(solution)/shard_map/reshape;squeeze | solution.py:66
  33.6 2.7 %reshape_squeeze.15 = f32[1600,256]{1,0:T(8,128)} reshape(f32[1,320,1280]{2,1,0:T(8,128)} %param.14) | data formatting | bytes 3276800 | tf_op jit(solution)/shard_map/reshape;squeeze | solution.py:68
  36.9 1.3 %scatter_custom_fusion.4 = s32[3200]{0:T(1024)S(1)} fusion(s32[128]{0:T(128)S(1)} %get-tuple-element.14, s32[128]{0:T(128)S(1)} %reshape.326, s32[]{:T(128)} %constant.46.clone.1), kind=kCustom, calls=%fused_computation.21 | custom fusion | flops 128 | bytes 12804 | tf_op jit(solution)/shard_map/scatter-max | solution.py:54
  38.9 2.5 %scatter_custom_fusion = f32[1600,256]{1,0:T(8,128)} fusion(s32[128]{0:T(128)S(1)} %fusion.12, f32[128,256]{1,0:T(8,128)S(1)} %bitcast.44, f32[]{:T(128)} %constant.22.clone.1), kind=kCustom, calls=%fused_computation.15 | custom fusion | flops 32768 | bytes 1638404 | tf_op jit(solution)/shard_map/scatter-add | solution.py:64
  41.4 3.9 %fusion.4 = f32[1600,256]{1,0:T(8,128)} fusion(f32[1600,256]{1,0:T(8,128)} %reshape_squeeze.15, f32[1600,256]{1,0:T(8,128)} %reshape_squeeze.12, f32[1600,256]{1,0:T(8,128)} %scatter_custom_fusion), kind=kLoop, calls=%fused_computation.17 | loop fusion | flops 1228800 | bytes 6553600 | tf_op jit(solution)/shard_map/sub | solution.py:69
  45.3 2.2 %gather_fusion.1 = f32[128,256]{1,0:T(8,128)S(1)} fusion(f32[1600,256]{1,0:T(8,128)} %fusion.4, s32[1024]{0:T(1024)S(1)} %pad_clamp_fusion), kind=kCustom, calls=%fused_computation.1 | custom fusion | bytes 262656 | tf_op jit(solution)/shard_map/gather | solution.py:74
  47.6 4.7 %collective-permute-start.1 = (f32[128,256]{1,0:T(8,128)S(1)}, f32[128,256]{1,0:T(8,128)S(1)}, u32[]{:S(2)}, u32[]{:S(2)}) collective-permute-start(f32[128,256]{1,0:T(8,128)S(1)} %broadcast_select_fusion), channel_id=1, source_target_pairs={{0,30},{2,0},{4,2},{6,4},{8,6},{10,8},{12,10},{14,12},{16,14},{18,... | collective-permute-start | bytes 393224 | tf_op jit(solution)/shard_map/ppermute | solution.py:14
  52.3 4.9 %add_select_fusion = f32[1,1,3200,256]{3,2,1,0:T(8,128)} fusion(f32[1,1,3200,256]{3,2,1,0:T(8,128)} %param.12, f32[1,1,3200,256]{3,2,1,0:T(8,128)} %reshape.272, pred[3200]{0:T(1024)(128)(4,1)S(1)} %broadcast_compare_fusion), kind=kLoop, calls=%fused_computation.9 | loop fusion | flops 1638400 | bytes 9833600 | tf_op jit(solution)/shard_map/jit(_where)/select_n | solution.py:57
  57.2 2.7 %reshape_squeeze.14 = f32[1600,256]{1,0:T(8,128)} reshape(f32[1,320,1280]{2,1,0:T(8,128)} %param.15) | data formatting | bytes 3276800 | tf_op jit(solution)/shard_map/reshape;squeeze | solution.py:88
  59.9 2.3 %scatter_custom_fusion.1 = f32[1600,256]{1,0:T(8,128)} fusion(s32[128]{0:T(128)S(1)} %get-tuple-element.10, f32[]{:T(128)} %constant.22.clone.1, f32[128,256]{1,0:T(8,128)S(1)} %gather_fusion.1, pred[128]{0:T(512)(128)(4,1)S(1)} %iota_compare_fusion.1), kind=kCustom, calls=%fused_computation.13 | custom fusion | flops 32768 | bytes 1769988 | tf_op jit(solution)/shard_map/scatter | solution.py:75
  62.3 2.7 %copy.14 = f32[1600,256]{1,0:T(8,128)} copy(f32[1600,256]{1,0:T(8,128)} %scatter_custom_fusion.1) | data formatting | bytes 3276800
  65.0 3.7 %scatter_fusion = f32[1600,256]{1,0:T(8,128)} fusion(f32[1600,256]{1,0:T(8,128)} %copy.14, s32[128]{0:T(128)S(1)} %get-tuple-element.11, f32[128,256]{1,0:T(8,128)S(1)} %collective-permute-done), kind=kCustom, calls=%fused_computation.4 | custom fusion | flops 32768 | bytes 393728 | tf_op jit(solution)/shard_map/scatter-add | solution.py:84
  68.7 3.7 %scatter_fusion.1 = f32[1600,256]{1,0:T(8,128)} fusion(f32[1600,256]{1,0:T(8,128)} %scatter_fusion, s32[128]{0:T(128)S(1)} %get-tuple-element.9, f32[128,256]{1,0:T(8,128)S(1)} %collective-permute-done.1), kind=kCustom, calls=%fused_computation.5 | custom fusion | flops 32768 | bytes 393728 | tf_op jit(solution)/shard_map/scatter-add | solution.py:86
  72.5 6.3 %multiply_add_fusion = (f32[1600,256]{1,0:T(8,128)}, f32[1600,256]{1,0:T(8,128)}, f32[1600,256]{1,0:T(8,128)}) fusion(f32[1600,256]{1,0:T(8,128)} %reshape_squeeze.12, f32[1600,256]{1,0:T(8,128)} %scatter_custom_fusion, f32[1600,256]{1,0:T(8,128)} %reshape_squeeze.15, f32[1600,256]{1,0:T(8,128)} %scatter_custom_fusion.1, f32[1600,256]{1,0:T(8,128)} %reshape_squeeze.14, ...), kind=kLoop, calls=%fused_computation.10 | loop fusion | flops 3276800 | bytes 14745600 | tf_op jit(solution)/shard_map/add | solution.py:89
  78.8 2.7 %reshape.269 = f32[1,320,1280]{2,1,0:T(8,128)} reshape(f32[1600,256]{1,0:T(8,128)} %get-tuple-element.4) | data formatting | bytes 3276800 | tf_op jit(solution)/shard_map/reshape | solution.py:91
  81.5 2.7 %reshape.270 = f32[1,320,1280]{2,1,0:T(8,128)} reshape(f32[1600,256]{1,0:T(8,128)} %get-tuple-element.5) | data formatting | bytes 3276800 | tf_op jit(solution)/shard_map/reshape | solution.py:92
  84.2 2.7 %reshape.271 = f32[1,320,1280]{2,1,0:T(8,128)} reshape(f32[1600,256]{1,0:T(8,128)} %get-tuple-element.6) | data formatting | bytes 3276800 | tf_op jit(solution)/shard_map/reshape | solution.py:93
  (31 shorter events, 4.2 us)
Async XLA Ops:
  0.6 1.8 %copy-start = (bf16[1024,1280]{1,0:T(8,128)(2,1)S(1)}, bf16[1024,1280]{1,0:T(8,128)(2,1)}, u32[]{:S(2)}) copy-start(bf16[1024,1280]{1,0:T(8,128)(2,1)} %param.10) | copy-start | bytes 7864324
  7.3 4.9 %copy-start.2 = (s32[1,2,2]{2,1,0:T(2,128)S(1)}, s32[1,2,2]{2,1,0:T(2,128)}, u32[]{:S(2)}) copy-start(s32[1,2,2]{2,1,0:T(2,128)} %param.17) | copy-start | bytes 52
  17.3 7.6 %copy-start.1 = (s32[1,2,2,64]{3,2,1,0:T(2,128)S(1)}, s32[1,2,2,64]{3,2,1,0:T(2,128)}, u32[]{:S(2)}) copy-start(s32[1,2,2,64]{3,2,1,0:T(2,128)} %param.16) | copy-start | bytes 3076
  20.7 18.1 %all-to-all-start = ((f32[2,64,256]{2,1,0:T(8,128)}), f32[2,64,256]{2,1,0:T(8,128)S(1)}, u32[]{:S(2)}, u32[]{:S(2)}) async-start(f32[2,64,256]{2,1,0:T(8,128)} %broadcast_select_fusion.1), calls=%async_computation | async-start | bytes 262144 | tf_op jit(solution)/shard_map/all_to_all | solution.py:59
  33.6 2.7 %copy-start.3 = (s32[16,1]{0,1:T(1,128)S(1)}, s32[16,1]{0,1:T(1,128)}, u32[]{:S(2)}) copy-start(s32[16,1]{0,1:T(1,128)} %param.19) | copy-start | bytes 196
  47.5 17.4 %collective-permute-start = (f32[128,256]{1,0:T(8,128)S(1)}, f32[128,256]{1,0:T(8,128)S(1)}, u32[]{:S(2)}, u32[]{:S(2)}) collective-permute-start(f32[128,256]{1,0:T(8,128)S(1)} %broadcast_select_fusion), channel_id=1, source_target_pairs={{0,2},{2,4},{4,6},{6,8},{8,10},{10,12},{12,14},{14,16},{16,18},{18... | collective-permute-start | bytes 393224 | tf_op jit(solution)/shard_map/ppermute | solution.py:14
  47.6 21.1 %collective-permute-start.1 = (f32[128,256]{1,0:T(8,128)S(1)}, f32[128,256]{1,0:T(8,128)S(1)}, u32[]{:S(2)}, u32[]{:S(2)}) collective-permute-start(f32[128,256]{1,0:T(8,128)S(1)} %broadcast_select_fusion), channel_id=1, source_target_pairs={{0,30},{2,0},{4,2},{6,4},{8,6},{10,8},{12,10},{14,12},{16,14},{18,... | collective-permute-start | bytes 393224 | tf_op jit(solution)/shard_map/ppermute | solution.py:14
where the time goes:
time: 87.6 us; the launch traced here: 86.9 us
  other arithmetic  36.9 us (42%)
  local copies, waits for them, and re-layouts  35.3 us (40%)
  starting transfers between devices  8.99 us (10%)
  matrix products  4.92 us (6%)
    reshape x2, local copies, waits for them, and re-layouts, body(): pending = error_memory[0, 0] + grad_local.reshape(nblocks, block_len)  9.74 us
    scatter-add x2, other arithmetic, body(): spread = delta_dense.at[silo_lists[lower_silo]].add(from_lower).at[silo_l...  7.5 us
    add x1, other arithmetic, body(): params_new = half_step + CONSENSUS * (mixed_new - estimate_new)  6.31 us
    add x1, other arithmetic, body(): pending = error_memory[0, 0] + grad_local.reshape(nblocks, block_len)  5.03 us
    dot_general x1, matrix products, body(): lax.dot_general(cotangent, activ, (((0,), (0,)), ((), ())), preferred_ele...  4.92 us
    select_n x1, other arithmetic, body(): error_new = jnp.where(keep_mask, jnp.float32(0.0), pending)  4.88 us
    ppermute x2, starting transfers between devices, shifted(): return lax.ppermute(value, axis, pairs)  4.79 us
    all_to_all x1, starting transfers between devices, body(): lax.all_to_all(slot_rows, 'shard', split_axis=0, concat_axis=0, tiled=True)  4.21 us
  transfers between devices with their start and end apart: 3, of which 0 were waited for; matrix products, arithmetic and copies ran while one was open for 35% of the time, Pallas kernels for 0%

commit v1 on v0

v1 whole, which is shorter than its diff:
```python
import functools

import jax
import jax.numpy as jnp
from jax import lax
from jax.experimental import pallas as pl
from jax.experimental.pallas import tpu as pltpu
from jax.sharding import PartitionSpec as P

LEARN_RATE = 0.25
CONSENSUS = 0.5
MIX_WEIGHT = 1.0 / 3.0

F32, BF16, I32 = jnp.float32, jnp.bfloat16, jnp.int32
ANY = pl.BlockSpec(memory_space=pl.ANY)
IN_VMEM = pl.BlockSpec(memory_space=pltpu.VMEM)
MIB = 1 << 20


def dot(a, b, dims=((1,), (0,))):
    return lax.dot_general(a, b, (dims, ((), ())), preferred_element_type=F32)


def as_column(row):
    n = row.shape[1]
    eye = lax.broadcasted_iota(I32, (n, n), 0) == lax.broadcasted_iota(I32, (n, n), 1)
    spread = jnp.where(eye, jnp.broadcast_to(row.astype(F32), (n, n)), 0.0)
    return jnp.sum(spread, axis=1, keepdims=True).astype(I32)


def thirds(rows):
    high = rows.astype(BF16)
    rest = rows - high.astype(F32)
    middle = rest.astype(BF16)
    low = (rest - middle.astype(F32)).astype(BF16)
    return high, middle, low


def pick(choice, parts):
    high, middle, low = parts
    return dot(choice, high) + (dot(choice, middle) + dot(choice, low))


def onehot(mask):
    return jnp.where(mask, 1.0, 0.0).astype(BF16)


def divide(value, by):
    return (value * ((1 << 16) // by + 1)) >> 16


def select_kernel(shards, own_blocks, per_row, scale, lists, counts, act, cot, err, *refs):
    outs, (list_s, count_s, list_v, count_v, act_v, cot_v, err_v, sems) = refs[:shards], refs[shards:]
    me = lax.axis_index("shard")
    slots = list_v.shape[1]
    tokens = act_v.shape[0]
    parts = 4
    step = tokens // parts
    small = [
        pltpu.make_async_copy(lists.at[0, me], list_s, sems.at[0]),
        pltpu.make_async_copy(lists.at[0, me], list_v, sems.at[1]),
        pltpu.make_async_copy(counts.at[0], count_s, sems.at[2]),
    ]
    for copy in small:
        copy.start()
    big = []
    for part in range(parts):
        rows = pl.ds(part * step, step)
        pair = [
            pltpu.make_async_copy(cot.at[rows], cot_v.at[rows], sems.at[4 + 2 * part]),
            pltpu.make_async_copy(act.at[rows], act_v.at[rows], sems.at[5 + 2 * part]),
        ]
        for copy in pair:
            copy.start()
        big.append(pair)
    for copy in small:
        copy.wait()

    for shift in range(shards):
        owner = lax.rem(me + shift, shards)

        def fetch(slot, carry, owner=owner, shift=shift):
            block = owner * own_blocks + list_s[owner, slot]
            pltpu.make_async_copy(
                err.at[0, 0, pl.ds(block, 1)], err_v.at[pl.ds(shift * slots + slot, 1)], sems.at[3]
            ).start()
            return carry

        lax.fori_loop(0, slots, fetch, 0, unroll=8)

    columns, fills = [], []
    width_out = cot_v.shape[1]
    for shift in range(shards):
        owner = lax.rem(me + shift, shards)
        row = list_v[pl.ds(owner, 1), :] + owner * own_blocks
        columns.append(as_column(row))
        slot_ids = lax.broadcasted_iota(I32, (slots, 1), 0)
        fills.append(slot_ids < count_s[me, owner])
    blocks = jnp.concatenate(columns, axis=0)
    filled = jnp.concatenate(fills, axis=0)
    out_row = divide(blocks, per_row)
    segment = blocks - out_row * per_row
    total = blocks.shape[0]
    chosen = onehot(lax.broadcasted_iota(I32, (total, width_out), 1) == out_row)
    acc = jnp.zeros((total, act_v.shape[1]), F32)
    for part in range(parts):
        for copy in big[part]:
            copy.wait()
        rows = pl.ds(part * step, step)
        picked = dot(chosen, cot_v[rows, :], ((1,), (1,))).astype(BF16)
        acc = acc + dot(picked, act_v[rows, :])
    width = act_v.shape[1] // per_row
    grad = jnp.zeros((total, width), F32)
    for part in range(per_row):
        grad = jnp.where(segment == part, acc[:, part * width : (part + 1) * width], grad)
    pltpu.make_async_copy(err.at[0, 0, pl.ds(0, total)], err_v, sems.at[3]).wait()
    pending = jnp.where(filled, err_v[...] + grad * scale, 0.0)
    for shift in range(shards):
        outs[shift][...] = pending[shift * slots : (shift + 1) * slots]


def select(shards, own_blocks, per_row, scale, lists, counts, act, cot, err):
    slots = lists.shape[3]
    width = err.shape[3]
    return pl.pallas_call(
        functools.partial(select_kernel, shards, own_blocks, per_row, scale),
        name="kept_rows",
        in_specs=[ANY] * 5,
        out_specs=[IN_VMEM] * shards,
        out_shape=[jax.ShapeDtypeStruct((slots, width), F32)] * shards,
        scratch_shapes=[
            pltpu.SMEM((shards, slots), I32),
            pltpu.SMEM((shards, shards), I32),
            pltpu.VMEM((shards, slots), I32),
            pltpu.VMEM((8, 128), I32),
            pltpu.VMEM(act.shape, BF16),
            pltpu.VMEM(cot.shape, BF16),
            pltpu.VMEM((shards * slots, width), F32),
            pltpu.SemaphoreType.DMA((12,)),
        ],
        compiler_params=pltpu.CompilerParams(vmem_limit_bytes=16 * MIB),
    )(lists, counts, act, cot, err)


def base_kernel(
    shards, silos, per_row, lists, g_lists, g_counts, params, estimate, mine, base, match, *scratch
):
    list_v, g_s, g_v, gc_s, p_v, e_v, sems = scratch
    me = lax.axis_index("shard")
    silo = lax.axis_index("silo")
    slots = list_v.shape[2]
    g_slots = g_v.shape[1]
    width = p_v.shape[1]
    small = [
        pltpu.make_async_copy(g_lists.at[silo], g_s, sems.at[0]),
        pltpu.make_async_copy(g_lists.at[silo], g_v, sems.at[1]),
        pltpu.make_async_copy(g_counts, gc_s, sems.at[2]),
        pltpu.make_async_copy(lists.at[0], list_v, sems.at[3]),
    ]
    for copy in small:
        copy.start()
    for copy in small:
        copy.wait()

    def fetch(slot, carry):
        block = g_s[0, slot]
        row = divide(block, per_row)
        column = pl.multiple_of((block - row * per_row) * width, width)
        where = (0, pl.ds(row, 1), pl.ds(column, width))
        into = pl.ds(slot, 1)
        pltpu.make_async_copy(params.at[where], p_v.at[into], sems.at[4]).start()
        pltpu.make_async_copy(estimate.at[where], e_v.at[into], sems.at[5]).start()
        return carry

    lax.fori_loop(0, g_slots, fetch, 0, unroll=8)
    blocks = as_column(g_v[...])
    slot_ids = lax.broadcasted_iota(I32, (g_slots, 1), 0)
    filled = slot_ids < gc_s[silo, 0]
    for shift in range(shards):
        sender = lax.rem(me - shift + shards, shards)
        kept = list_v[sender, pl.ds(me, 1), :]
        same = onehot((blocks == kept) & filled)
        if shift == 0:
            own = pick(same, thirds(mine[...]))
        else:
            match[:, (shift - 1) * slots : shift * slots] = same
    pltpu.make_async_copy(p_v, p_v, sems.at[4]).wait()
    pltpu.make_async_copy(e_v, e_v, sems.at[5]).wait()
    base[...] = jnp.where(filled, p_v[...] - e_v[...], 0.0) - LEARN_RATE * own


def base_rows(shards, silos, per_row, lists, g_lists, g_counts, params, estimate, mine):
    slots, width = mine.shape
    g_slots = g_lists.shape[2]
    return pl.pallas_call(
        functools.partial(base_kernel, shards, silos, per_row),
        name="gossip_base",
        in_specs=[ANY] * 5 + [IN_VMEM],
        out_specs=[IN_VMEM] * 2,
        out_shape=[
            jax.ShapeDtypeStruct((g_slots, width), F32),
            jax.ShapeDtypeStruct((g_slots, (shards - 1) * slots), BF16),
        ],
        scratch_shapes=[
            pltpu.VMEM((shards, shards, slots), I32),
            pltpu.SMEM((1, g_slots), I32),
            pltpu.VMEM((1, g_slots), I32),
            pltpu.SMEM(g_counts.shape, I32),
            pltpu.VMEM((g_slots, width), F32),
            pltpu.VMEM((g_slots, width), F32),
            pltpu.SemaphoreType.DMA((6,)),
        ],
        compiler_params=pltpu.CompilerParams(vmem_limit_bytes=8 * MIB),
    )(lists, g_lists, g_counts, params, estimate, mine)


def delta_kernel(base, match, *refs):
    *arrived, out = refs
    slots = arrived[0].shape[0]
    total = base[...]
    for place, rows in enumerate(arrived):
        same = match[:, place * slots : (place + 1) * slots]
        total = total - LEARN_RATE * pick(same, thirds(rows[...]))
    out[...] = total


def delta_rows(base, match, arrived):
    return pl.pallas_call(
        delta_kernel,
        name="delta_rows",
        in_specs=[IN_VMEM] * (2 + len(arrived)),
        out_specs=IN_VMEM,
        out_shape=jax.ShapeDtypeStruct(base.shape, F32),
        compiler_params=pltpu.CompilerParams(vmem_limit_bytes=8 * MIB),
    )(base, match, *arrived)


def dense_kernel(
    shards, silos, own_blocks, per_row, scale,
    lists, counts, g_lists, g_counts, act, cot, err, params, estimate, mixed, delta, *refs
):
    kept = refs[:shards]
    (err_out, est_out, mixed_pre, params_pre, spread,
     list_s, count_s, list_v, g_v, act_v, cot_v, err_v, p_v, e_v, m_v, sems) = refs[shards:]
    me = lax.axis_index("shard")
    silo = lax.axis_index("silo")
    slots = list_v.shape[2]
    g_slots = g_v.shape[2]
    width = delta.shape[1]
    width_out = cot_v.shape[1]
    out_rows = p_v.shape[0]
    small = [
        pltpu.make_async_copy(lists.at[0, me], list_s, sems.at[0]),
        pltpu.make_async_copy(lists.at[0], list_v, sems.at[1]),
        pltpu.make_async_copy(counts.at[0], count_s, sems.at[2]),
        pltpu.make_async_copy(g_lists, g_v, sems.at[3]),
    ]
    owned = [
        pltpu.make_async_copy(params.at[0], p_v, sems.at[4]),
        pltpu.make_async_copy(estimate.at[0], e_v, sems.at[5]),
        pltpu.make_async_copy(mixed.at[0], m_v, sems.at[6]),
    ]
    big = [
        pltpu.make_async_copy(cot, cot_v, sems.at[7]),
        pltpu.make_async_copy(act, act_v, sems.at[8]),
    ]
    halves = range(width // 128)
    for half in halves:
        lanes = pl.ds(half * 128, 128)
        big.append(
            pltpu.make_async_copy(
                err.at[0, 0, :, lanes], err_v.at[half, pl.ds(0, shards * own_blocks)], sems.at[9 + half]
            )
        )
    for copy in small + owned + big:
        copy.start()
    for copy in small + owned:
        copy.wait()

    first, second = neighbours(silo, silos)
    kept_parts = thirds(jnp.concatenate([rows[...] for rows in kept], axis=0))
    kept_ids = jnp.concatenate(
        [list_v[lax.rem(me - shift + shards, shards), pl.ds(me, 1), :] for shift in range(shards)], axis=1
    )
    delta_parts = thirds(delta[...])
    own_ids = g_v[silo]
    next_ids = jnp.concatenate([g_v[first], g_v[second]], axis=1)
    for part in range(per_row):
        lanes = slice(part * width, (part + 1) * width)

        def places(ids):
            here = lax.broadcasted_iota(I32, (out_rows, ids.shape[1]), 0) * per_row + part
            return onehot(here == ids)

        grad = pick(places(kept_ids), kept_parts)
        change = pick(places(own_ids), delta_parts)
        spread[part * out_rows : (part + 1) * out_rows, :] = places(next_ids)
        half = p_v[:, lanes] - LEARN_RATE * grad
        est = e_v[:, lanes] + change
        mix = m_v[:, lanes] + MIX_WEIGHT * change
        e_v[:, lanes] = est
        mixed_pre[:, lanes] = mix
        params_pre[:, lanes] = half + CONSENSUS * (mix - est)
    est_copy = pltpu.make_async_copy(e_v, est_out.at[0], sems.at[4])
    est_copy.start()

    for copy in big:
        copy.wait()
    tile = 128
    for part in range(width_out // tile):
        grad = dot(cot_v[:, part * tile : (part + 1) * tile], act_v[...], ((0,), (0,))) * scale
        for seg in range(per_row):
            where = pl.ds(part * tile * per_row + seg, tile, stride=per_row)
            for half in halves:
                lane = seg * width + half * 128
                err_v[half, where, :] = err_v[half, where, :] + grad[:, lane : lane + 128]

    spare = shards * own_blocks
    for owner in range(shards):
        limit = count_s[me, owner]

        def clear(slot, carry, owner=owner, limit=limit):
            block = jnp.where(slot < limit, owner * own_blocks + list_s[owner, slot], spare)
            for half in halves:
                err_v[half, pl.ds(block, 1), :] = jnp.zeros((1, 128), F32)
            return carry

        lax.fori_loop(0, slots, clear, 0, unroll=8)
    stores = [
        pltpu.make_async_copy(
            err_v.at[half, pl.ds(0, spare)], err_out.at[0, 0, :, pl.ds(half * 128, 128)], sems.at[9 + half]
        )
        for half in halves
    ]
    for copy in stores:
        copy.start()
    for copy in stores:
        copy.wait()
    est_copy.wait()


def dense(shards, silos, own_blocks, per_row, scale, lists, counts, g_lists, g_counts, act, cot, err, params, estimate, mixed, delta, kept):
    slots = lists.shape[3]
    g_slots = g_lists.shape[2]
    width = err.shape[3]
    owned = params.shape[1:]
    return pl.pallas_call(
        functools.partial(dense_kernel, shards, silos, own_blocks, per_row, scale),
        name="dense",
        in_specs=[ANY] * 10 + [IN_VMEM] * (1 + shards),
        out_specs=[ANY, ANY, IN_VMEM, IN_VMEM, IN_VMEM],
        out_shape=[
            jax.ShapeDtypeStruct(err.shape, F32),
            jax.ShapeDtypeStruct(estimate.shape, F32),
            jax.ShapeDtypeStruct(owned, F32),
            jax.ShapeDtypeStruct(owned, F32),
            jax.ShapeDtypeStruct((own_blocks, 2 * g_slots), BF16),
        ],
        scratch_shapes=[
            pltpu.SMEM((shards, slots), I32),
            pltpu.SMEM((shards, shards), I32),
            pltpu.VMEM((shards, shards, slots), I32),
            pltpu.VMEM(g_lists.shape, I32),
            pltpu.VMEM(act.shape, BF16),
            pltpu.VMEM(cot.shape, BF16),
            pltpu.VMEM((width // 128, shards * own_blocks + 8, 128), F32),
            pltpu.VMEM(owned, F32),
            pltpu.VMEM(owned, F32),
            pltpu.VMEM(owned, F32),
            pltpu.SemaphoreType.DMA((9 + width // 128,)),
        ],
        compiler_params=pltpu.CompilerParams(vmem_limit_bytes=32 * MIB),
    )(lists, counts, g_lists, g_counts, act, cot, err, params, estimate, mixed, delta, *kept)


def final_kernel(per_row, mixed_pre, params_pre, spread, first, second, mixed_out, params_out, m_v, p_v, sems):
    out_rows = m_v.shape[0]
    width = m_v.shape[1] // per_row
    parts = thirds(jnp.concatenate([first[...], second[...]], axis=0))
    copies = []
    for part in range(per_row):
        lanes = slice(part * width, (part + 1) * width)
        change = pick(spread[part * out_rows : (part + 1) * out_rows, :], parts)
        m_v[:, lanes] = mixed_pre[:, lanes] + MIX_WEIGHT * change
        p_v[:, lanes] = params_pre[:, lanes] + (CONSENSUS * MIX_WEIGHT) * change
        pair = [
            pltpu.make_async_copy(m_v.at[:, lanes], mixed_out.at[0, :, lanes], sems.at[2 * part]),
            pltpu.make_async_copy(p_v.at[:, lanes], params_out.at[0, :, lanes], sems.at[2 * part + 1]),
        ]
        for copy in pair:
            copy.start()
        copies += pair
    for copy in copies:
        copy.wait()


def final(per_row, shape, mixed_pre, params_pre, spread, first, second):
    return pl.pallas_call(
        functools.partial(final_kernel, per_row),
        name="neighbours",
        in_specs=[IN_VMEM] * 5,
        out_specs=[ANY] * 2,
        out_shape=[jax.ShapeDtypeStruct(shape, F32)] * 2,
        scratch_shapes=[
            pltpu.VMEM(mixed_pre.shape, F32),
            pltpu.VMEM(mixed_pre.shape, F32),
            pltpu.SemaphoreType.DMA((2 * per_row,)),
        ],
        compiler_params=pltpu.CompilerParams(vmem_limit_bytes=20 * MIB),
    )(mixed_pre, params_pre, spread, first, second)


def neighbours(silo, silos):
    lower, upper = lax.rem(silo + silos - 1, silos), lax.rem(silo + 1, silos)
    if silos % 2:
        return lower, upper
    even = lax.rem(silo, 2) == 0
    return jnp.where(even, upper, lower), jnp.where(even, lower, upper)


def exchange(rows, silos):
    if silos % 2:
        routes = [[(a, (a + 1) % silos) for a in range(silos)], [(a, (a - 1) % silos) for a in range(silos)]]
    else:
        routes = [
            [(a, a ^ 1) for a in range(silos)],
            [(a, (a + 1 if a % 2 else a - 1) % silos) for a in range(silos)],
        ]
    far = lax.ppermute(rows, "silo", routes[1])
    near = lax.ppermute(rows, "silo", routes[0])
    return near, far


def body(
    activ, cotangent, error_memory, params, estimate, mixed,
    kept_blocks, kept_counts, gossip_blocks, gossip_counts,
):
    shards = lax.axis_size("shard")
    silos = lax.axis_size("silo")
    nblocks, block_len = error_memory.shape[2:]
    own_blocks = nblocks // shards
    per_row = activ.shape[1] // block_len
    scale = activ.shape[1] ** (-0.5)
    mine, *outgoing = select(
        shards, own_blocks, per_row, scale, kept_blocks, kept_counts, activ, cotangent, error_memory
    )
    arrived = [
        lax.ppermute(rows, "shard", [(r, (r + shift) % shards) for r in range(shards)])
        for shift, rows in enumerate(outgoing, 1)
    ]
    base, match = base_rows(
        shards, silos, per_row, kept_blocks, gossip_blocks, gossip_counts, params, estimate, mine
    )
    delta = delta_rows(base, match, arrived)
    first, second = exchange(delta, silos)
    error_out, estimate_out, mixed_pre, params_pre, spread = dense(
        shards, silos, own_blocks, per_row, scale, kept_blocks, kept_counts, gossip_blocks, gossip_counts,
        activ, cotangent, error_memory, params, estimate, mixed, delta, [mine, *arrived],
    )
    mixed_out, params_out = final(per_row, mixed.shape, mixed_pre, params_pre, spread, first, second)
    return params_out, estimate_out, mixed_out, error_out


def solution(mesh):
    in_specs = (
        P(("silo", "shard"), None),
        P(("silo", "shard"), None),
        P("silo", "shard", None, None),
        P("silo", "shard", None),
        P("silo", "shard", None),
        P("silo", "shard", None),
        P("silo", None, None, None),
        P("silo", None, None),
        P(None, "shard", None),
        P(None, "shard"),
    )
    out_specs = (
        P("silo", "shard", None),
        P("silo", "shard", None),
        P("silo", "shard", None),
        P("silo", "shard", None, None),
    )
    return jax.shard_map(body, mesh=mesh, in_specs=in_specs, out_specs=out_specs, check_vma=False)
```

time: 87.6 us -> 40 us (0.46)
  other arithmetic: 36.9 us -> 0 us
  local copies, waits for them, and re-layouts: 35.3 us -> 14.9 us
  Pallas kernels: 0 us -> 17 us
  matrix products: 4.92 us -> 0 us
  starting transfers between devices: 8.99 us -> 6.79 us
    reshape x5 -> x0, local copies, waits for them, and re-layouts: 17.8 us -> none  [the longest x2 9.74 us: body(): pending = error_memory[0, 0] + grad_local.reshape(nblocks, block_len)]
    pallas_call x0 -> x5, Pallas kernels: none -> 17 us  [the longest x1 6.98 us: dense(): pl.pallas_call(functools.partial(dense_kernel, shards, silos, own_blocks,...]
    unnamed x9 -> x35, local copies, waits for them, and re-layouts: 3.45 us -> 14.9 us
    add x2 -> x0, other arithmetic: 11.3 us -> none  [the longest x1 6.31 us: body(): params_new = half_step + CONSENSUS * (mixed_new - estimate_new)]
    scatter-add x3 -> x0, other arithmetic: 9.98 us -> none  [the longest x2 7.5 us: body(): spread = delta_dense.at[silo_lists[lower_silo]].add(from_lower).at[silo_l...]
    another operation x4 -> x0, local copies, waits for them, and re-layouts: 8.18 us -> none  [the longest x1 2.72 us: body(): mixed_new = mixed[0].reshape(own_blocks, block_len) + MIX_WEIGHT * spread]
    select_n x6 -> x0, other arithmetic: 7.31 us -> none  [the longest x1 4.88 us: body(): error_new = jnp.where(keep_mask, jnp.float32(0.0), pending)]
    dot_general x1 -> x0, matrix products: 4.92 us -> none  [body(): lax.dot_general(cotangent, activ, (((0,), (0,)), ((), ())), preferred_ele...]
  transfers between devices with their start and end apart: 3 -> 3, of which waited for: 0 -> 0; matrix products, arithmetic and copies ran while one was open for 35% -> 0% of each run, Pallas kernels for 0% -> 25%
where the time goes in v1:
time: 40 us; the launch traced here: 39.5 us
  Pallas kernels  17 us (42%)
  local copies, waits for them, and re-layouts  14.9 us (37%)
  starting transfers between devices  6.79 us (17%)
  between operations  0.73 us (2%)
    unnamed x35, local copies, waits for them, and re-layouts  14.9 us
    pallas_call x1, Pallas kernels, dense(): pl.pallas_call(functools.partial(dense_kernel, shards, silos, own_blocks,...  6.98 us
    pallas_call x1, Pallas kernels, select(): pl.pallas_call(functools.partial(select_kernel, shards, own_blocks, per_r...  4.81 us
    ppermute x1, starting transfers between devices, exchange(): far = lax.ppermute(rows, 'silo', routes[1])  3.78 us
    ppermute x1, starting transfers between devices, body(): lax.ppermute(rows, 'shard', [(r, (r + shift) % shards) for r in range(sha...  3 us
    pallas_call x1, Pallas kernels, base_rows(): pl.pallas_call(functools.partial(base_kernel, shards, silos, per_row), na...  2.84 us
    pallas_call x1, Pallas kernels, final(): pl.pallas_call(functools.partial(final_kernel, per_row), name='neighbours...  2.21 us
  transfers between devices with their start and end apart: 3, of which 0 were waited for; matrix products, arithmetic and copies ran while one was open for 0% of the time, Pallas kernels for 25%

profile of v1, /device:TPU:0, one launch (start us, length us, event | category | flops | bytes accessed | tf_op | source)
XLA Modules:
  0.0 39.5 jit_solution(8422371885137411173)
XLA Ops:
  0.6 0.0 copy-start
  0.6 1.9 %copy-done = f32[1,1,3200,256]{3,2,1,0:T(8,128)S(1)} copy-done((f32[1,1,3200,256]{3,2,1,0:T(8,128)S(1)}, f32[1,1,3200,256]{3,2,1,0:T(8,128)}, u32[]{:S(2)}) %copy-start) | copy-done | bytes 3276824
  2.6 1.7 %copy-done.2 = bf16[1024,1280]{1,0:T(8,128)(2,1)S(1)} copy-done((bf16[1024,1280]{1,0:T(8,128)(2,1)S(1)}, bf16[1024,1280]{1,0:T(8,128)(2,1)}, u32[]{:S(2)}) %copy-start.2) | copy-done | bytes 2621464
  4.3 1.3 %copy-done.8 = bf16[1024,640]{1,0:T(8,128)(2,1)S(1)} copy-done((bf16[1024,640]{1,0:T(8,128)(2,1)S(1)}, bf16[1024,640]{1,0:T(8,128)(2,1)}, u32[]{:S(2)}) %copy-start.8) | copy-done | bytes 1310744
  5.6 0.7 %copy-done.12 = s32[1,2,2,64]{3,2,1,0:T(2,128)S(1)} copy-done((s32[1,2,2,64]{3,2,1,0:T(2,128)S(1)}, s32[1,2,2,64]{3,2,1,0:T(2,128)}, u32[]{:S(2)}) %copy-start.12) | copy-done | bytes 1048
  6.3 0.7 %copy-done.14 = s32[1,2,2]{2,1,0:T(2,128)S(1)} copy-done((s32[1,2,2]{2,1,0:T(2,128)S(1)}, s32[1,2,2]{2,1,0:T(2,128)}, u32[]{:S(2)}) %copy-start.14) | copy-done | bytes 40
  7.0 4.8 %kept_rows.1 = (f32[64,256]{1,0:T(8,128)S(1)}, f32[64,256]{1,0:T(8,128)S(1)}) custom-call(s32[1,2,2,64]{3,2,1,0:T(2,128)S(1)} %copy-done.12, s32[1,2,2]{2,1,0:T(2,128)S(1)} %copy-done.14, bf16[1024,1280]{1,0:T(8,128)(2,1)S(1)} %copy-done.2, bf16[1024,640]{1,0:T(8,128)(2,1)S(1)} %copy-done.8, f32[1,1,3200,256]{3,2,1,0:T(8,128)S(1)} %copy-done), custom_call_target="tpu_custom_call" | custom-call | tf_op jit(solution)/shard_map/kept_rows/pallas_call | solution.py:125
  11.8 3.0 %collective-permute-start = (f32[64,256]{1,0:T(8,128)S(1)}, f32[64,256]{1,0:T(8,128)S(1)}, u32[]{:S(2)}, u32[]{:S(2)}) collective-permute-start(f32[64,256]{1,0:T(8,128)S(1)} %get-tuple-element.18), channel_id=1, source_target_pairs={{0,1},{1,0},{2,3},{3,2},{4,5},{5,4},{6,7},{7,6},{8,9},{9,8},{10,11... | collective-permute-start | bytes 196616 | tf_op jit(solution)/shard_map/ppermute | solution.py:448
  14.8 0.1 copy.15.g_counts
  14.9 1.4 %copy-done.4 = f32[1,320,1280]{2,1,0:T(8,128)S(1)} copy-done((f32[1,320,1280]{2,1,0:T(8,128)S(1)}, f32[1,320,1280]{2,1,0:T(8,128)}, u32[]{:S(2)}) %copy-start.4) | copy-done | bytes 1638424
  16.3 1.4 %copy-done.6 = f32[1,320,1280]{2,1,0:T(8,128)S(1)} copy-done((f32[1,320,1280]{2,1,0:T(8,128)S(1)}, f32[1,320,1280]{2,1,0:T(8,128)}, u32[]{:S(2)}) %copy-start.6) | copy-done | bytes 1638424
  17.8 2.8 %gossip_base.1 = (f32[128,256]{1,0:T(8,128)S(1)}, bf16[128,64]{1,0:T(8,128)(2,1)S(1)}) custom-call(s32[1,2,2,64]{3,2,1,0:T(2,128)S(1)} %copy-done.13, s32[16,1,128]{2,1,0:T(1,128)S(1)} %copy-done.11, s32[16,1]{1,0:T(8,128)S(1)} %copy.15.g_counts, f32[1,320,1280]{2,1,0:T(8,128)S(1)} %copy-done.4, f32[1,320,1280]{2,1,0:T(8,128)S(1)} %copy-done.6, ...), custom_call_target="tpu_custom_call" | custom-call | tf_op jit(solution)/shard_map/gossip_base/pallas_call | solution.py:195
  20.6 0.0 collective-permute-done.refs_0_.refs_1_
  20.6 0.2 delta_rows.1.delta
  20.8 3.8 %collective-permute-start.2 = (f32[128,256]{1,0:T(8,128)S(1)}, f32[128,256]{1,0:T(8,128)S(1)}, u32[]{:S(2)}, u32[]{:S(2)}) collective-permute-start(f32[128,256]{1,0:T(8,128)S(1)} %delta_rows.1.delta), channel_id=1, source_target_pairs={{0,30},{2,4},{4,2},{6,8},{8,6},{10,12},{12,10},{14,16},{16,14},{18... | collective-permute-start | bytes 393224 | tf_op jit(solution)/shard_map/ppermute | solution.py:429
  24.6 0.0 collective-permute-start.1
  24.6 0.0 copy-start.5
  24.7 1.4 %copy-done.5 = f32[1,320,1280]{2,1,0:T(8,128)S(1)} copy-done((f32[1,320,1280]{2,1,0:T(8,128)S(1)}, f32[1,320,1280]{2,1,0:T(8,128)}, u32[]{:S(2)}) %copy-start.5) | copy-done | bytes 1638424
  26.1 1.4 %copy-done.7 = f32[1,320,1280]{2,1,0:T(8,128)S(1)} copy-done((f32[1,320,1280]{2,1,0:T(8,128)S(1)}, f32[1,320,1280]{2,1,0:T(8,128)}, u32[]{:S(2)}) %copy-start.7) | copy-done | bytes 1638424
  27.5 1.3 %copy-done.9 = bf16[1024,640]{1,0:T(8,128)(2,1)S(1)} copy-done((bf16[1024,640]{1,0:T(8,128)(2,1)S(1)}, bf16[1024,640]{1,0:T(8,128)(2,1)}, u32[]{:S(2)}) %copy-start.9) | copy-done | bytes 1310744
  28.8 1.4 %copy-done.10 = f32[1,320,1280]{2,1,0:T(8,128)S(1)} copy-done((f32[1,320,1280]{2,1,0:T(8,128)S(1)}, f32[1,320,1280]{2,1,0:T(8,128)}, u32[]{:S(2)}) %copy-start.10) | copy-done | bytes 1638424
  30.3 7.0 %dense.1 = (f32[1,1,3200,256]{3,2,1,0:T(8,128)}, f32[1,320,1280]{2,1,0:T(8,128)}, f32[320,1280]{1,0:T(8,128)S(1)}, f32[320,1280]{1,0:T(8,128)S(1)}, bf16[1600,256]{1,0:T(8,128)(2,1)S(1)}) custom-call(s32[1,2,2,64]{3,2,1,0:T(2,128)S(1)} %copy-done.13, s32[1,2,2]{2,1,0:T(2,128)S(1)} %copy-done.15, s32[16,1,128]{2,1,0:T(1,128)S(1)} %copy-done.11, ...), custom_call_target="tpu_custom_call" | custom-call | tf_op jit(solution)/shard_map/dense/pallas_call | solution.py:347
  37.3 0.0 collective-permute-done.1.first
  37.3 2.2 %neighbours.1 = (f32[1,320,1280]{2,1,0:T(8,128)}, f32[1,320,1280]{2,1,0:T(8,128)}) custom-call(f32[320,1280]{1,0:T(8,128)S(1)} %get-tuple-element.19.mixed_pre, f32[320,1280]{1,0:T(8,128)S(1)} %get-tuple-element.20.params_pre, bf16[1600,256]{1,0:T(8,128)(2,1)S(1)} %get-tuple-element.21.spread, f32[128,256]{1,0:T(8,128)S(1)} %collective-permute-done.1.first, ...), custom_call_target="tpu_custom_call" | custom-call | tf_op jit(solution)/shard_map/neighbours/pallas_call | solution.py:398
  (22 shorter events, 0.0 us)
Async XLA Ops:
  0.6 1.9 %copy-start = (f32[1,1,3200,256]{3,2,1,0:T(8,128)S(1)}, f32[1,1,3200,256]{3,2,1,0:T(8,128)}, u32[]{:S(2)}) copy-start(f32[1,1,3200,256]{3,2,1,0:T(8,128)} %err.3) | copy-start | bytes 9830404
  2.6 1.7 %copy-start.2 = (bf16[1024,1280]{1,0:T(8,128)(2,1)S(1)}, bf16[1024,1280]{1,0:T(8,128)(2,1)}, u32[]{:S(2)}) copy-start(bf16[1024,1280]{1,0:T(8,128)(2,1)} %act.3) | copy-start | bytes 7864324
  4.3 1.3 %copy-start.8 = (bf16[1024,640]{1,0:T(8,128)(2,1)S(1)}, bf16[1024,640]{1,0:T(8,128)(2,1)}, u32[]{:S(2)}) copy-start(bf16[1024,640]{1,0:T(8,128)(2,1)} %cot.3) | copy-start | bytes 3932164
  5.6 0.7 %copy-start.12 = (s32[1,2,2,64]{3,2,1,0:T(2,128)S(1)}, s32[1,2,2,64]{3,2,1,0:T(2,128)}, u32[]{:S(2)}) copy-start(s32[1,2,2,64]{3,2,1,0:T(2,128)} %lists.5) | copy-start | bytes 3076
  6.3 0.7 %copy-start.14 = (s32[1,2,2]{2,1,0:T(2,128)S(1)}, s32[1,2,2]{2,1,0:T(2,128)}, u32[]{:S(2)}) copy-start(s32[1,2,2]{2,1,0:T(2,128)} %counts.3) | copy-start | bytes 52
  7.0 7.8 %copy-start.16 = (s32[16,1]{0,1:T(1,128)S(1)}, s32[16,1]{0,1:T(1,128)}, u32[]{:S(2)}) copy-start(s32[16,1]{0,1:T(1,128)} %param.19) | copy-start | bytes 196
  7.0 7.9 %copy-start.11 = (s32[16,1,128]{2,1,0:T(1,128)S(1)}, s32[16,1,128]{2,1,0:T(1,128)}, u32[]{:S(2)}) copy-start(s32[16,1,128]{2,1,0:T(1,128)} %g_lists.3) | copy-start | bytes 24580
  7.0 7.9 %copy-start.13 = (s32[1,2,2,64]{3,2,1,0:T(2,128)S(1)}, s32[1,2,2,64]{3,2,1,0:T(2,128)}, u32[]{:S(2)}) copy-start(s32[1,2,2,64]{3,2,1,0:T(2,128)} %lists.5) | copy-start | bytes 3076
  7.0 17.6 %copy-start.3 = (bf16[1024,1280]{1,0:T(8,128)(2,1)S(1)}, bf16[1024,1280]{1,0:T(8,128)(2,1)}, u32[]{:S(2)}) copy-start(bf16[1024,1280]{1,0:T(8,128)(2,1)} %act.3) | copy-start | bytes 7864324
  11.8 8.8 %collective-permute-start = (f32[64,256]{1,0:T(8,128)S(1)}, f32[64,256]{1,0:T(8,128)S(1)}, u32[]{:S(2)}, u32[]{:S(2)}) collective-permute-start(f32[64,256]{1,0:T(8,128)S(1)} %get-tuple-element.18), channel_id=1, source_target_pairs={{0,1},{1,0},{2,3},{3,2},{4,5},{5,4},{6,7},{7,6},{8,9},{9,8},{10,11... | collective-permute-start | bytes 196616 | tf_op jit(solution)/shard_map/ppermute | solution.py:448
  14.9 1.4 %copy-start.4 = (f32[1,320,1280]{2,1,0:T(8,128)S(1)}, f32[1,320,1280]{2,1,0:T(8,128)}, u32[]{:S(2)}) copy-start(f32[1,320,1280]{2,1,0:T(8,128)} %params.3) | copy-start | bytes 4915204
  16.3 1.4 %copy-start.6 = (f32[1,320,1280]{2,1,0:T(8,128)S(1)}, f32[1,320,1280]{2,1,0:T(8,128)}, u32[]{:S(2)}) copy-start(f32[1,320,1280]{2,1,0:T(8,128)} %estimate.3) | copy-start | bytes 4915204
  17.8 6.9 %copy-start.1 = (f32[1,1,3200,256]{3,2,1,0:T(8,128)S(1)}, f32[1,1,3200,256]{3,2,1,0:T(8,128)}, u32[]{:S(2)}) copy-start(f32[1,1,3200,256]{3,2,1,0:T(8,128)} %err.3) | copy-start | bytes 9830404
  17.8 6.9 %copy-start.15 = (s32[1,2,2]{2,1,0:T(2,128)S(1)}, s32[1,2,2]{2,1,0:T(2,128)}, u32[]{:S(2)}) copy-start(s32[1,2,2]{2,1,0:T(2,128)} %counts.3) | copy-start | bytes 52
  20.8 16.4 %collective-permute-start.2 = (f32[128,256]{1,0:T(8,128)S(1)}, f32[128,256]{1,0:T(8,128)S(1)}, u32[]{:S(2)}, u32[]{:S(2)}) collective-permute-start(f32[128,256]{1,0:T(8,128)S(1)} %delta_rows.1.delta), channel_id=1, source_target_pairs={{0,30},{2,4},{4,2},{6,8},{8,6},{10,12},{12,10},{14,16},{16,14},{18... | collective-permute-start | bytes 393224 | tf_op jit(solution)/shard_map/ppermute | solution.py:429
  24.6 12.6 %collective-permute-start.1 = (f32[128,256]{1,0:T(8,128)S(1)}, f32[128,256]{1,0:T(8,128)S(1)}, u32[]{:S(2)}, u32[]{:S(2)}) collective-permute-start(f32[128,256]{1,0:T(8,128)S(1)} %delta_rows.1.delta), channel_id=1, source_target_pairs={{0,2},{2,0},{4,6},{6,4},{8,10},{10,8},{12,14},{14,12},{16,18},{18,... | collective-permute-start | bytes 393224 | tf_op jit(solution)/shard_map/ppermute | solution.py:430
  24.6 1.4 %copy-start.5 = (f32[1,320,1280]{2,1,0:T(8,128)S(1)}, f32[1,320,1280]{2,1,0:T(8,128)}, u32[]{:S(2)}) copy-start(f32[1,320,1280]{2,1,0:T(8,128)} %params.3) | copy-start | bytes 4915204
  26.1 1.4 %copy-start.7 = (f32[1,320,1280]{2,1,0:T(8,128)S(1)}, f32[1,320,1280]{2,1,0:T(8,128)}, u32[]{:S(2)}) copy-start(f32[1,320,1280]{2,1,0:T(8,128)} %estimate.3) | copy-start | bytes 4915204
  27.5 1.3 %copy-start.9 = (bf16[1024,640]{1,0:T(8,128)(2,1)S(1)}, bf16[1024,640]{1,0:T(8,128)(2,1)}, u32[]{:S(2)}) copy-start(bf16[1024,640]{1,0:T(8,128)(2,1)} %cot.3) | copy-start | bytes 3932164
  28.8 1.4 %copy-start.10 = (f32[1,320,1280]{2,1,0:T(8,128)S(1)}, f32[1,320,1280]{2,1,0:T(8,128)}, u32[]{:S(2)}) copy-start(f32[1,320,1280]{2,1,0:T(8,128)} %mixed.1) | copy-start | bytes 4915204

commit v2 on v1

v2 whole, which is shorter than its diff:
```python
import functools

import jax
import jax.numpy as jnp
from jax import lax
from jax.experimental import pallas as pl
from jax.experimental.pallas import tpu as pltpu
from jax.sharding import PartitionSpec as P

LEARN_RATE = 0.25
CONSENSUS = 0.5
MIX_WEIGHT = 1.0 / 3.0

F32, BF16, I32 = jnp.float32, jnp.bfloat16, jnp.int32
ANY = pl.BlockSpec(memory_space=pl.ANY)
IN_VMEM = pl.BlockSpec(memory_space=pltpu.VMEM)
MIB = 1 << 20


def dot(a, b, dims=((1,), (0,))):
    return lax.dot_general(a, b, (dims, ((), ())), preferred_element_type=F32)


def as_column(row):
    n = row.shape[1]
    eye = lax.broadcasted_iota(I32, (n, n), 0) == lax.broadcasted_iota(I32, (n, n), 1)
    spread = jnp.where(eye, jnp.broadcast_to(row.astype(F32), (n, n)), 0.0)
    return jnp.sum(spread, axis=1, keepdims=True).astype(I32)


def thirds(rows):
    high = rows.astype(BF16)
    rest = rows - high.astype(F32)
    middle = rest.astype(BF16)
    low = (rest - middle.astype(F32)).astype(BF16)
    return high, middle, low


def pick(choice, parts):
    high, middle, low = parts
    return dot(choice, high) + (dot(choice, middle) + dot(choice, low))


def onehot(mask):
    return jnp.where(mask, 1.0, 0.0).astype(BF16)


def divide(value, by):
    return (value * ((1 << 16) // by + 1)) >> 16


def select_kernel(shards, own_blocks, per_row, scale, lists, counts, act, cot, err, *refs):
    mine, *outs = refs[:shards]
    act_v, cot_v, list_s, count_s, list_v, err_v, sems = refs[shards:]
    me = lax.axis_index("shard")
    slots = list_v.shape[1]
    tokens = act_v.shape[0]
    parts = 2
    step = tokens // parts
    small = [
        pltpu.make_async_copy(lists.at[0, me], list_s, sems.at[0]),
        pltpu.make_async_copy(lists.at[0, me], list_v, sems.at[1]),
        pltpu.make_async_copy(counts.at[0], count_s, sems.at[2]),
    ]
    for copy in small:
        copy.start()
    big = []
    for part in range(parts):
        rows = pl.ds(part * step, step)
        pair = [
            pltpu.make_async_copy(cot.at[rows], cot_v.at[rows], sems.at[4 + 2 * part]),
            pltpu.make_async_copy(act.at[rows], act_v.at[rows], sems.at[5 + 2 * part]),
        ]
        for copy in pair:
            copy.start()
        big.append(pair)
    for copy in small:
        copy.wait()

    for shift in range(1, shards):
        owner = lax.rem(me + shift, shards)

        def fetch(slot, carry, owner=owner, shift=shift):
            block = owner * own_blocks + list_s[owner, slot]
            pltpu.make_async_copy(
                err.at[0, 0, pl.ds(block, 1)], err_v.at[pl.ds((shift - 1) * slots + slot, 1)], sems.at[3]
            ).start()
            return carry

        lax.fori_loop(0, slots, fetch, 0, unroll=slots)

    columns, fills = [], []
    width_out = cot_v.shape[1]
    for shift in range(shards):
        owner = lax.rem(me + shift, shards)
        row = list_v[pl.ds(owner, 1), :] + owner * own_blocks
        columns.append(as_column(row))
        slot_ids = lax.broadcasted_iota(I32, (slots, 1), 0)
        fills.append(slot_ids < count_s[me, owner])
    blocks = jnp.concatenate(columns, axis=0)
    out_row = divide(blocks, per_row)
    segment = blocks - out_row * per_row
    total = blocks.shape[0]
    chosen = onehot(lax.broadcasted_iota(I32, (total, width_out), 1) == out_row)
    acc = jnp.zeros((total, act_v.shape[1]), F32)
    for part in range(parts):
        for copy in big[part]:
            copy.wait()
        rows = pl.ds(part * step, step)
        picked = dot(chosen, cot_v[rows, :], ((1,), (1,))).astype(BF16)
        acc = acc + dot(picked, act_v[rows, :])
    width = act_v.shape[1] // per_row
    grad = jnp.zeros((total, width), F32)
    for part in range(per_row):
        grad = jnp.where(segment == part, acc[:, part * width : (part + 1) * width], grad)
    grad = grad * scale
    mine[...] = grad[:slots]
    pltpu.make_async_copy(err.at[0, 0, pl.ds(0, total - slots)], err_v, sems.at[3]).wait()
    for shift in range(1, shards):
        here = slice((shift - 1) * slots, shift * slots)
        pending = err_v[here, :] + grad[shift * slots : (shift + 1) * slots]
        outs[shift - 1][...] = jnp.where(fills[shift], pending, 0.0)


def select(shards, own_blocks, per_row, scale, lists, counts, act, cot, err):
    slots = lists.shape[3]
    width = err.shape[3]
    return pl.pallas_call(
        functools.partial(select_kernel, shards, own_blocks, per_row, scale),
        name="kept_rows",
        in_specs=[ANY] * 5,
        out_specs=[IN_VMEM] * (shards + 2),
        out_shape=[pltpu.VMEM((slots, width), F32)] * shards
        + [pltpu.VMEM(act.shape, BF16), pltpu.VMEM(cot.shape, BF16)],
        scratch_shapes=[
            pltpu.SMEM((shards, slots), I32),
            pltpu.SMEM((shards, shards), I32),
            pltpu.VMEM((shards, slots), I32),
            pltpu.VMEM(((shards - 1) * slots, width), F32),
            pltpu.SemaphoreType.DMA((8,)),
        ],
        compiler_params=pltpu.CompilerParams(vmem_limit_bytes=16 * MIB),
    )(lists, counts, act, cot, err)


def add_gradient(cot_v, act_v, err_v, columns, per_row, scale):
    tile = 128
    halves = err_v.shape[0]
    for part in range(columns.start, columns.stop, tile):
        grad = dot(cot_v[:, part : part + tile], act_v[...], ((0,), (0,))) * scale
        for seg in range(per_row):
            where = pl.ds((part - columns.start) * per_row + seg, tile, stride=per_row)
            for half in range(halves):
                lane = (seg * halves + half) * 128
                err_v[half, where, :] = err_v[half, where, :] + grad[:, lane : lane + 128]


def clear_kept(err_v, list_s, count_s, me, own_blocks, first, spare):
    shards, slots = list_s.shape
    for owner in range(shards):
        if first >= (owner + 1) * own_blocks or first + spare <= owner * own_blocks:
            continue
        limit = count_s[me, owner]

        def clear(slot, carry, owner=owner, limit=limit):
            block = owner * own_blocks + list_s[owner, slot] - first
            kept = (slot < limit) & (block >= 0) & (block < spare)
            block = jnp.where(kept, block, spare)
            for half in range(err_v.shape[0]):
                err_v[half, pl.ds(block, 1), :] = jnp.zeros((1, 128), F32)
            return carry

        lax.fori_loop(0, slots, clear, 0, unroll=16)


def memory_copies(err, err_v, first, spare, sems):
    return [
        pltpu.make_async_copy(
            err.at[0, 0, pl.ds(first, spare), pl.ds(half * 128, 128)], err_v.at[half, pl.ds(0, spare)], sems[half]
        )
        for half in range(err_v.shape[0])
    ]


def base_kernel(
    shards, own_blocks, per_row, scale, split,
    lists, counts, g_lists, g_counts, params, estimate, err, grad, act_v, cot_v,
    base, match, mine, p_v, e_v, err_a,
    list_s, count_s, list_v, g_s, g_v, gc_s, pr_v, er_v, mr_v, sems,
):
    me = lax.axis_index("shard")
    silo = lax.axis_index("silo")
    slots = list_v.shape[2]
    g_slots = g_v.shape[1]
    width = pr_v.shape[1]
    spare = split * per_row
    small = [
        pltpu.make_async_copy(g_lists.at[silo], g_s, sems.at[0]),
        pltpu.make_async_copy(lists.at[0, me], list_s, sems.at[1]),
        pltpu.make_async_copy(counts.at[0], count_s, sems.at[2]),
        pltpu.make_async_copy(g_lists.at[silo], g_v, sems.at[3]),
        pltpu.make_async_copy(g_counts, gc_s, sems.at[4]),
        pltpu.make_async_copy(lists.at[0], list_v, sems.at[5]),
    ]
    for copy in small:
        copy.start()
    memory = memory_copies(err, err_a, 0, spare, [sems.at[6 + half] for half in range(err_a.shape[0])])
    for copy in memory:
        copy.start()
    for copy in small:
        copy.wait()

    def fetch(slot, carry):
        block = g_s[0, slot]
        row = divide(block, per_row)
        column = pl.multiple_of((block - row * per_row) * width, width)
        where = (0, pl.ds(row, 1), pl.ds(column, width))
        into = pl.ds(slot, 1)
        pltpu.make_async_copy(params.at[where], pr_v.at[into], sems.at[0]).start()
        pltpu.make_async_copy(estimate.at[where], er_v.at[into], sems.at[1]).start()
        return carry

    lax.fori_loop(0, g_slots, fetch, 0, unroll=32)

    def fetch_own(slot, carry):
        block = me * own_blocks + list_s[me, slot]
        pltpu.make_async_copy(err.at[0, 0, pl.ds(block, 1)], mr_v.at[pl.ds(slot, 1)], sems.at[2]).start()
        return carry

    lax.fori_loop(0, slots, fetch_own, 0, unroll=32)
    owned = [
        pltpu.make_async_copy(params.at[0], p_v, sems.at[3]),
        pltpu.make_async_copy(estimate.at[0], e_v, sems.at[4]),
    ]
    for copy in owned:
        copy.start()

    for copy in memory:
        copy.wait()
    add_gradient(cot_v, act_v, err_a, slice(0, split), per_row, scale)
    clear_kept(err_a, list_s, count_s, me, own_blocks, 0, spare)

    blocks = as_column(g_v[...])
    filled = lax.broadcasted_iota(I32, (g_slots, 1), 0) < gc_s[silo]
    kept_here = lax.broadcasted_iota(I32, (slots, 1), 0) < count_s[me, me]
    for shift in range(shards):
        sender = lax.rem(me - shift + shards, shards)
        same = onehot((blocks == list_v[sender, pl.ds(me, 1), :]) & filled)
        if shift == 0:
            own = same
        else:
            match[:, (shift - 1) * slots : shift * slots] = same
    pltpu.make_async_copy(pr_v, pr_v, sems.at[0]).wait()
    pltpu.make_async_copy(er_v, er_v, sems.at[1]).wait()
    pltpu.make_async_copy(mr_v, mr_v, sems.at[2]).wait()
    rows = jnp.where(kept_here, mr_v[...] + grad[...], 0.0)
    mine[...] = rows
    base[...] = jnp.where(filled, pr_v[...] - er_v[...], 0.0) - LEARN_RATE * pick(own, thirds(rows))
    for copy in owned:
        copy.wait()


def base_rows(
    shards, own_blocks, per_row, scale, split,
    lists, counts, g_lists, g_counts, params, estimate, err, grad, act_v, cot_v,
):
    slots, width = grad.shape
    g_slots = g_lists.shape[2]
    owned = params.shape[1:]
    return pl.pallas_call(
        functools.partial(base_kernel, shards, own_blocks, per_row, scale, split),
        name="gossip_base",
        in_specs=[ANY] * 7 + [IN_VMEM] * 3,
        out_specs=[IN_VMEM] * 6,
        out_shape=[
            pltpu.VMEM((g_slots, width), F32),
            pltpu.VMEM((g_slots, (shards - 1) * slots), BF16),
            pltpu.VMEM((slots, width), F32),
            pltpu.VMEM(owned, F32),
            pltpu.VMEM(owned, F32),
            pltpu.VMEM((width // 128, split * per_row + 8, 128), F32),
        ],
        scratch_shapes=[
            pltpu.SMEM((shards, slots), I32),
            pltpu.SMEM((shards, shards), I32),
            pltpu.VMEM((shards, shards, slots), I32),
            pltpu.SMEM((1, g_slots), I32),
            pltpu.VMEM((1, g_slots), I32),
            pltpu.SMEM(g_counts.shape, I32),
            pltpu.VMEM((g_slots, width), F32),
            pltpu.VMEM((g_slots, width), F32),
            pltpu.VMEM((slots, width), F32),
            pltpu.SemaphoreType.DMA((6 + width // 128,)),
        ],
        compiler_params=pltpu.CompilerParams(vmem_limit_bytes=16 * MIB),
    )(lists, counts, g_lists, g_counts, params, estimate, err, grad, act_v, cot_v)


def delta_kernel(base, match, *refs):
    *arrived, out = refs
    slots = arrived[0].shape[0]
    total = base[...]
    for place, rows in enumerate(arrived):
        same = match[:, place * slots : (place + 1) * slots]
        total = total - LEARN_RATE * pick(same, thirds(rows[...]))
    out[...] = total


def delta_rows(base, match, arrived):
    return pl.pallas_call(
        delta_kernel,
        name="delta_rows",
        in_specs=[IN_VMEM] * (2 + len(arrived)),
        out_specs=IN_VMEM,
        out_shape=pltpu.VMEM(base.shape, F32),
        compiler_params=pltpu.CompilerParams(vmem_limit_bytes=8 * MIB),
    )(base, match, *arrived)


def dense_kernel(
    shards, silos, own_blocks, per_row, scale, split,
    lists, counts, g_lists, err, mixed, p_v, e_v, act_v, cot_v, err_a, delta, *refs
):
    kept = refs[:shards]
    (err_out, est_out, mixed_pre, params_pre, spread,
     list_s, count_s, list_v, g_v, err_b, m_v, est_v, sems) = refs[shards:]
    me = lax.axis_index("shard")
    silo = lax.axis_index("silo")
    width = delta.shape[1]
    width_out = cot_v.shape[1]
    out_rows = p_v.shape[0]
    halves = width // 128
    done, rest = split * per_row, (width_out - split) * per_row
    small = [
        pltpu.make_async_copy(lists.at[0, me], list_s, sems.at[0]),
        pltpu.make_async_copy(lists.at[0], list_v, sems.at[1]),
        pltpu.make_async_copy(counts.at[0], count_s, sems.at[2]),
        pltpu.make_async_copy(g_lists, g_v, sems.at[3]),
    ]
    memory = memory_copies(err, err_b, done, rest, [sems.at[5 + half] for half in range(halves)])
    mixed_copy = pltpu.make_async_copy(mixed.at[0], m_v, sems.at[4])
    stores = [
        pltpu.make_async_copy(
            err_a.at[half, pl.ds(0, done)],
            err_out.at[0, 0, pl.ds(0, done), pl.ds(half * 128, 128)],
            sems.at[5 + halves + half],
        )
        for half in range(halves)
    ]
    for copy in small + memory + [mixed_copy] + stores:
        copy.start()
    for copy in memory:
        copy.wait()
    add_gradient(cot_v, act_v, err_b, slice(split, width_out), per_row, scale)
    for copy in small:
        copy.wait()
    clear_kept(err_b, list_s, count_s, me, own_blocks, done, rest)
    for half in range(halves):
        copy = pltpu.make_async_copy(
            err_b.at[half, pl.ds(0, rest)],
            err_out.at[0, 0, pl.ds(done, rest), pl.ds(half * 128, 128)],
            sems.at[5 + half],
        )
        copy.start()
        stores.append(copy)

    first, second = neighbours(silo, silos)
    kept_parts = thirds(jnp.concatenate([rows[...] for rows in kept], axis=0))
    kept_ids = jnp.concatenate(
        [list_v[lax.rem(me - shift + shards, shards), pl.ds(me, 1), :] for shift in range(shards)], axis=1
    )
    delta_parts = thirds(delta[...])
    own_ids = g_v[silo]
    next_ids = jnp.concatenate([g_v[first], g_v[second]], axis=1)
    mixed_copy.wait()
    for part in range(per_row):
        lanes = slice(part * width, (part + 1) * width)

        def places(ids):
            here = lax.broadcasted_iota(I32, (out_rows, ids.shape[1]), 0) * per_row + part
            return onehot(here == ids)

        grad = pick(places(kept_ids), kept_parts)
        change = pick(places(own_ids), delta_parts)
        spread[part * out_rows : (part + 1) * out_rows, :] = places(next_ids)
        half_step = p_v[:, lanes] - LEARN_RATE * grad
        est = e_v[:, lanes] + change
        mix = m_v[:, lanes] + MIX_WEIGHT * change
        est_v[:, lanes] = est
        mixed_pre[:, lanes] = mix
        params_pre[:, lanes] = half_step + CONSENSUS * (mix - est)
    est_copy = pltpu.make_async_copy(est_v, est_out.at[0], sems.at[4])
    est_copy.start()
    for copy in stores:
        copy.wait()
    est_copy.wait()


def dense(
    shards, silos, own_blocks, per_row, scale, split,
    lists, counts, g_lists, err, mixed, p_v, e_v, act_v, cot_v, err_a, delta, kept,
):
    slots = lists.shape[3]
    g_slots = g_lists.shape[2]
    width = err.shape[3]
    owned = p_v.shape
    rest = (cot_v.shape[1] - split) * per_row
    return pl.pallas_call(
        functools.partial(dense_kernel, shards, silos, own_blocks, per_row, scale, split),
        name="dense",
        in_specs=[ANY] * 5 + [IN_VMEM] * (6 + shards),
        out_specs=[ANY, ANY, IN_VMEM, IN_VMEM, IN_VMEM],
        out_shape=[
            pltpu.HBM(err.shape, F32),
            pltpu.HBM(mixed.shape, F32),
            pltpu.VMEM(owned, F32),
            pltpu.VMEM(owned, F32),
            pltpu.VMEM((own_blocks, 2 * g_slots), BF16),
        ],
        scratch_shapes=[
            pltpu.SMEM((shards, slots), I32),
            pltpu.SMEM((shards, shards), I32),
            pltpu.VMEM((shards, shards, slots), I32),
            pltpu.VMEM(g_lists.shape, I32),
            pltpu.VMEM((width // 128, rest + 8, 128), F32),
            pltpu.VMEM(owned, F32),
            pltpu.VMEM(owned, F32),
            pltpu.SemaphoreType.DMA((5 + 2 * (width // 128),)),
        ],
        compiler_params=pltpu.CompilerParams(vmem_limit_bytes=24 * MIB),
    )(lists, counts, g_lists, err, mixed, p_v, e_v, act_v, cot_v, err_a, delta, *kept)


def final_kernel(per_row, mixed_pre, params_pre, spread, first, second, mixed_out, params_out, m_v, p_v, sems):
    out_rows = m_v.shape[0]
    width = m_v.shape[1] // per_row
    parts = thirds(jnp.concatenate([first[...], second[...]], axis=0))
    copies = []
    for part in range(per_row):
        lanes = slice(part * width, (part + 1) * width)
        change = pick(spread[part * out_rows : (part + 1) * out_rows, :], parts)
        m_v[:, lanes] = mixed_pre[:, lanes] + MIX_WEIGHT * change
        p_v[:, lanes] = params_pre[:, lanes] + (CONSENSUS * MIX_WEIGHT) * change
        pair = [
            pltpu.make_async_copy(m_v.at[:, lanes], mixed_out.at[0, :, lanes], sems.at[2 * part]),
            pltpu.make_async_copy(p_v.at[:, lanes], params_out.at[0, :, lanes], sems.at[2 * part + 1]),
        ]
        for copy in pair:
            copy.start()
        copies += pair
    for copy in copies:
        copy.wait()


def final(per_row, shape, mixed_pre, params_pre, spread, first, second):
    return pl.pallas_call(
        functools.partial(final_kernel, per_row),
        name="neighbours",
        in_specs=[IN_VMEM] * 5,
        out_specs=[ANY] * 2,
        out_shape=[pltpu.HBM(shape, F32)] * 2,
        scratch_shapes=[
            pltpu.VMEM(mixed_pre.shape, F32),
            pltpu.VMEM(mixed_pre.shape, F32),
            pltpu.SemaphoreType.DMA((2 * per_row,)),
        ],
        compiler_params=pltpu.CompilerParams(vmem_limit_bytes=20 * MIB),
    )(mixed_pre, params_pre, spread, first, second)


def neighbours(silo, silos):
    lower, upper = lax.rem(silo + silos - 1, silos), lax.rem(silo + 1, silos)
    if silos % 2:
        return lower, upper
    even = lax.rem(silo, 2) == 0
    return jnp.where(even, upper, lower), jnp.where(even, lower, upper)


def exchange(rows, silos):
    if silos % 2:
        routes = [[(a, (a + 1) % silos) for a in range(silos)], [(a, (a - 1) % silos) for a in range(silos)]]
    else:
        routes = [
            [(a, a ^ 1) for a in range(silos)],
            [(a, (a + 1 if a % 2 else a - 1) % silos) for a in range(silos)],
        ]
    far = lax.ppermute(rows, "silo", routes[1])
    near = lax.ppermute(rows, "silo", routes[0])
    return near, far


def body(
    activ, cotangent, error_memory, params, estimate, mixed,
    kept_blocks, kept_counts, gossip_blocks, gossip_counts,
):
    shards = lax.axis_size("shard")
    silos = lax.axis_size("silo")
    nblocks, block_len = error_memory.shape[2:]
    own_blocks = nblocks // shards
    per_row = activ.shape[1] // block_len
    scale = activ.shape[1] ** (-0.5)
    split = cotangent.shape[1] // 2 // 128 * 128
    activ, cotangent, error_memory, params, estimate, mixed, kept_blocks, kept_counts, gossip_blocks, gossip_counts = (
        pltpu.with_memory_space_constraint(array, pltpu.HBM)
        for array in (
            activ, cotangent, error_memory, params, estimate, mixed,
            kept_blocks, kept_counts, gossip_blocks, gossip_counts.reshape(silos),
        )
    )
    grad, *outgoing, act_v, cot_v = select(
        shards, own_blocks, per_row, scale, kept_blocks, kept_counts, activ, cotangent, error_memory
    )
    arrived = [
        lax.ppermute(rows, "shard", [(r, (r + shift) % shards) for r in range(shards)])
        for shift, rows in enumerate(outgoing, 1)
    ]
    base, match, mine, p_v, e_v, err_a = base_rows(
        shards, own_blocks, per_row, scale, split, kept_blocks, kept_counts, gossip_blocks, gossip_counts,
        params, estimate, error_memory, grad, act_v, cot_v,
    )
    delta = delta_rows(base, match, arrived)
    first, second = exchange(delta, silos)
    error_out, estimate_out, mixed_pre, params_pre, spread = dense(
        shards, silos, own_blocks, per_row, scale, split, kept_blocks, kept_counts, gossip_blocks,
        error_memory, mixed, p_v, e_v, act_v, cot_v, err_a, delta, [mine, *arrived],
    )
    mixed_out, params_out = final(per_row, mixed.shape, mixed_pre, params_pre, spread, first, second)
    return params_out, estimate_out, mixed_out, error_out


def solution(mesh):
    in_specs = (
        P(("silo", "shard"), None),
        P(("silo", "shard"), None),
        P("silo", "shard", None, None),
        P("silo", "shard", None),
        P("silo", "shard", None),
        P("silo", "shard", None),
        P("silo", None, None, None),
        P("silo", None, None),
        P(None, "shard", None),
        P(None, "shard"),
    )
    out_specs = (
        P("silo", "shard", None),
        P("silo", "shard", None),
        P("silo", "shard", None),
        P("silo", "shard", None, None),
    )
    return jax.shard_map(body, mesh=mesh, in_specs=in_specs, out_specs=out_specs, check_vma=False)
```

time: 40 us -> 25.3 us (0.63)
  local copies, waits for them, and re-layouts: 14.9 us -> 0 us
  starting transfers between devices: 6.79 us -> 7.73 us
    unnamed x35 -> x0, local copies, waits for them, and re-layouts: 14.9 us -> none
    pallas_call x1, Pallas kernels: 4.81 us -> 3.07 us  [select(): pl.pallas_call(functools.partial(select_kernel, shards, own_blocks, per_r...]
    pallas_call x1, Pallas kernels: 2.84 us -> 4.56 us  [base_rows(): pl.pallas_call(functools.partial(base_kernel, shards, own_blocks, per_row...]
    ppermute x1, starting transfers between devices: 3.78 us -> 4.66 us  [exchange(): far = lax.ppermute(rows, 'silo', routes[1])]
  transfers between devices with their start and end apart: 3 -> 3, of which waited for: 0 -> 0; matrix products, arithmetic and copies ran while one was open for 0% -> 0% of each run, Pallas kernels for 25% -> 45%
where the time goes in v2:
time: 25.3 us; the launch traced here: 25.1 us
  Pallas kernels  16.7 us (66%)
  starting transfers between devices  7.73 us (31%)
  between operations  0.69 us (3%)
    pallas_call x1, Pallas kernels, dense(): pl.pallas_call(functools.partial(dense_kernel, shards, silos, own_blocks,...  6.64 us
    ppermute x1, starting transfers between devices, exchange(): far = lax.ppermute(rows, 'silo', routes[1])  4.66 us
    pallas_call x1, Pallas kernels, base_rows(): pl.pallas_call(functools.partial(base_kernel, shards, own_blocks, per_row...  4.56 us
    pallas_call x1, Pallas kernels, select(): pl.pallas_call(functools.partial(select_kernel, shards, own_blocks, per_r...  3.07 us
    ppermute x1, starting transfers between devices, body(): lax.ppermute(rows, 'shard', [(r, (r + shift) % shards) for r in range(sha...  3 us
    pallas_call x1, Pallas kernels, final(): pl.pallas_call(functools.partial(final_kernel, per_row), name='neighbours...  2.21 us
  transfers between devices with their start and end apart: 3, of which 0 were waited for; matrix products, arithmetic and copies ran while one was open for 0% of the time, Pallas kernels for 45%

profile of v2, /device:TPU:0, one launch (start us, length us, event | category | flops | bytes accessed | tf_op | source)
XLA Modules:
  0.0 25.1 jit_solution(10209548646199503374)
XLA Ops:
  0.6 3.1 %kept_rows.1 = (f32[64,256]{1,0:T(8,128)S(1)}, f32[64,256]{1,0:T(8,128)S(1)}, bf16[1024,1280]{1,0:T(8,128)(2,1)S(1)}, bf16[1024,640]{1,0:T(8,128)(2,1)S(1)}) custom-call(s32[1,2,2,64]{3,2,1,0:T(2,128)} %lists.5, s32[1,2,2]{2,1,0:T(2,128)} %counts.5, bf16[1024,1280]{1,0:T(8,128)(2,1)} %act.1, bf16[1024,640]{1,0:T(8,128)(2,1)} %cot.1, f32[1,1,3200,256]{3,2,1,0:T(8,128)} %err.5), custom_call_target="tpu_custom_call" | custom-call | tf_op jit(solution)/shard_map/kept_rows/pallas_call | solution.py:128
  3.7 3.0 %collective-permute-start = (f32[64,256]{1,0:T(8,128)S(1)}, f32[64,256]{1,0:T(8,128)S(1)}, u32[]{:S(2)}, u32[]{:S(2)}) collective-permute-start(f32[64,256]{1,0:T(8,128)S(1)} %get-tuple-element.29), channel_id=1, source_target_pairs={{0,1},{1,0},{2,3},{3,2},{4,5},{5,4},{6,7},{7,6},{8,9},{9,8},{10,11... | collective-permute-start | bytes 196616 | tf_op jit(solution)/shard_map/ppermute | solution.py:514
  6.7 4.6 %gossip_base.1 = (f32[128,256]{1,0:T(8,128)S(1)}, bf16[128,64]{1,0:T(8,128)(2,1)S(1)}, f32[64,256]{1,0:T(8,128)S(1)}, f32[320,1280]{1,0:T(8,128)S(1)}, f32[320,1...) custom-call(s32[1,2,2,64]{3,2,1,0:T(2,128)} %lists.5, s32[1,2,2]{2,1,0:T(2,128)} %counts.5, s32[16,1,128]{2,1,0:T(1,128)} %g_lists.3, ...), custom_call_target="tpu_custom_call" | custom-call | tf_op jit(solution)/shard_map/gossip_base/pallas_call | solution.py:270
  11.3 0.0 collective-permute-done.refs_0_.refs_1_
  11.3 0.2 delta_rows.1.delta
  11.5 0.1 collective-permute-start.1
  11.6 4.7 %collective-permute-start.2 = (f32[128,256]{1,0:T(8,128)S(1)}, f32[128,256]{1,0:T(8,128)S(1)}, u32[]{:S(2)}, u32[]{:S(2)}) collective-permute-start(f32[128,256]{1,0:T(8,128)S(1)} %delta_rows.1.delta), channel_id=1, source_target_pairs={{0,30},{2,4},{4,2},{6,8},{8,6},{10,12},{12,10},{14,16},{16,14},{18... | collective-permute-start | bytes 393224 | tf_op jit(solution)/shard_map/ppermute | solution.py:487
  16.2 6.6 %dense.1 = (f32[1,1,3200,256]{3,2,1,0:T(8,128)}, f32[1,320,1280]{2,1,0:T(8,128)}, f32[320,1280]{1,0:T(8,128)S(1)}, f32[320,1280]{1,0:T(8,128)S(1)}, bf16[1600,256]{1,0:T(8,128)(2,1)S(1)}) custom-call(s32[1,2,2,64]{3,2,1,0:T(2,128)} %lists.5, s32[1,2,2]{2,1,0:T(2,128)} %counts.5, s32[16,1,128]{2,1,0:T(1,128)} %g_lists.3, f32[1,1,3200,256]{3,2,1,0:T(8,128)} %err.5, ...), custom_call_target="tpu_custom_call" | custom-call | tf_op jit(solution)/shard_map/dense/pallas_call | solution.py:408
  22.9 0.0 collective-permute-done.1.first
  22.9 0.0 collective-permute-done.2.second
  22.9 2.2 %neighbours.1 = (f32[1,320,1280]{2,1,0:T(8,128)}, f32[1,320,1280]{2,1,0:T(8,128)}) custom-call(f32[320,1280]{1,0:T(8,128)S(1)} %get-tuple-element.31.mixed_pre, f32[320,1280]{1,0:T(8,128)S(1)} %get-tuple-element.32.params_pre, bf16[1600,256]{1,0:T(8,128)(2,1)S(1)} %get-tuple-element.33.spread, f32[128,256]{1,0:T(8,128)S(1)} %collective-permute-done.1.first, ...), custom_call_target="tpu_custom_call" | custom-call | tf_op jit(solution)/shard_map/neighbours/pallas_call | solution.py:456
Async XLA Ops:
  3.7 7.6 %collective-permute-start = (f32[64,256]{1,0:T(8,128)S(1)}, f32[64,256]{1,0:T(8,128)S(1)}, u32[]{:S(2)}, u32[]{:S(2)}) collective-permute-start(f32[64,256]{1,0:T(8,128)S(1)} %get-tuple-element.29), channel_id=1, source_target_pairs={{0,1},{1,0},{2,3},{3,2},{4,5},{5,4},{6,7},{7,6},{8,9},{9,8},{10,11... | collective-permute-start | bytes 196616 | tf_op jit(solution)/shard_map/ppermute | solution.py:514
  11.5 11.4 %collective-permute-start.1 = (f32[128,256]{1,0:T(8,128)S(1)}, f32[128,256]{1,0:T(8,128)S(1)}, u32[]{:S(2)}, u32[]{:S(2)}) collective-permute-start(f32[128,256]{1,0:T(8,128)S(1)} %delta_rows.1.delta), channel_id=1, source_target_pairs={{0,2},{2,0},{4,6},{6,4},{8,10},{10,8},{12,14},{14,12},{16,18},{18,... | collective-permute-start | bytes 393224 | tf_op jit(solution)/shard_map/ppermute | solution.py:488
  11.6 11.3 %collective-permute-start.2 = (f32[128,256]{1,0:T(8,128)S(1)}, f32[128,256]{1,0:T(8,128)S(1)}, u32[]{:S(2)}, u32[]{:S(2)}) collective-permute-start(f32[128,256]{1,0:T(8,128)S(1)} %delta_rows.1.delta), channel_id=1, source_target_pairs={{0,30},{2,4},{4,2},{6,8},{8,6},{10,12},{12,10},{14,16},{16,14},{18... | collective-permute-start | bytes 393224 | tf_op jit(solution)/shard_map/ppermute | solution.py:487

commit v3 on v1

v3 whole, which is shorter than its diff:
```python
import functools

import jax
import jax.numpy as jnp
from jax import lax
from jax.experimental import pallas as pl
from jax.experimental.pallas import tpu as pltpu
from jax.sharding import PartitionSpec as P

LEARN_RATE = 0.25
CONSENSUS = 0.5
MIX_WEIGHT = 1.0 / 3.0

F32, BF16, I32 = jnp.float32, jnp.bfloat16, jnp.int32
ANY = pl.BlockSpec(memory_space=pl.ANY)
IN_VMEM = pl.BlockSpec(memory_space=pltpu.VMEM)
MIB = 1 << 20


def dot(a, b, dims=((1,), (0,))):
    return lax.dot_general(a, b, (dims, ((), ())), preferred_element_type=F32)


def as_column(row):
    n = row.shape[1]
    eye = lax.broadcasted_iota(I32, (n, n), 0) == lax.broadcasted_iota(I32, (n, n), 1)
    spread = jnp.where(eye, jnp.broadcast_to(row.astype(F32), (n, n)), 0.0)
    return jnp.sum(spread, axis=1, keepdims=True).astype(I32)


def split(rows):
    high = rows.astype(BF16)
    return jnp.concatenate([high, (rows - high.astype(F32)).astype(BF16)], axis=0)


def pick(choice, rows):
    return dot(jnp.concatenate([choice, choice], axis=1), rows)


def onehot(mask):
    return jnp.where(mask, 1.0, 0.0).astype(BF16)


def divide(value, by):
    return (value * ((1 << 16) // by + 1)) >> 16


def rows_kernel(shards, own_blocks, per_row, scale, lists, counts, g_lists, act, cot, err, *refs):
    outs = refs[: shards - 1]
    act_v, cot_v, lists_v, g_v, list_s, count_s, err_v, sems = refs[shards - 1 :]
    me = lax.axis_index("shard")
    slots = lists_v.shape[2]
    width = err_v.shape[1]
    parts = 4
    step = act_v.shape[0] // parts
    small = [
        pltpu.make_async_copy(lists.at[0, me], list_s, sems.at[0]),
        pltpu.make_async_copy(lists.at[0], lists_v, sems.at[1]),
        pltpu.make_async_copy(counts.at[0], count_s, sems.at[2]),
        pltpu.make_async_copy(g_lists, g_v, sems.at[3]),
    ]
    for copy in small:
        copy.start()
    big = []
    for part in range(parts):
        rows = pl.ds(part * step, step)
        pair = [
            pltpu.make_async_copy(cot.at[rows], cot_v.at[rows], sems.at[4 + 2 * part]),
            pltpu.make_async_copy(act.at[rows], act_v.at[rows], sems.at[5 + 2 * part]),
        ]
        for copy in pair:
            copy.start()
        big.append(pair)
    for copy in small:
        copy.wait()

    columns, fills = [], []
    for shift in range(1, shards):
        owner = lax.rem(me + shift, shards)

        def fetch(slot, carry, owner=owner, shift=shift):
            block = owner * own_blocks + list_s[owner, slot]
            into = err_v.at[pl.ds((shift - 1) * slots + slot, 1)]
            pltpu.make_async_copy(err.at[0, 0, pl.ds(block, 1)], into, sems.at[0]).start()
            return carry

        lax.fori_loop(0, slots, fetch, 0, unroll=slots)
        row = lists_v[me, pl.ds(owner, 1), :] + owner * own_blocks
        columns.append(as_column(row))
        slot_ids = lax.broadcasted_iota(I32, (slots, 1), 0)
        fills.append(slot_ids < count_s[me, owner])
    blocks = jnp.concatenate(columns, axis=0)
    filled = jnp.concatenate(fills, axis=0)
    out_row = divide(blocks, per_row)
    segment = blocks - out_row * per_row
    total = blocks.shape[0]
    chosen = onehot(lax.broadcasted_iota(I32, (total, cot_v.shape[1]), 1) == out_row)
    acc = jnp.zeros((total, act_v.shape[1]), F32)
    for part in range(parts):
        for copy in big[part]:
            copy.wait()
        rows = pl.ds(part * step, step)
        picked = dot(chosen, cot_v[rows, :], ((1,), (1,))).astype(BF16)
        acc = acc + dot(picked, act_v[rows, :])
    grad = jnp.zeros((total, width), F32)
    for part in range(per_row):
        grad = jnp.where(segment == part, acc[:, part * width : (part + 1) * width], grad)
    pltpu.make_async_copy(err_v, err_v, sems.at[0]).wait()
    pending = jnp.where(filled, err_v[...] + grad * scale, 0.0)
    for place, out in enumerate(outs):
        out[...] = pending[place * slots : (place + 1) * slots]


def moving_rows(shards, own_blocks, per_row, scale, lists, counts, g_lists, act, cot, err):
    slots = lists.shape[3]
    width = err.shape[3]
    return pl.pallas_call(
        functools.partial(rows_kernel, shards, own_blocks, per_row, scale),
        name="moving_rows",
        in_specs=[ANY] * 6,
        out_specs=[IN_VMEM] * (shards + 3),
        out_shape=[pltpu.VMEM((slots, width), F32)] * (shards - 1)
        + [
            pltpu.VMEM(act.shape, BF16),
            pltpu.VMEM(cot.shape, BF16),
            pltpu.VMEM(lists.shape[1:], I32),
            pltpu.VMEM(g_lists.shape, I32),
        ],
        scratch_shapes=[
            pltpu.SMEM((shards, slots), I32),
            pltpu.SMEM((shards, shards), I32),
            pltpu.VMEM(((shards - 1) * slots, width), F32),
            pltpu.SemaphoreType.DMA((12,)),
        ],
        compiler_params=pltpu.CompilerParams(vmem_limit_bytes=16 * MIB),
    )(lists, counts, g_lists, act, cot, err)


def take_kept(err_v, rows_v, list_s, count_s, me, own_blocks):
    shards, slots = list_s.shape
    halves = range(err_v.shape[0])

    def take(slot, carry):
        block = me * own_blocks + list_s[me, slot]
        for half in halves:
            rows_v[half, pl.ds(slot, 1), :] = err_v[half, pl.ds(block, 1), :]
        return carry

    lax.fori_loop(0, slots, take, 0, unroll=slots)
    for owner in range(shards):
        limit = count_s[me, owner]

        def clear(slot, carry, owner=owner, limit=limit):
            block = jnp.where(slot < limit, owner * own_blocks + list_s[owner, slot], shards * own_blocks)
            for half in halves:
                err_v[half, pl.ds(block, 1), :] = jnp.zeros((1, 128), F32)
            return carry

        lax.fori_loop(0, slots, clear, 0, unroll=slots)


def gradient_kernel(
    shards, own_blocks, per_row, scale,
    lists, counts, g_lists, g_counts, err, params, estimate, mixed, lists_v, g_v, act_v, cot_v,
    mine, base, match, err_v, p_v, e_v, m_v,
    list_s, count_s, g_s, gc_s, rows_v, grad_v, sems,
):
    me = lax.axis_index("shard")
    silo = lax.axis_index("silo")
    slots, width = mine.shape
    g_slots = g_v.shape[2]
    tile = 128
    tiles = cot_v.shape[1] // tile
    step = tile * per_row
    halves = err_v.shape[0]
    small = [
        pltpu.make_async_copy(g_counts, gc_s, sems.at[0]),
        pltpu.make_async_copy(counts.at[0], count_s, sems.at[1]),
        pltpu.make_async_copy(lists.at[0, me], list_s, sems.at[2]),
        pltpu.make_async_copy(g_lists.at[silo], g_s, sems.at[6]),
    ]
    for copy in small:
        copy.start()
    memory = []
    for part in range(tiles):
        rows = pl.ds(part * step, step)
        memory.append(
            [
                pltpu.make_async_copy(
                    err.at[0, 0, rows, pl.ds(half * 128, 128)],
                    err_v.at[half, rows],
                    sems.at[7 + part * halves + half],
                )
                for half in range(halves)
            ]
        )
    for copy in sum(memory, []):
        copy.start()
    out_rows = params.shape[1]
    owned = [
        pltpu.make_async_copy(
            array.at[0, :, pl.ds(chunk * 128, 128)], array_v.at[pl.ds(chunk * out_rows, out_rows)], sems.at[3 + place]
        )
        for place, (array, array_v) in enumerate([(params, p_v), (estimate, e_v), (mixed, m_v)])
        for chunk in range(per_row * halves)
    ]

    for copy in owned:
        copy.start()
    ahead = tiles - 1

    def tile_gradient(part):
        columns = pl.ds(pl.multiple_of(part * tile, tile), tile)
        return dot(cot_v[:, columns], act_v[...], ((0,), (0,))) * scale

    def pieces(grad, part):
        for seg in range(per_row):
            for half in range(halves):
                lane = (seg * halves + half) * 128
                yield (half, pl.ds(part * step + seg, tile, stride=per_row)), grad[:, lane : lane + 128]

    def store(part, carry):
        for where, piece in pieces(tile_gradient(part), part):
            grad_v[where] = piece
        return carry

    lax.fori_loop(0, ahead, store, 0)
    for copy in sum(memory, []):
        copy.wait()
    for where, piece in pieces(tile_gradient(ahead), ahead):
        err_v[where] = err_v[where] + piece
    for half in range(halves):
        err_v[half, : ahead * step, :] = err_v[half, : ahead * step, :] + grad_v[half]
    for copy in small:
        copy.wait()
    take_kept(err_v, rows_v, list_s, count_s, me, own_blocks)
    kept = lax.broadcasted_iota(I32, (slots, 1), 0) < count_s[me, me]
    mine[...] = jnp.where(kept, jnp.concatenate([rows_v[half, :slots] for half in range(halves)], axis=1), 0.0)
    blocks = as_column(g_v[silo])
    filled = lax.broadcasted_iota(I32, (g_slots, 1), 0) < gc_s[silo]
    for shift in range(shards):
        sender = lax.rem(me - shift + shards, shards)
        ids = lists_v[sender, pl.ds(me, 1), :]
        same = onehot((blocks == jnp.concatenate([ids, ids], axis=1)) & filled)
        if shift == 0:
            own = dot(same, split(mine[...]))
        else:
            match[:, 2 * (shift - 1) * slots : 2 * shift * slots] = same
    for copy in owned:
        copy.wait()

    def gather(slot, carry):
        block = g_s[0, slot]
        row = divide(block, per_row)
        start = (block - row * per_row) * (halves * out_rows) + row
        for half in range(halves):
            where = pl.ds(start + half * out_rows, 1)
            rows_v[half, pl.ds(slot, 1), :] = p_v[where, :] - e_v[where, :]
        return carry

    lax.fori_loop(0, g_slots, gather, 0, unroll=g_slots)
    rows = jnp.concatenate([rows_v[half, :g_slots] for half in range(halves)], axis=1)
    base[...] = jnp.where(filled, rows, 0.0) - LEARN_RATE * own


def gradient(
    shards, own_blocks, per_row, scale,
    lists, counts, g_lists, g_counts, err, params, estimate, mixed, lists_v, g_v, act_v, cot_v,
):
    slots = lists.shape[3]
    width = err.shape[3]
    g_slots = g_v.shape[2]
    owned = (params.shape[1] * params.shape[2] // 128, 128)
    halves = width // 128
    return pl.pallas_call(
        functools.partial(gradient_kernel, shards, own_blocks, per_row, scale),
        name="gradient",
        in_specs=[ANY] * 8 + [IN_VMEM] * 4,
        out_specs=[IN_VMEM] * 7,
        out_shape=[
            pltpu.VMEM((slots, width), F32),
            pltpu.VMEM((g_slots, width), F32),
            pltpu.VMEM((g_slots, 2 * (shards - 1) * slots), BF16),
            pltpu.VMEM((halves, shards * own_blocks + 8, 128), F32),
            pltpu.VMEM(owned, F32),
            pltpu.VMEM(owned, F32),
            pltpu.VMEM(owned, F32),
        ],
        scratch_shapes=[
            pltpu.SMEM((shards, slots), I32),
            pltpu.SMEM((shards, shards), I32),
            pltpu.SMEM((1, g_slots), I32),
            pltpu.SMEM(g_counts.shape, I32),
            pltpu.VMEM((halves, max(slots, g_slots), 128), F32),
            pltpu.VMEM((halves, (cot_v.shape[1] - 128) * per_row, 128), F32),
            pltpu.SemaphoreType.DMA((7 + cot_v.shape[1] // 128 * halves,)),
        ],
        compiler_params=pltpu.CompilerParams(vmem_limit_bytes=16 * MIB),
    )(lists, counts, g_lists, g_counts, err, params, estimate, mixed, lists_v, g_v, act_v, cot_v)


def delta_kernel(base, match, *refs):
    *arrived, out = refs
    rows = jnp.concatenate([split(each[...]) for each in arrived], axis=0)
    out[...] = base[...] - LEARN_RATE * dot(match[...], rows)


def delta_rows(base, match, arrived):
    return pl.pallas_call(
        delta_kernel,
        name="delta_rows",
        in_specs=[IN_VMEM] * (2 + len(arrived)),
        out_specs=IN_VMEM,
        out_shape=pltpu.VMEM(base.shape, F32),
        compiler_params=pltpu.CompilerParams(vmem_limit_bytes=8 * MIB),
    )(base, match, *arrived)


def own_kernel(shards, silos, per_row, lists_v, g_v, err_v, p_v, e_v, m_v, delta, *refs):
    kept = refs[:shards]
    err_out, est_out, mixed_pre, params_pre, spread, est_v, sems = refs[shards:]
    me = lax.axis_index("shard")
    silo = lax.axis_index("silo")
    width = delta.shape[1]
    halves = err_v.shape[0]
    out_rows = p_v.shape[0] // (per_row * halves)
    nblocks = err_out.shape[2]
    copies = [
        pltpu.make_async_copy(
            err_v.at[half, pl.ds(0, nblocks)], err_out.at[0, 0, :, pl.ds(half * 128, 128)], sems.at[half]
        )
        for half in range(err_v.shape[0])
    ]
    for copy in copies:
        copy.start()
    first, second = neighbours(silo, silos)
    kept_parts = split(jnp.concatenate([rows[...] for rows in kept], axis=0))
    kept_ids = jnp.concatenate(
        [lists_v[lax.rem(me - shift + shards, shards), pl.ds(me, 1), :] for shift in range(shards)], axis=1
    )
    delta_parts = split(delta[...])
    own_ids = g_v[silo]
    next_ids = jnp.concatenate([g_v[first], g_v[second]], axis=1)
    for part in range(per_row):
        lanes = slice(part * width, (part + 1) * width)

        def places(ids):
            here = lax.broadcasted_iota(I32, (out_rows, ids.shape[1]), 0) * per_row + part
            return onehot(here == ids)

        grad = pick(places(kept_ids), kept_parts)
        change = pick(places(own_ids), delta_parts)
        p, e, m = (
            jnp.concatenate(
                [
                    array[(part * halves + half) * out_rows : (part * halves + half + 1) * out_rows, :]
                    for half in range(halves)
                ],
                axis=1,
            )
            for array in (p_v, e_v, m_v)
        )
        half_step = p - LEARN_RATE * grad
        est = e + change
        mix = m + MIX_WEIGHT * change
        est_v[:, lanes] = est
        copy = pltpu.make_async_copy(est_v.at[:, lanes], est_out.at[0, :, lanes], sems.at[err_v.shape[0] + part])
        copy.start()
        copies.append(copy)
        mixed_pre[:, lanes] = mix
        params_pre[:, lanes] = half_step + CONSENSUS * (mix - est)
        spread[part * out_rows : (part + 1) * out_rows, :] = places(next_ids)
    for copy in copies:
        copy.wait()


def own_updates(shards, silos, per_row, err_shape, est_shape, lists_v, g_v, err_v, p_v, e_v, m_v, delta, kept):
    g_slots = g_v.shape[2]
    owned = est_shape[1:]
    return pl.pallas_call(
        functools.partial(own_kernel, shards, silos, per_row),
        name="own_updates",
        in_specs=[IN_VMEM] * (7 + shards),
        out_specs=[ANY, ANY, IN_VMEM, IN_VMEM, IN_VMEM],
        out_shape=[
            pltpu.HBM(err_shape, F32),
            pltpu.HBM(est_shape, F32),
            pltpu.VMEM(owned, F32),
            pltpu.VMEM(owned, F32),
            pltpu.VMEM((owned[0] * per_row, 2 * g_slots), BF16),
        ],
        scratch_shapes=[
            pltpu.VMEM(owned, F32),
            pltpu.SemaphoreType.DMA((err_v.shape[0] + per_row,)),
        ],
        compiler_params=pltpu.CompilerParams(vmem_limit_bytes=16 * MIB),
    )(lists_v, g_v, err_v, p_v, e_v, m_v, delta, *kept)


def final_kernel(per_row, mixed_pre, params_pre, spread, first, second, mixed_out, params_out, m_v, p_v, sems):
    out_rows = m_v.shape[0]
    width = m_v.shape[1] // per_row
    rows = split(jnp.concatenate([first[...], second[...]], axis=0))
    depth = spread.shape[1]
    copies = []
    for part in range(per_row):
        lanes = slice(part * width, (part + 1) * width)
        choice = spread[part * out_rows : (part + 1) * out_rows, :]
        change = dot(choice, rows[:depth]) + dot(choice, rows[depth:])
        m_v[:, lanes] = mixed_pre[:, lanes] + MIX_WEIGHT * change
        p_v[:, lanes] = params_pre[:, lanes] + (CONSENSUS * MIX_WEIGHT) * change
        pair = [
            pltpu.make_async_copy(m_v.at[:, lanes], mixed_out.at[0, :, lanes], sems.at[2 * part]),
            pltpu.make_async_copy(p_v.at[:, lanes], params_out.at[0, :, lanes], sems.at[2 * part + 1]),
        ]
        for copy in pair:
            copy.start()
        copies += pair
    for copy in copies:
        copy.wait()


def final(per_row, shape, mixed_pre, params_pre, spread, first, second):
    return pl.pallas_call(
        functools.partial(final_kernel, per_row),
        name="neighbours",
        in_specs=[IN_VMEM] * 5,
        out_specs=[ANY] * 2,
        out_shape=[pltpu.HBM(shape, F32)] * 2,
        scratch_shapes=[
            pltpu.VMEM(mixed_pre.shape, F32),
            pltpu.VMEM(mixed_pre.shape, F32),
            pltpu.SemaphoreType.DMA((2 * per_row,)),
        ],
        compiler_params=pltpu.CompilerParams(vmem_limit_bytes=20 * MIB),
    )(mixed_pre, params_pre, spread, first, second)


def neighbours(silo, silos):
    lower, upper = lax.rem(silo + silos - 1, silos), lax.rem(silo + 1, silos)
    if silos % 2:
        return lower, upper
    even = lax.rem(silo, 2) == 0
    return jnp.where(even, lower, upper), jnp.where(even, upper, lower)


def exchange(rows, silos):
    if silos % 2:
        routes = [[(a, (a + 1) % silos) for a in range(silos)], [(a, (a - 1) % silos) for a in range(silos)]]
    else:
        routes = [
            [(a, (a + 1 if a % 2 else a - 1) % silos) for a in range(silos)],
            [(a, a ^ 1) for a in range(silos)],
        ]
    far = lax.ppermute(rows, "silo", routes[0])
    near = lax.ppermute(rows, "silo", routes[1])
    return far, near


def body(
    activ, cotangent, error_memory, params, estimate, mixed,
    kept_blocks, kept_counts, gossip_blocks, gossip_counts,
):
    shards = lax.axis_size("shard")
    silos = lax.axis_size("silo")
    nblocks, block_len = error_memory.shape[2:]
    own_blocks = nblocks // shards
    per_row = activ.shape[1] // block_len
    scale = activ.shape[1] ** (-0.5)
    activ, cotangent, error_memory, params, estimate, mixed, kept_blocks, kept_counts, gossip_blocks, gossip_counts = (
        pltpu.with_memory_space_constraint(array, pltpu.HBM)
        for array in (
            activ, cotangent, error_memory, params, estimate, mixed,
            kept_blocks, kept_counts, gossip_blocks, gossip_counts.reshape(silos),
        )
    )
    *outgoing, act_v, cot_v, lists_v, g_v = moving_rows(
        shards, own_blocks, per_row, scale,
        kept_blocks, kept_counts, gossip_blocks, activ, cotangent, error_memory,
    )
    arrived = [
        lax.ppermute(rows, "shard", [(r, (r + shift) % shards) for r in range(shards)])
        for shift, rows in enumerate(outgoing, 1)
    ]
    mine, base, match, err_v, p_v, e_v, m_v = gradient(
        shards, own_blocks, per_row, scale, kept_blocks, kept_counts, gossip_blocks, gossip_counts,
        error_memory, params, estimate, mixed, lists_v, g_v, act_v, cot_v,
    )
    delta = delta_rows(base, match, arrived)
    first, second = exchange(delta, silos)
    error_out, estimate_out, mixed_pre, params_pre, spread = own_updates(
        shards, silos, per_row, error_memory.shape, estimate.shape,
        lists_v, g_v, err_v, p_v, e_v, m_v, delta, [mine, *arrived],
    )
    mixed_out, params_out = final(per_row, mixed.shape, mixed_pre, params_pre, spread, first, second)
    return params_out, estimate_out, mixed_out, error_out


def solution(mesh):
    in_specs = (
        P(("silo", "shard"), None),
        P(("silo", "shard"), None),
        P("silo", "shard", None, None),
        P("silo", "shard", None),
        P("silo", "shard", None),
        P("silo", "shard", None),
        P("silo", None, None, None),
        P("silo", None, None),
        P(None, "shard", None),
        P(None, "shard"),
    )
    out_specs = (
        P("silo", "shard", None),
        P("silo", "shard", None),
        P("silo", "shard", None),
        P("silo", "shard", None, None),
    )
    return jax.shard_map(body, mesh=mesh, in_specs=in_specs, out_specs=out_specs, check_vma=False)
```

time: 40 us -> 20.3 us (0.51)
  local copies, waits for them, and re-layouts: 14.9 us -> 0 us
  Pallas kernels: 17 us -> 11.6 us
  waiting for transfers between devices: 0.01 us -> 1.02 us
    unnamed x35 -> x0, local copies, waits for them, and re-layouts: 14.9 us -> none
    pallas_call x3, Pallas kernels: 14.6 us -> 9.4 us  [the longest x1 3.99 us: gradient(): pl.pallas_call(functools.partial(gradient_kernel, shards, own_blocks, per...]
    ppermute x2, waiting for transfers between devices: 0.01 us -> 1.02 us  [the longest x1 1.01 us: exchange(): far = lax.ppermute(rows, 'silo', routes[0])]
  transfers between devices with their start and end apart: 3 -> 3, of which waited for: 0 -> 1; matrix products, arithmetic and copies ran while one was open for 0% -> 0% of each run, Pallas kernels for 25% -> 32%
where the time goes in v3:
time: 20.3 us; the launch traced here: 20.1 us
  Pallas kernels  11.6 us (57%)
  starting transfers between devices  6.79 us (33%)
  waiting for transfers between devices  1.02 us (5%)
  between operations  0.67 us (3%)
    pallas_call x1, Pallas kernels, gradient(): pl.pallas_call(functools.partial(gradient_kernel, shards, own_blocks, per...  3.99 us
    ppermute x1, starting transfers between devices, exchange(): far = lax.ppermute(rows, 'silo', routes[0])  3.79 us
    pallas_call x1, Pallas kernels, moving_rows(): pl.pallas_call(functools.partial(rows_kernel, shards, own_blocks, per_row...  3.07 us
    ppermute x1, starting transfers between devices, body(): lax.ppermute(rows, 'shard', [(r, (r + shift) % shards) for r in range(sha...  3 us
    pallas_call x1, Pallas kernels, own_updates(): pl.pallas_call(functools.partial(own_kernel, shards, silos, per_row), nam...  2.34 us
    pallas_call x1, Pallas kernels, final(): pl.pallas_call(functools.partial(final_kernel, per_row), name='neighbours...  2.08 us
    ppermute x1, waiting for transfers between devices, exchange(): far = lax.ppermute(rows, 'silo', routes[0])  1.01 us
  transfers between devices with their start and end apart: 3, of which 1 were waited for; matrix products, arithmetic and copies ran while one was open for 0% of the time, Pallas kernels for 32%

profile of v3, /device:TPU:0, one launch (start us, length us, event | category | flops | bytes accessed | tf_op | source)
XLA Modules:
  0.0 20.1 jit_solution(4163057925480895486)
XLA Ops:
  0.6 3.1 %moving_rows.1 = (f32[64,256]{1,0:T(8,128)S(1)}, bf16[1024,1280]{1,0:T(8,128)(2,1)S(1)}, bf16[1024,640]{1,0:T(8,128)(2,1)S(1)}, s32[2,2,64]{2,1,0:T(2,128)S(1)}, s32[16,1,128]{2,1,0:T(1,128)S(1)}) custom-call(s32[1,2,2,64]{3,2,1,0:T(2,128)} %lists.3, s32[1,2,2]{2,1,0:T(2,128)} %counts.3, s32[16,1,128]{2,1,0:T(1,128)} %g_lists.3, bf16[1024,1280]{1,0:T(8,128)(2,1)} %act.1, ...), custom_call_target="tpu_custom_call" | custom-call | tf_op jit(solution)/shard_map/moving_rows/pallas_call | solution.py:117
  3.7 3.0 %collective-permute-start = (f32[64,256]{1,0:T(8,128)S(1)}, f32[64,256]{1,0:T(8,128)S(1)}, u32[]{:S(2)}, u32[]{:S(2)}) collective-permute-start(f32[64,256]{1,0:T(8,128)S(1)} %get-tuple-element.33), channel_id=1, source_target_pairs={{0,1},{1,0},{2,3},{3,2},{4,5},{5,4},{6,7},{7,6},{8,9},{9,8},{10,11... | collective-permute-start | bytes 196616 | tf_op jit(solution)/shard_map/ppermute | solution.py:482
  6.7 4.0 %gradient.1 = (f32[64,256]{1,0:T(8,128)S(1)}, f32[128,256]{1,0:T(8,128)S(1)}, bf16[128,128]{1,0:T(8,128)(2,1)S(1)}, f32[2,3208,128]{2,1,0:T(8,128)S(1)}, f32[320...) custom-call(s32[1,2,2,64]{3,2,1,0:T(2,128)} %lists.3, s32[1,2,2]{2,1,0:T(2,128)} %counts.3, ...), custom_call_target="tpu_custom_call" | custom-call | tf_op jit(solution)/shard_map/gradient/pallas_call | solution.py:275
  10.7 0.0 collective-permute-done.refs_0_.refs_1_
  10.7 0.1 delta_rows.1.delta
  10.9 3.8 %collective-permute-start.1 = (f32[128,256]{1,0:T(8,128)S(1)}, f32[128,256]{1,0:T(8,128)S(1)}, u32[]{:S(2)}, u32[]{:S(2)}) collective-permute-start(f32[128,256]{1,0:T(8,128)S(1)} %delta_rows.1.delta), channel_id=1, source_target_pairs={{0,30},{2,4},{4,2},{6,8},{8,6},{10,12},{12,10},{14,16},{16,14},{18... | collective-permute-start | bytes 393224 | tf_op jit(solution)/shard_map/ppermute | solution.py:455
  14.7 0.0 collective-permute-start.2
  14.7 2.3 %own_updates.1 = (f32[1,1,3200,256]{3,2,1,0:T(8,128)}, f32[1,320,1280]{2,1,0:T(8,128)}, f32[320,1280]{1,0:T(8,128)S(1)}, f32[320,1280]{1,0:T(8,128)S(1)}, bf16[1600,256]{1,0:T(8,128)(2,1)S(1)}) custom-call(s32[2,2,64]{2,1,0:T(2,128)S(1)} %get-tuple-element.23.lists_v, s32[16,1,128]{2,1,0:T(1,128)S(1)} %get-tuple-element.24.g_v, ...), custom_call_target="tpu_custom_call" | custom-call | tf_op jit(solution)/shard_map/own_updates/pallas_call | solution.py:380
  17.0 1.0 %collective-permute-done.1.first = f32[128,256]{1,0:T(8,128)S(1)} collective-permute-done((f32[128,256]{1,0:T(8,128)S(1)}, f32[128,256]{1,0:T(8,128)S(1)}, u32[]{:S(2)}, u32[]{:S(2)}) %collective-permute-start.1) | collective-permute-done | bytes 131104 | tf_op jit(solution)/shard_map/ppermute | solution.py:455
  18.0 0.0 collective-permute-done.2.second
  18.0 2.1 %neighbours.1 = (f32[1,320,1280]{2,1,0:T(8,128)}, f32[1,320,1280]{2,1,0:T(8,128)}) custom-call(f32[320,1280]{1,0:T(8,128)S(1)} %get-tuple-element.35.mixed_pre, f32[320,1280]{1,0:T(8,128)S(1)} %get-tuple-element.36.params_pre, bf16[1600,256]{1,0:T(8,128)(2,1)S(1)} %get-tuple-element.37.spread, f32[128,256]{1,0:T(8,128)S(1)} %collective-permute-done.1.first, ...), custom_call_target="tpu_custom_call" | custom-call | tf_op jit(solution)/shard_map/neighbours/pallas_call | solution.py:424
Async XLA Ops:
  3.7 7.0 %collective-permute-start = (f32[64,256]{1,0:T(8,128)S(1)}, f32[64,256]{1,0:T(8,128)S(1)}, u32[]{:S(2)}, u32[]{:S(2)}) collective-permute-start(f32[64,256]{1,0:T(8,128)S(1)} %get-tuple-element.33), channel_id=1, source_target_pairs={{0,1},{1,0},{2,3},{3,2},{4,5},{5,4},{6,7},{7,6},{8,9},{9,8},{10,11... | collective-permute-start | bytes 196616 | tf_op jit(solution)/shard_map/ppermute | solution.py:482
  10.9 7.2 %collective-permute-start.1 = (f32[128,256]{1,0:T(8,128)S(1)}, f32[128,256]{1,0:T(8,128)S(1)}, u32[]{:S(2)}, u32[]{:S(2)}) collective-permute-start(f32[128,256]{1,0:T(8,128)S(1)} %delta_rows.1.delta), channel_id=1, source_target_pairs={{0,30},{2,4},{4,2},{6,8},{8,6},{10,12},{12,10},{14,16},{16,14},{18... | collective-permute-start | bytes 393224 | tf_op jit(solution)/shard_map/ppermute | solution.py:455
  14.7 3.4 %collective-permute-start.2 = (f32[128,256]{1,0:T(8,128)S(1)}, f32[128,256]{1,0:T(8,128)S(1)}, u32[]{:S(2)}, u32[]{:S(2)}) collective-permute-start(f32[128,256]{1,0:T(8,128)S(1)} %delta_rows.1.delta), channel_id=1, source_target_pairs={{0,2},{2,0},{4,6},{6,4},{8,10},{10,8},{12,14},{14,12},{16,18},{18,... | collective-permute-start | bytes 393224 | tf_op jit(solution)/shard_map/ppermute | solution.py:456

commit v4 on v3

v4 whole, which is shorter than its diff:
```python
import functools

import jax
import jax.numpy as jnp
from jax import lax
from jax.experimental import pallas as pl
from jax.experimental.pallas import tpu as pltpu
from jax.sharding import PartitionSpec as P

LEARN_RATE = 0.25
CONSENSUS = 0.5
MIX_WEIGHT = 1.0 / 3.0

F32, BF16, I32 = jnp.float32, jnp.bfloat16, jnp.int32
ANY = pl.BlockSpec(memory_space=pl.ANY)
IN_VMEM = pl.BlockSpec(memory_space=pltpu.VMEM)
MIB = 1 << 20


def dot(a, b, dims=((1,), (0,))):
    return lax.dot_general(a, b, (dims, ((), ())), preferred_element_type=F32)


def as_column(row):
    n = row.shape[1]
    eye = lax.broadcasted_iota(I32, (n, n), 0) == lax.broadcasted_iota(I32, (n, n), 1)
    spread = jnp.where(eye, jnp.broadcast_to(row.astype(F32), (n, n)), 0.0)
    return jnp.sum(spread, axis=1, keepdims=True).astype(I32)


def split(rows):
    high = rows.astype(BF16)
    return jnp.concatenate([high, (rows - high.astype(F32)).astype(BF16)], axis=0)


def pick(choice, rows):
    return dot(jnp.concatenate([choice, choice], axis=1), rows)


def onehot(mask):
    return jnp.where(mask, 1.0, 0.0).astype(BF16)


def divide(value, by):
    return (value * ((1 << 16) // by + 1)) >> 16


TILE = 128


def owner_tiles(shards, width_out):
    rows = width_out // shards
    return max(-(-(owner + 1) * rows // TILE) - owner * rows // TILE for owner in range(shards))


def first_tile(me, shards, width_out):
    last = width_out // TILE - owner_tiles(shards, width_out)
    return jnp.minimum(lax.div(me * (width_out // shards), TILE), last)


def rows_kernel(shards, silos, own_blocks, per_row, scale, lists, counts, g_lists, g_counts, act, cot, err, *refs):
    grad_rows, err_rows = refs[:2]
    (act_v, cot_v, own_match, match, kept_hot, own_hot, spread, row_table, g_table,
     list_s, count_s, gc_s, lists_v, g_v, sems) = refs[2:]
    me = lax.axis_index("shard")
    silo = lax.axis_index("silo")
    slots = lists_v.shape[2]
    g_slots = g_v.shape[2]
    width = err_rows.shape[1]
    parts = 4
    depth = act_v.shape[0] // parts
    small = [
        pltpu.make_async_copy(lists.at[0, me], list_s, sems.at[0]),
        pltpu.make_async_copy(lists.at[0], lists_v, sems.at[1]),
        pltpu.make_async_copy(counts.at[0], count_s, sems.at[2]),
        pltpu.make_async_copy(g_lists, g_v, sems.at[3]),
        pltpu.make_async_copy(g_counts, gc_s, sems.at[4]),
    ]
    cot_copy = pltpu.make_async_copy(cot, cot_v, sems.at[5])
    act_copies = [
        pltpu.make_async_copy(act.at[rows], act_v.at[rows], sems.at[6 + part])
        for part, rows in enumerate(pl.ds(part * depth, depth) for part in range(parts))
    ]
    for copy in [*small, cot_copy, *act_copies]:
        copy.start()
    for copy in small:
        copy.wait()

    columns, fills = [], []
    for shift in range(1, shards):
        owner = lax.rem(me + shift, shards)

        def fetch(slot, carry, owner=owner, shift=shift):
            block = owner * own_blocks + list_s[owner, slot]
            into = err_rows.at[pl.ds((shift - 1) * slots + slot, 1)]
            pltpu.make_async_copy(err.at[0, 0, pl.ds(block, 1)], into, sems.at[0]).start()
            return carry

        lax.fori_loop(0, slots, fetch, 0, unroll=slots)
        row = lists_v[me, pl.ds(owner, 1), :] + owner * own_blocks
        columns.append(as_column(row))
        slot_ids = lax.broadcasted_iota(I32, (slots, 1), 0)
        fills.append(slot_ids < count_s[me, owner])
    blocks = jnp.concatenate(columns, axis=0)
    filled = jnp.concatenate(fills, axis=0)
    out_row = divide(blocks, per_row)
    segment = blocks - out_row * per_row
    total = blocks.shape[0]
    chosen = onehot(lax.broadcasted_iota(I32, (total, cot_v.shape[1]), 1) == out_row)

    senders = [lists_v[lax.rem(me - shift + shards, shards), pl.ds(me, 1), :] for shift in range(shards)]
    gossiped = as_column(g_v[silo])
    sent = lax.broadcasted_iota(I32, (g_slots, 1), 0) < gc_s[silo]
    for shift, ids in enumerate(senders):
        same = onehot((gossiped == jnp.concatenate([ids, ids], axis=1)) & sent)
        if shift:
            match[:, 2 * (shift - 1) * slots : 2 * shift * slots] = same
        else:
            own_match[...] = same
    nblocks = shards * own_blocks
    step = TILE * per_row
    own_span = owner_tiles(shards, cot_v.shape[1]) * step
    start = first_tile(me, shards, cot_v.shape[1]) * step
    slot_ids = lax.broadcasted_iota(I32, (1, slots), 1)
    for owner in range(shards):
        place = lists_v[me, owner : owner + 1, :] + (owner * own_blocks - start)
        place = jnp.where(place < 0, place + nblocks, place)
        keep = slot_ids < count_s[me, owner]
        row_table[owner : owner + 1, :] = jnp.where(keep & (place < own_span), place, nblocks)
        row_table[shards + owner : shards + owner + 1, :] = jnp.where(
            keep & (place >= own_span), place - own_span, nblocks - own_span
        )
    place = lists_v[me, pl.ds(me, 1), :] + (me * own_blocks - start)
    row_table[2 * shards : 2 * shards + 1, :] = jnp.where(slot_ids < count_s[me, me], place, nblocks)
    out_rows = own_blocks // per_row
    chunks = per_row * width // 128
    row = divide(g_v[silo], per_row)
    place = (g_v[silo] - row * per_row) * (width // 128 * out_rows) + row
    sent = lax.broadcasted_iota(I32, (1, g_slots), 1) < gc_s[silo]
    g_table[...] = jnp.where(sent, place, chunks * out_rows)
    first, second = neighbours(silo, silos)
    for ids, into in (
        (jnp.concatenate(senders, axis=1), kept_hot),
        (g_v[silo], own_hot),
        (jnp.concatenate([g_v[first], g_v[second]], axis=1), spread),
    ):
        for part in range(per_row):
            here = lax.broadcasted_iota(I32, (out_rows, ids.shape[1]), 0) * per_row + part
            into[part * out_rows : (part + 1) * out_rows, :] = onehot(here == ids)

    cot_copy.wait()
    picked = dot(chosen, cot_v[...], ((1,), (1,))).astype(BF16)
    acc = jnp.zeros((total, act_v.shape[1]), F32)
    for part, copy in enumerate(act_copies):
        copy.wait()
        acc = acc + dot(picked[:, part * depth : (part + 1) * depth], act_v[part * depth : (part + 1) * depth, :])
    grad = jnp.zeros((total, width), F32)
    for part in range(per_row):
        grad = jnp.where(segment == part, acc[:, part * width : (part + 1) * width], grad)
    grad_rows[...] = jnp.where(filled, grad * scale, 0.0)
    pltpu.make_async_copy(err_rows, err_rows, sems.at[0]).wait()
    err_rows[...] = jnp.where(filled, err_rows[...], 0.0)


def moving_rows(shards, silos, own_blocks, per_row, scale, lists, counts, g_lists, g_counts, act, cot, err):
    slots = lists.shape[3]
    g_slots = g_lists.shape[2]
    width = err.shape[3]
    return pl.pallas_call(
        functools.partial(rows_kernel, shards, silos, own_blocks, per_row, scale),
        name="moving_rows",
        in_specs=[ANY] * 7,
        out_specs=[IN_VMEM] * 11,
        out_shape=[pltpu.VMEM(((shards - 1) * slots, width), F32)] * 2
        + [
            pltpu.VMEM(act.shape, BF16),
            pltpu.VMEM(cot.shape, BF16),
            pltpu.VMEM((g_slots, 2 * slots), BF16),
            pltpu.VMEM((g_slots, 2 * (shards - 1) * slots), BF16),
            pltpu.VMEM((own_blocks, shards * slots), BF16),
            pltpu.VMEM((own_blocks, g_slots), BF16),
            pltpu.VMEM((own_blocks, 2 * g_slots), BF16),
            pltpu.VMEM((2 * shards + 1, slots), I32),
            pltpu.VMEM((1, g_slots), I32),
        ],
        scratch_shapes=[
            pltpu.SMEM((shards, slots), I32),
            pltpu.SMEM((shards, shards), I32),
            pltpu.SMEM(g_counts.shape, I32),
            pltpu.VMEM(lists.shape[1:], I32),
            pltpu.VMEM(g_lists.shape, I32),
            pltpu.SemaphoreType.DMA((10,)),
        ],
        compiler_params=pltpu.CompilerParams(vmem_limit_bytes=16 * MIB),
    )(lists, counts, g_lists, g_counts, act, cot, err)


def sum_kernel(grad_rows, err_rows, *outs):
    slots = outs[0].shape[0]
    for place, out in enumerate(outs):
        rows = slice(place * slots, (place + 1) * slots)
        out[...] = err_rows[rows, :] + grad_rows[rows, :]


def outgoing_rows(shards, grad_rows, err_rows):
    shape = (grad_rows.shape[0] // (shards - 1), grad_rows.shape[1])
    return pl.pallas_call(
        sum_kernel,
        name="outgoing_rows",
        in_specs=[IN_VMEM] * 2,
        out_specs=[IN_VMEM] * (shards - 1),
        out_shape=[pltpu.VMEM(shape, F32)] * (shards - 1),
        compiler_params=pltpu.CompilerParams(vmem_limit_bytes=8 * MIB),
        cost_estimate=pl.CostEstimate(flops=10**10, bytes_accessed=3 * 10**7, transcendentals=0),
    )(grad_rows, err_rows)


def load_memory(err, err_v, tiles, step, into, sems):
    copies = [
        pltpu.make_async_copy(
            err.at[0, 0, pl.ds(pl.multiple_of(tile * step, 8), step), pl.ds(half * 128, 128)],
            err_v.at[half, pl.ds(place * step, step)],
            sems[half],
        )
        for place, tile in enumerate(tiles, into)
        for half in range(err_v.shape[0])
    ]
    for copy in copies:
        copy.start()
    return copies


def tile_gradient(cot_v, act_v, scale, tile):
    columns = pl.ds(pl.multiple_of(tile * TILE, TILE), TILE)
    return dot(cot_v[:, columns], act_v[...], ((0,), (0,))) * scale


def pieces(grad, place, per_row, halves):
    for seg in range(per_row):
        for half in range(halves):
            lane = (seg * halves + half) * 128
            where = pl.ds(place * TILE * per_row + seg, TILE, stride=per_row)
            yield (half, where, slice(None)), grad[:, lane : lane + 128]


def clear_rows(err_v, table_s, first, shards):
    for owner in range(first, first + shards):

        def clear(slot, carry, owner=owner):
            block = table_s[owner, slot]
            for half in range(err_v.shape[0]):
                err_v[half, pl.ds(block, 1), :] = jnp.zeros((1, 128), F32)
            return carry

        lax.fori_loop(0, table_s.shape[1], clear, 0, unroll=table_s.shape[1])


def gradient_kernel(
    shards, per_row, scale,
    err, p_v, e_v, own_match, act_v, cot_v, row_table, g_table,
    mine, base, err_v, table_s, g_s, rows_v, grad_v, drift_v, sems,
):
    me = lax.axis_index("shard")
    slots = mine.shape[0]
    g_slots = base.shape[0]
    halves = err_v.shape[0]
    out_rows = p_v.shape[1]
    chunks = p_v.shape[2] // 128
    step = TILE * per_row
    tiles = cot_v.shape[1] // TILE
    count = owner_tiles(shards, cot_v.shape[1])
    start = first_tile(me, shards, cot_v.shape[1])
    small = [
        pltpu.make_async_copy(row_table, table_s, sems.at[0]),
        pltpu.make_async_copy(g_table, g_s, sems.at[1]),
    ]
    for copy in small:
        copy.start()
    own_memory, other_memory = (
        load_memory(
            err, err_v, [lax.rem(start + place, tiles) for place in places], step, places[0],
            [sems.at[sem + half] for half in range(halves)],
        )
        for sem, places in ((2, range(count)), (2 + halves, range(count, tiles)))
    )

    def store(place, carry):
        for where, piece in pieces(tile_gradient(cot_v, act_v, scale, start + place), place, per_row, halves):
            grad_v[where] = piece
        return carry

    lax.fori_loop(0, count, store, 0)
    for chunk in range(chunks):
        lanes = slice(chunk * 128, (chunk + 1) * 128)
        drift_v[chunk * out_rows : (chunk + 1) * out_rows, :] = p_v[0, :, lanes] - e_v[0, :, lanes]
    for half in range(halves):
        nothing = (chunks + half) * out_rows
        drift_v[nothing : nothing + 8, :] = jnp.zeros((8, 128), F32)
        err_v[half, tiles * step :, :] = jnp.zeros((8, 128), F32)
    for copy in small:
        copy.wait()

    def gather(slot, carry):
        for half in range(halves):
            rows_v[half, pl.ds(slot, 1), :] = drift_v[pl.ds(g_s[0, slot] + half * out_rows, 1), :]
        return carry

    lax.fori_loop(0, g_slots, gather, 0, unroll=g_slots)
    base[...] = jnp.concatenate([rows_v[half, :g_slots] for half in range(halves)], axis=1)
    for copy in own_memory:
        copy.wait()
    for half in range(halves):
        err_v[half, : count * step, :] = err_v[half, : count * step, :] + grad_v[half]

    def take(slot, carry):
        for half in range(halves):
            rows_v[half, pl.ds(slot, 1), :] = err_v[half, pl.ds(table_s[2 * shards, slot], 1), :]
        return carry

    lax.fori_loop(0, slots, take, 0, unroll=slots)
    mine[...] = jnp.concatenate([rows_v[half, :slots] for half in range(halves)], axis=1)
    clear_rows(err_v, table_s, 0, shards)
    base[...] = base[...] - LEARN_RATE * dot(own_match[...], split(mine[...]))
    for copy in other_memory:
        copy.wait()


def gradient(shards, per_row, scale, err, params, estimate, own_match, act_v, cot_v, row_table, g_table):
    slots = row_table.shape[1]
    g_slots = g_table.shape[1]
    nblocks, width = err.shape[2:]
    halves = width // 128
    count = owner_tiles(shards, cot_v.shape[1])
    step = TILE * per_row
    chunks = params.shape[2] // 128
    return pl.pallas_call(
        functools.partial(gradient_kernel, shards, per_row, scale),
        name="gradient",
        in_specs=[ANY] + [IN_VMEM] * 7,
        out_specs=[IN_VMEM] * 3,
        out_shape=[
            pltpu.VMEM((slots, width), F32),
            pltpu.VMEM((g_slots, width), F32),
            pltpu.VMEM((halves, nblocks + 8, 128), F32),
        ],
        scratch_shapes=[
            pltpu.SMEM(row_table.shape, I32),
            pltpu.SMEM(g_table.shape, I32),
            pltpu.VMEM((halves, max(slots, g_slots), 128), F32),
            pltpu.VMEM((halves, count * step, 128), F32),
            pltpu.VMEM(((chunks + halves - 1) * params.shape[1] + 8, 128), F32),
            pltpu.SemaphoreType.DMA((2 + 2 * halves,)),
        ],
        compiler_params=pltpu.CompilerParams(vmem_limit_bytes=16 * MIB),
    )(err, params, estimate, own_match, act_v, cot_v, row_table, g_table)


def delta_kernel(base, match, *refs):
    *arrived, out, again = refs
    rows = jnp.concatenate([split(each[...]) for each in arrived], axis=0)
    total = base[...] - LEARN_RATE * dot(match[...], rows)
    out[: total.shape[0]] = total
    out[total.shape[0] :] = jnp.zeros((8, total.shape[1]), F32)
    again[...] = total


def delta_rows(base, match, arrived):
    return pl.pallas_call(
        delta_kernel,
        name="delta_rows",
        in_specs=[IN_VMEM] * (2 + len(arrived)),
        out_specs=[IN_VMEM] * 2,
        out_shape=[pltpu.VMEM((base.shape[0] + 8, base.shape[1]), F32), pltpu.VMEM(base.shape, F32)],
        compiler_params=pltpu.CompilerParams(vmem_limit_bytes=8 * MIB),
    )(base, match, *arrived)


def own_kernel(
    shards, per_row, scale,
    p_v, e_v, m_v, err_v, act_v, cot_v, row_table, kept_hot, own_hot, delta, *refs
):
    kept = refs[:shards]
    err_out, est_out, mixed_pre, params_pre, table_s, rest_v, est_v, sems = refs[shards:]
    me = lax.axis_index("shard")
    width = delta.shape[1]
    halves = err_v.shape[0]
    out_rows = p_v.shape[1]
    step = TILE * per_row
    tiles = cot_v.shape[1] // TILE
    count = owner_tiles(shards, cot_v.shape[1])
    start = first_tile(me, shards, cot_v.shape[1])
    small = pltpu.make_async_copy(row_table, table_s, sems.at[0])
    small.start()
    copies = []

    def store_memory(source, first, places):
        for place in places:
            tile = lax.rem(start + place, tiles)
            for half in range(halves):
                copy = pltpu.make_async_copy(
                    source.at[half, pl.ds((place - first) * step, step)],
                    err_out.at[0, 0, pl.ds(pl.multiple_of(tile * step, 8), step), pl.ds(half * 128, 128)],
                    sems.at[1 + half],
                )
                copy.start()
                copies.append(copy)

    store_memory(err_v, 0, range(count))

    def store(place, carry):
        grad = tile_gradient(cot_v, act_v, scale, lax.rem(start + count + place, tiles))
        for where, piece in pieces(grad, place, per_row, halves):
            rest_v[where] = piece
        return carry

    lax.fori_loop(0, tiles - count, store, 0)
    rest = (tiles - count) * step
    for half in range(halves):
        rest_v[half, :rest, :] = rest_v[half, :rest, :] + err_v[half, count * step : tiles * step, :]
    small.wait()
    clear_rows(rest_v, table_s, shards, shards)
    store_memory(rest_v, count, range(count, tiles))

    kept_parts = split(jnp.concatenate([rows[...] for rows in kept], axis=0))
    delta_parts = split(delta[...])
    for part in range(per_row):
        lanes = slice(part * width, (part + 1) * width)
        blocks = slice(part * out_rows, (part + 1) * out_rows)
        grad = pick(kept_hot[blocks, :], kept_parts)
        change = pick(own_hot[blocks, :], delta_parts)
        half_step = p_v[0, :, lanes] - LEARN_RATE * grad
        est = e_v[0, :, lanes] + change
        mix = m_v[0, :, lanes] + MIX_WEIGHT * change
        est_v[:, lanes] = est
        copy = pltpu.make_async_copy(est_v.at[:, lanes], est_out.at[0, :, lanes], sems.at[1 + halves + part])
        copy.start()
        copies.append(copy)
        mixed_pre[:, lanes] = mix
        params_pre[:, lanes] = half_step + CONSENSUS * (mix - est)
    for copy in copies:
        copy.wait()


def own_updates(
    shards, per_row, scale, err_shape, params, estimate, mixed, err_v, act_v, cot_v, row_table, kept_hot, own_hot, delta, kept
):
    owned = mixed.shape[1:]
    halves = err_v.shape[0]
    others = cot_v.shape[1] // TILE - owner_tiles(shards, cot_v.shape[1])
    return pl.pallas_call(
        functools.partial(own_kernel, shards, per_row, scale),
        name="own_updates",
        in_specs=[IN_VMEM] * (10 + shards),
        out_specs=[ANY, ANY, IN_VMEM, IN_VMEM],
        out_shape=[
            pltpu.HBM(err_shape, F32),
            pltpu.HBM(mixed.shape, F32),
            pltpu.VMEM(owned, F32),
            pltpu.VMEM(owned, F32),
        ],
        scratch_shapes=[
            pltpu.SMEM(row_table.shape, I32),
            pltpu.VMEM((halves, others * TILE * per_row + 8, 128), F32),
            pltpu.VMEM(owned, F32),
            pltpu.SemaphoreType.DMA((1 + halves + per_row,)),
        ],
        compiler_params=pltpu.CompilerParams(vmem_limit_bytes=16 * MIB),
    )(params, estimate, mixed, err_v, act_v, cot_v, row_table, kept_hot, own_hot, delta, *kept)


def final_kernel(per_row, mixed_pre, params_pre, spread, first, second, mixed_out, params_out, m_v, p_v, sems):
    out_rows = m_v.shape[0]
    width = m_v.shape[1] // per_row
    slots = second.shape[0]
    rows = split(jnp.concatenate([first[:slots, :], second[...]], axis=0))
    depth = spread.shape[1]
    copies = []
    for part in range(per_row):
        lanes = slice(part * width, (part + 1) * width)
        choice = spread[part * out_rows : (part + 1) * out_rows, :]
        change = dot(choice, rows[:depth]) + dot(choice, rows[depth:])
        m_v[:, lanes] = mixed_pre[:, lanes] + MIX_WEIGHT * change
        p_v[:, lanes] = params_pre[:, lanes] + (CONSENSUS * MIX_WEIGHT) * change
        pair = [
            pltpu.make_async_copy(m_v.at[:, lanes], mixed_out.at[0, :, lanes], sems.at[2 * part]),
            pltpu.make_async_copy(p_v.at[:, lanes], params_out.at[0, :, lanes], sems.at[2 * part + 1]),
        ]
        for copy in pair:
            copy.start()
        copies += pair
    for copy in copies:
        copy.wait()


def final(per_row, shape, mixed_pre, params_pre, spread, first, second):
    return pl.pallas_call(
        functools.partial(final_kernel, per_row),
        name="neighbours",
        in_specs=[IN_VMEM] * 5,
        out_specs=[ANY] * 2,
        out_shape=[pltpu.HBM(shape, F32)] * 2,
        scratch_shapes=[
            pltpu.VMEM(mixed_pre.shape, F32),
            pltpu.VMEM(mixed_pre.shape, F32),
            pltpu.SemaphoreType.DMA((2 * per_row,)),
        ],
        compiler_params=pltpu.CompilerParams(vmem_limit_bytes=20 * MIB),
    )(mixed_pre, params_pre, spread, first, second)


def neighbours(silo, silos):
    lower, upper = lax.rem(silo + silos - 1, silos), lax.rem(silo + 1, silos)
    if silos % 2:
        return lower, upper
    even = lax.rem(silo, 2) == 0
    return jnp.where(even, lower, upper), jnp.where(even, upper, lower)


def exchange(rows, again, silos):
    if silos % 2:
        routes = [[(a, (a + 1) % silos) for a in range(silos)], [(a, (a - 1) % silos) for a in range(silos)]]
    else:
        routes = [
            [(a, (a + 1 if a % 2 else a - 1) % silos) for a in range(silos)],
            [(a, a ^ 1) for a in range(silos)],
        ]
    far = lax.ppermute(rows, "silo", routes[0])
    near = lax.ppermute(again, "silo", routes[1])
    return far, near


def body(
    activ, cotangent, error_memory, params, estimate, mixed,
    kept_blocks, kept_counts, gossip_blocks, gossip_counts,
):
    shards = lax.axis_size("shard")
    silos = lax.axis_size("silo")
    nblocks, block_len = error_memory.shape[2:]
    own_blocks = nblocks // shards
    per_row = activ.shape[1] // block_len
    scale = activ.shape[1] ** (-0.5)
    activ, cotangent, error_memory, kept_blocks, kept_counts, gossip_blocks, gossip_counts = (
        pltpu.with_memory_space_constraint(array, pltpu.HBM)
        for array in (
            activ, cotangent, error_memory,
            kept_blocks, kept_counts, gossip_blocks, gossip_counts.reshape(silos),
        )
    )
    grad_rows, err_rows, act_v, cot_v, own_match, match, kept_hot, own_hot, spread, row_table, g_table = moving_rows(
        shards, silos, own_blocks, per_row, scale,
        kept_blocks, kept_counts, gossip_blocks, gossip_counts, activ, cotangent, error_memory,
    )
    outgoing = outgoing_rows(shards, grad_rows, err_rows)
    arrived = [
        lax.ppermute(rows, "shard", [(r, (r + shift) % shards) for r in range(shards)])
        for shift, rows in enumerate(outgoing, 1)
    ]
    params, estimate, mixed, row_table = lax.optimization_barrier((params, estimate, mixed, row_table))
    params, estimate, mixed = (
        pltpu.with_memory_space_constraint(array, pltpu.VMEM) for array in (params, estimate, mixed)
    )
    mine, base, err_v = gradient(
        shards, per_row, scale, error_memory, params, estimate, own_match, act_v, cot_v, row_table, g_table
    )
    delta, again = delta_rows(base, match, arrived)
    first, second = exchange(delta, again, silos)
    error_out, estimate_out, mixed_pre, params_pre = own_updates(
        shards, per_row, scale, error_memory.shape, params, estimate, mixed,
        err_v, act_v, cot_v, row_table, kept_hot, own_hot, again, [mine, *arrived],
    )
    mixed_out, params_out = final(per_row, mixed.shape, mixed_pre, params_pre, spread, first, second)
    return params_out, estimate_out, mixed_out, error_out


def solution(mesh):
    in_specs = (
        P(("silo", "shard"), None),
        P(("silo", "shard"), None),
        P("silo", "shard", None, None),
        P("silo", "shard", None),
        P("silo", "shard", None),
        P("silo", "shard", None),
        P("silo", None, None, None),
        P("silo", None, None),
        P(None, "shard", None),
        P(None, "shard"),
    )
    out_specs = (
        P("silo", "shard", None),
        P("silo", "shard", None),
        P("silo", "shard", None),
        P("silo", "shard", None, None),
    )
    return jax.shard_map(body, mesh=mesh, in_specs=in_specs, out_specs=out_specs, check_vma=False)
```

time: 20.3 us -> 19.1 us (0.941)
  waiting for transfers between devices: 1.02 us -> 0.01 us
  Pallas kernels: 11.6 us -> 10.8 us
  starting transfers between devices: 6.79 us -> 7.38 us
    ppermute x1, waiting for transfers between devices: 1.01 us -> 0.01 us  [exchange(): far = lax.ppermute(rows, 'silo', routes[0])]
    pallas_call x3 -> x4, Pallas kernels: 9.4 us -> 8.6 us  [the longest x1 3.21 us: own_updates(): pl.pallas_call(functools.partial(own_kernel, shards, per_row, scale), nam...]
    ppermute x1, starting transfers between devices: 3.79 us -> 4.37 us  [exchange(): far = lax.ppermute(rows, 'silo', routes[0])]
  transfers between devices with their start and end apart: 3 -> 3, of which waited for: 1 -> 0; matrix products, arithmetic and copies ran while one was open for 0% -> 0% of each run, Pallas kernels for 32% -> 31%
where the time goes in v4:
time: 19.1 us; the launch traced here: 18.9 us
  Pallas kernels  10.8 us (57%)
  starting transfers between devices  7.38 us (39%)
  between operations  0.71 us (4%)
    ppermute x1, starting transfers between devices, exchange(): far = lax.ppermute(rows, 'silo', routes[0])  4.37 us
    pallas_call x1, Pallas kernels, own_updates(): pl.pallas_call(functools.partial(own_kernel, shards, per_row, scale), nam...  3.21 us
    ppermute x1, starting transfers between devices, body(): lax.ppermute(rows, 'shard', [(r, (r + shift) % shards) for r in range(sha...  3 us
    pallas_call x1, Pallas kernels, moving_rows(): pl.pallas_call(functools.partial(rows_kernel, shards, silos, own_blocks,...  2.78 us
    pallas_call x1, Pallas kernels, gradient(): pl.pallas_call(functools.partial(gradient_kernel, shards, per_row, scale)...  2.6 us
    pallas_call x1, Pallas kernels, final(): pl.pallas_call(functools.partial(final_kernel, per_row), name='neighbours...  2.07 us
  transfers between devices with their start and end apart: 3, of which 0 were waited for; matrix products, arithmetic and copies ran while one was open for 0% of the time, Pallas kernels for 31%

profile of v4, /device:TPU:0, one launch (start us, length us, event | category | flops | bytes accessed | tf_op | source)
XLA Modules:
  0.0 18.9 jit_solution(8900011546204617560)
XLA Ops:
  0.6 2.8 %moving_rows.1 = (f32[64,256]{1,0:T(8,128)S(1)}, f32[64,256]{1,0:T(8,128)S(1)}, bf16[1024,1280]{1,0:T(8,128)(2,1)S(1)}, bf16[1024,640]{1,0:T(8,128)(2,1)S(1)}, b...) custom-call(s32[1,2,2,64]{3,2,1,0:T(2,128)} %lists.1, ...), custom_call_target="tpu_custom_call" | custom-call | tf_op jit(solution)/shard_map/moving_rows/pallas_call | solution.py:169
  3.4 0.0 copy-start
  3.4 0.0 copy-start.1
  3.5 3.0 %collective-permute-start = (f32[64,256]{1,0:T(8,128)S(1)}, f32[64,256]{1,0:T(8,128)S(1)}, u32[]{:S(2)}, u32[]{:S(2)}) collective-permute-start(f32[64,256]{1,0:T(8,128)S(1)} %outgoing_rows.1), channel_id=1, source_target_pairs={{0,1},{1,0},{2,3},{3,2},{4,5},{5,4},{6,7},{7,6},{8,9},{9,8},{10,11... | collective-permute-start | bytes 196616 | tf_op jit(solution)/shard_map/ppermute | solution.py:555
  6.5 0.0 copy-done
  6.5 0.0 copy-done.1
  6.5 0.0 copy-start.2
  6.5 2.6 %gradient.1 = (f32[64,256]{1,0:T(8,128)S(1)}, f32[128,256]{1,0:T(8,128)S(1)}, f32[2,3208,128]{2,1,0:T(8,128)S(1)}) custom-call(f32[1,1,3200,256]{3,2,1,0:T(8,128)} %err.3, f32[1,320,1280]{2,1,0:T(8,128)S(1)} %copy-done, f32[1,320,1280]{2,1,0:T(8,128)S(1)} %copy-done.1, bf16[128,128]{1,0:T(8,128)(2,1)S(1)} %get-tuple-element.34.own_match, ...), custom_call_target="tpu_custom_call" | custom-call | tf_op jit(solution)/shard_map/gradient/pallas_call | solution.py:336
  9.1 0.0 collective-permute-done.refs_0_.refs_1_
  9.1 0.2 delta_rows.1
  9.2 4.4 %collective-permute-start.1 = (f32[136,256]{1,0:T(8,128)S(1)}, f32[136,256]{1,0:T(8,128)S(1)}, u32[]{:S(2)}, u32[]{:S(2)}) collective-permute-start(f32[136,256]{1,0:T(8,128)S(1)} %get-tuple-element.51), channel_id=1, source_target_pairs={{0,30},{2,4},{4,2},{6,8},{8,6},{10,12},{12,10},{14,16},{16,14},{18... | collective-permute-start | bytes 417800 | tf_op jit(solution)/shard_map/ppermute | solution.py:527
  13.6 0.0 collective-permute-start.2
  13.6 0.0 copy-done.2
  13.6 3.2 %own_updates.1 = (f32[1,1,3200,256]{3,2,1,0:T(8,128)}, f32[1,320,1280]{2,1,0:T(8,128)}, f32[320,1280]{1,0:T(8,128)S(1)}, f32[320,1280]{1,0:T(8,128)S(1)}) custom-call(f32[1,320,1280]{2,1,0:T(8,128)S(1)} %copy-done, f32[1,320,1280]{2,1,0:T(8,128)S(1)} %copy-done.1, f32[1,320,1280]{2,1,0:T(8,128)S(1)} %copy-done.2, ...), custom_call_target="tpu_custom_call" | custom-call | tf_op jit(solution)/shard_map/own_updates/pallas_call | solution.py:450
  16.8 0.0 collective-permute-done.2.second
  16.9 0.0 collective-permute-done.1.first
  16.9 2.1 %neighbours.1 = (f32[1,320,1280]{2,1,0:T(8,128)}, f32[1,320,1280]{2,1,0:T(8,128)}) custom-call(f32[320,1280]{1,0:T(8,128)S(1)} %get-tuple-element.48.mixed_pre, f32[320,1280]{1,0:T(8,128)S(1)} %get-tuple-element.49.params_pre, bf16[1600,256]{1,0:T(8,128)(2,1)S(1)} %get-tuple-element.50.spread, f32[136,256]{1,0:T(8,128)S(1)} %collective-permute-done.1.first, ...), custom_call_target="tpu_custom_call" | custom-call | tf_op jit(solution)/shard_map/neighbours/pallas_call | solution.py:496
  (1 shorter events, 0.0 us)
Async XLA Ops:
  3.4 3.0 %copy-start = (f32[1,320,1280]{2,1,0:T(8,128)S(1)}, f32[1,320,1280]{2,1,0:T(8,128)}, u32[]{:S(2)}) copy-start(f32[1,320,1280]{2,1,0:T(8,128)} %p_v.1) | copy-start | bytes 4915204
  3.4 3.0 %copy-start.1 = (f32[1,320,1280]{2,1,0:T(8,128)S(1)}, f32[1,320,1280]{2,1,0:T(8,128)}, u32[]{:S(2)}) copy-start(f32[1,320,1280]{2,1,0:T(8,128)} %e_v.1) | copy-start | bytes 4915204
  3.5 5.6 %collective-permute-start = (f32[64,256]{1,0:T(8,128)S(1)}, f32[64,256]{1,0:T(8,128)S(1)}, u32[]{:S(2)}, u32[]{:S(2)}) collective-permute-start(f32[64,256]{1,0:T(8,128)S(1)} %outgoing_rows.1), channel_id=1, source_target_pairs={{0,1},{1,0},{2,3},{3,2},{4,5},{5,4},{6,7},{7,6},{8,9},{9,8},{10,11... | collective-permute-start | bytes 196616 | tf_op jit(solution)/shard_map/ppermute | solution.py:555
  6.5 7.2 %copy-start.2 = (f32[1,320,1280]{2,1,0:T(8,128)S(1)}, f32[1,320,1280]{2,1,0:T(8,128)}, u32[]{:S(2)}) copy-start(f32[1,320,1280]{2,1,0:T(8,128)} %m_v) | copy-start | bytes 4915204
  9.2 7.6 %collective-permute-start.1 = (f32[136,256]{1,0:T(8,128)S(1)}, f32[136,256]{1,0:T(8,128)S(1)}, u32[]{:S(2)}, u32[]{:S(2)}) collective-permute-start(f32[136,256]{1,0:T(8,128)S(1)} %get-tuple-element.51), channel_id=1, source_target_pairs={{0,30},{2,4},{4,2},{6,8},{8,6},{10,12},{12,10},{14,16},{16,14},{18... | collective-permute-start | bytes 417800 | tf_op jit(solution)/shard_map/ppermute | solution.py:527
  13.6 3.2 %collective-permute-start.2 = (f32[128,256]{1,0:T(8,128)S(1)}, f32[128,256]{1,0:T(8,128)S(1)}, u32[]{:S(2)}, u32[]{:S(2)}) collective-permute-start(f32[128,256]{1,0:T(8,128)S(1)} %get-tuple-element.46.delta), channel_id=1, source_target_pairs={{0,2},{2,0},{4,6},{6,4},{8,10},{10,8},{12,14},{14,12},{16,18},{18,... | collective-permute-start | bytes 393224 | tf_op jit(solution)/shard_map/ppermute | solution.py:528

commit v5 on v4

--- a/solution.py
+++ b/solution.py
@@ -195,24 +195,40 @@
     )(lists, counts, g_lists, g_counts, act, cot, err)
 
 
-def sum_kernel(grad_rows, err_rows, *outs):
+def early_tiles(me, silo):
+    return jnp.where((me == 0) & (silo < 2), 2, 0)
+
+
+def sum_kernel(shards, per_row, scale, grad_rows, err_rows, act_v, cot_v, *outs):
+    *outs, grad_v = outs
+    me = lax.axis_index("shard")
+    start = first_tile(me, shards, cot_v.shape[1])
+
+    def store(place, carry):
+        grad = tile_gradient(cot_v, act_v, scale, start + place)
+        for where, piece in pieces(grad, place, per_row, grad_v.shape[0]):
+            grad_v[where] = piece
+        return carry
+
+    lax.fori_loop(0, early_tiles(me, lax.axis_index("silo")), store, 0)
     slots = outs[0].shape[0]
     for place, out in enumerate(outs):
         rows = slice(place * slots, (place + 1) * slots)
         out[...] = err_rows[rows, :] + grad_rows[rows, :]
 
 
-def outgoing_rows(shards, grad_rows, err_rows):
+def outgoing_rows(shards, per_row, scale, grad_rows, err_rows, act_v, cot_v):
     shape = (grad_rows.shape[0] // (shards - 1), grad_rows.shape[1])
     return pl.pallas_call(
-        sum_kernel,
+        functools.partial(sum_kernel, shards, per_row, scale),
         name="outgoing_rows",
-        in_specs=[IN_VMEM] * 2,
-        out_specs=[IN_VMEM] * (shards - 1),
-        out_shape=[pltpu.VMEM(shape, F32)] * (shards - 1),
+        in_specs=[IN_VMEM] * 4,
+        out_specs=[IN_VMEM] * shards,
+        out_shape=[pltpu.VMEM(shape, F32)] * (shards - 1)
+        + [pltpu.VMEM((shape[1] // 128, owner_tiles(shards, cot_v.shape[1]) * TILE * per_row, 128), F32)],
         compiler_params=pltpu.CompilerParams(vmem_limit_bytes=8 * MIB),
         cost_estimate=pl.CostEstimate(flops=10**10, bytes_accessed=3 * 10**7, transcendentals=0),
-    )(grad_rows, err_rows)
+    )(grad_rows, err_rows, act_v, cot_v)
 
 
 def load_memory(err, err_v, tiles, step, into, sems):
@@ -257,15 +273,15 @@
 
 def gradient_kernel(
     shards, per_row, scale,
-    err, p_v, e_v, own_match, act_v, cot_v, row_table, g_table,
-    mine, base, err_v, table_s, g_s, rows_v, grad_v, drift_v, sems,
+    err, params, e_v, own_match, act_v, cot_v, row_table, g_table, _,
+    mine, base, err_v, p_v, grad_v, table_s, g_s, rows_v, drift_v, sems,
 ):
     me = lax.axis_index("shard")
     slots = mine.shape[0]
     g_slots = base.shape[0]
     halves = err_v.shape[0]
-    out_rows = p_v.shape[1]
-    chunks = p_v.shape[2] // 128
+    out_rows = e_v.shape[1]
+    chunks = e_v.shape[2] // 128
     step = TILE * per_row
     tiles = cot_v.shape[1] // TILE
     count = owner_tiles(shards, cot_v.shape[1])
@@ -276,29 +292,43 @@
     ]
     for copy in small:
         copy.start()
-    own_memory, other_memory = (
-        load_memory(
-            err, err_v, [lax.rem(start + place, tiles) for place in places], step, places[0],
-            [sems.at[sem + half] for half in range(halves)],
-        )
-        for sem, places in ((2, range(count)), (2 + halves, range(count, tiles)))
-    )
+
+    def load(places, sem):
+        order = [lax.rem(start + place, tiles) for place in places]
+        return load_memory(err, err_v, order, step, places[0], [sems.at[sem + half] for half in range(halves)])
+
+    own_memory = load(range(count), 3)
+    p_copy = pltpu.make_async_copy(params, p_v, sems.at[2])
+    p_copy.start()
+    other_memory = load(range(count, tiles), 3 + halves)
 
     def store(place, carry):
         for where, piece in pieces(tile_gradient(cot_v, act_v, scale, start + place), place, per_row, halves):
             grad_v[where] = piece
         return carry
 
-    lax.fori_loop(0, count, store, 0)
+    lax.fori_loop(early_tiles(me, lax.axis_index("silo")), count, store, 0)
+    for copy in small + own_memory:
+        copy.wait()
+    for half in range(halves):
+        err_v[half, : count * step, :] = err_v[half, : count * step, :] + grad_v[half]
+        err_v[half, tiles * step :, :] = jnp.zeros((8, 128), F32)
+
+    def take(slot, carry):
+        for half in range(halves):
+            rows_v[half, pl.ds(slot, 1), :] = err_v[half, pl.ds(table_s[2 * shards, slot], 1), :]
+        return carry
+
+    lax.fori_loop(0, slots, take, 0, unroll=slots)
+    mine[...] = jnp.concatenate([rows_v[half, :slots] for half in range(halves)], axis=1)
+    clear_rows(err_v, table_s, 0, shards)
+    p_copy.wait()
     for chunk in range(chunks):
         lanes = slice(chunk * 128, (chunk + 1) * 128)
         drift_v[chunk * out_rows : (chunk + 1) * out_rows, :] = p_v[0, :, lanes] - e_v[0, :, lanes]
     for half in range(halves):
         nothing = (chunks + half) * out_rows
         drift_v[nothing : nothing + 8, :] = jnp.zeros((8, 128), F32)
-        err_v[half, tiles * step :, :] = jnp.zeros((8, 128), F32)
-    for copy in small:
-        copy.wait()
 
     def gather(slot, carry):
         for half in range(halves):
@@ -306,53 +336,40 @@
         return carry
 
     lax.fori_loop(0, g_slots, gather, 0, unroll=g_slots)
-    base[...] = jnp.concatenate([rows_v[half, :g_slots] for half in range(halves)], axis=1)
-    for copy in own_memory:
-        copy.wait()
-    for half in range(halves):
-        err_v[half, : count * step, :] = err_v[half, : count * step, :] + grad_v[half]
-
-    def take(slot, carry):
-        for half in range(halves):
-            rows_v[half, pl.ds(slot, 1), :] = err_v[half, pl.ds(table_s[2 * shards, slot], 1), :]
-        return carry
-
-    lax.fori_loop(0, slots, take, 0, unroll=slots)
-    mine[...] = jnp.concatenate([rows_v[half, :slots] for half in range(halves)], axis=1)
-    clear_rows(err_v, table_s, 0, shards)
-    base[...] = base[...] - LEARN_RATE * dot(own_match[...], split(mine[...]))
+    rows = jnp.concatenate([rows_v[half, :g_slots] for half in range(halves)], axis=1)
+    base[...] = rows - LEARN_RATE * dot(own_match[...], split(mine[...]))
     for copy in other_memory:
         copy.wait()
 
 
-def gradient(shards, per_row, scale, err, params, estimate, own_match, act_v, cot_v, row_table, g_table):
+def gradient(shards, per_row, scale, err, params, estimate, own_match, act_v, cot_v, row_table, g_table, grad_v):
     slots = row_table.shape[1]
-    g_slots = g_table.shape[1]
+    g_slots = own_match.shape[0]
     nblocks, width = err.shape[2:]
     halves = width // 128
-    count = owner_tiles(shards, cot_v.shape[1])
-    step = TILE * per_row
     chunks = params.shape[2] // 128
     return pl.pallas_call(
         functools.partial(gradient_kernel, shards, per_row, scale),
         name="gradient",
-        in_specs=[ANY] + [IN_VMEM] * 7,
-        out_specs=[IN_VMEM] * 3,
+        in_specs=[ANY] * 2 + [IN_VMEM] * 7,
+        out_specs=[IN_VMEM] * 5,
         out_shape=[
             pltpu.VMEM((slots, width), F32),
             pltpu.VMEM((g_slots, width), F32),
             pltpu.VMEM((halves, nblocks + 8, 128), F32),
+            pltpu.VMEM(params.shape, F32),
+            pltpu.VMEM(grad_v.shape, F32),
         ],
+        input_output_aliases={8: 4},
         scratch_shapes=[
             pltpu.SMEM(row_table.shape, I32),
             pltpu.SMEM(g_table.shape, I32),
             pltpu.VMEM((halves, max(slots, g_slots), 128), F32),
-            pltpu.VMEM((halves, count * step, 128), F32),
             pltpu.VMEM(((chunks + halves - 1) * params.shape[1] + 8, 128), F32),
-            pltpu.SemaphoreType.DMA((2 + 2 * halves,)),
+            pltpu.SemaphoreType.DMA((3 + 2 * halves,)),
         ],
         compiler_params=pltpu.CompilerParams(vmem_limit_bytes=16 * MIB),
-    )(err, params, estimate, own_match, act_v, cot_v, row_table, g_table)
+    )(err, params, estimate, own_match, act_v, cot_v, row_table, g_table, grad_v)
 
 
 def delta_kernel(base, match, *refs):
@@ -409,14 +426,12 @@
 
     def store(place, carry):
         grad = tile_gradient(cot_v, act_v, scale, lax.rem(start + count + place, tiles))
-        for where, piece in pieces(grad, place, per_row, halves):
-            rest_v[where] = piece
+        held = pieces(grad, count + place, per_row, halves)
+        for (where, piece), (there, _) in zip(pieces(grad, place, per_row, halves), held):
+            rest_v[where] = err_v[there] + piece
         return carry
 
     lax.fori_loop(0, tiles - count, store, 0)
-    rest = (tiles - count) * step
-    for half in range(halves):
-        rest_v[half, :rest, :] = rest_v[half, :rest, :] + err_v[half, count * step : tiles * step, :]
     small.wait()
     clear_rows(rest_v, table_s, shards, shards)
     store_memory(rest_v, count, range(count, tiles))
@@ -539,10 +554,10 @@
     own_blocks = nblocks // shards
     per_row = activ.shape[1] // block_len
     scale = activ.shape[1] ** (-0.5)
-    activ, cotangent, error_memory, kept_blocks, kept_counts, gossip_blocks, gossip_counts = (
+    activ, cotangent, error_memory, params, kept_blocks, kept_counts, gossip_blocks, gossip_counts = (
         pltpu.with_memory_space_constraint(array, pltpu.HBM)
         for array in (
-            activ, cotangent, error_memory,
+            activ, cotangent, error_memory, params,
             kept_blocks, kept_counts, gossip_blocks, gossip_counts.reshape(silos),
         )
     )
@@ -550,17 +565,14 @@
         shards, silos, own_blocks, per_row, scale,
         kept_blocks, kept_counts, gossip_blocks, gossip_counts, activ, cotangent, error_memory,
     )
-    outgoing = outgoing_rows(shards, grad_rows, err_rows)
+    *outgoing, grad_v = outgoing_rows(shards, per_row, scale, grad_rows, err_rows, act_v, cot_v)
     arrived = [
         lax.ppermute(rows, "shard", [(r, (r + shift) % shards) for r in range(shards)])
         for shift, rows in enumerate(outgoing, 1)
     ]
-    params, estimate, mixed, row_table = lax.optimization_barrier((params, estimate, mixed, row_table))
-    params, estimate, mixed = (
-        pltpu.with_memory_space_constraint(array, pltpu.VMEM) for array in (params, estimate, mixed)
-    )
-    mine, base, err_v = gradient(
-        shards, per_row, scale, error_memory, params, estimate, own_match, act_v, cot_v, row_table, g_table
+    estimate, mixed = (pltpu.with_memory_space_constraint(array, pltpu.VMEM) for array in (estimate, mixed))
+    mine, base, err_v, params, _ = gradient(
+        shards, per_row, scale, error_memory, params, estimate, own_match, act_v, cot_v, row_table, g_table, grad_v
     )
     delta, again = delta_rows(base, match, arrived)
     first, second = exchange(delta, again, silos)

time: 19.1 us -> 18.7 us (0.979)
  starting transfers between devices: 7.38 us -> 5.76 us
  Pallas kernels: 10.8 us -> 11.8 us
  waiting for transfers between devices: 0.01 us -> 0.33 us
    pallas_call x1, Pallas kernels: 0.01 us -> 1.14 us  [outgoing_rows(): pl.pallas_call(functools.partial(sum_kernel, shards, per_row, scale), nam...]
    ppermute x1, starting transfers between devices: 3 us -> 1.89 us  [body(): lax.ppermute(rows, 'shard', [(r, (r + shift) % shards) for r in range(sha...]
    ppermute x1, starting transfers between devices: 4.37 us -> 3.87 us  [exchange(): far = lax.ppermute(rows, 'silo', routes[0])]
    ppermute x1, waiting for transfers between devices: 0.01 us -> 0.3 us  [exchange(): far = lax.ppermute(rows, 'silo', routes[0])]
  transfers between devices with their start and end apart: 3 -> 3, of which waited for: 0 -> 1; matrix products, arithmetic and copies ran while one was open for 0% -> 0% of each run, Pallas kernels for 31% -> 30%
where the time goes in v5:
time: 18.7 us; the launch traced here: 18.6 us
  Pallas kernels  11.8 us (63%)
  starting transfers between devices  5.76 us (31%)
  between operations  0.68 us (4%)
  waiting for transfers between devices  0.33 us (2%)
    ppermute x1, starting transfers between devices, exchange(): far = lax.ppermute(rows, 'silo', routes[0])  3.87 us
    pallas_call x1, Pallas kernels, own_updates(): pl.pallas_call(functools.partial(own_kernel, shards, per_row, scale), nam...  3.04 us
    pallas_call x1, Pallas kernels, moving_rows(): pl.pallas_call(functools.partial(rows_kernel, shards, silos, own_blocks,...  2.78 us
    pallas_call x1, Pallas kernels, gradient(): pl.pallas_call(functools.partial(gradient_kernel, shards, per_row, scale)...  2.59 us
    pallas_call x1, Pallas kernels, final(): pl.pallas_call(functools.partial(final_kernel, per_row), name='neighbours...  2.08 us
    ppermute x1, starting transfers between devices, body(): lax.ppermute(rows, 'shard', [(r, (r + shift) % shards) for r in range(sha...  1.89 us
    pallas_call x1, Pallas kernels, outgoing_rows(): pl.pallas_call(functools.partial(sum_kernel, shards, per_row, scale), nam...  1.14 us
  transfers between devices with their start and end apart: 3, of which 1 were waited for; matrix products, arithmetic and copies ran while one was open for 0% of the time, Pallas kernels for 30%

profile of v5, /device:TPU:0, one launch (start us, length us, event | category | flops | bytes accessed | tf_op | source)
XLA Modules:
  0.0 18.6 jit_solution(9767559654922033472)
XLA Ops:
  0.6 2.8 %moving_rows.1 = (f32[64,256]{1,0:T(8,128)S(1)}, f32[64,256]{1,0:T(8,128)S(1)}, bf16[1024,1280]{1,0:T(8,128)(2,1)S(1)}, bf16[1024,640]{1,0:T(8,128)(2,1)S(1)}, b...) custom-call(s32[1,2,2,64]{3,2,1,0:T(2,128)} %lists.1, ...), custom_call_target="tpu_custom_call" | custom-call | tf_op jit(solution)/shard_map/moving_rows/pallas_call | solution.py:169
  3.4 0.0 copy-start
  3.4 1.1 %outgoing_rows.1 = (f32[64,256]{1,0:T(8,128)S(1)}, f32[2,1920,128]{2,1,0:T(8,128)S(1)}) custom-call(f32[64,256]{1,0:T(8,128)S(1)} %get-tuple-element.34.grad_rows, f32[64,256]{1,0:T(8,128)S(1)} %get-tuple-element.35.err_rows, bf16[1024,1280]{1,0:T(8,128)(2,1)S(1)} %get-tuple-element.30.act_v, bf16[1024,640]{1,0:T(8,128)(2,1)S(1)} %get-tuple-element.31.cot_v), custom_call_target="tpu_custom_call" | custom-call | flops 10000000000 | bytes 30000000 | tf_op jit(solution)/shard_map/outgoing_rows/pallas_call | solution.py:222
  4.6 1.9 %collective-permute-start = (f32[64,256]{1,0:T(8,128)S(1)}, f32[64,256]{1,0:T(8,128)S(1)}, u32[]{:S(2)}, u32[]{:S(2)}) collective-permute-start(f32[64,256]{1,0:T(8,128)S(1)} %get-tuple-element.43), channel_id=1, source_target_pairs={{0,1},{1,0},{2,3},{3,2},{4,5},{5,4},{6,7},{7,6},{8,9},{9,8},{10,11... | collective-permute-start | bytes 196616 | tf_op jit(solution)/shard_map/ppermute | solution.py:570
  6.5 0.0 copy-done
  6.5 0.0 copy-start.1
  6.5 2.6 %gradient.1 = (f32[64,256]{1,0:T(8,128)S(1)}, f32[128,256]{1,0:T(8,128)S(1)}, f32[2,3208,128]{2,1,0:T(8,128)S(1)}, f32[1,320,1280]{2,1,0:T(8,128)S(1)}, f32[2,1920,128]{2,1,0:T(8,128)S(1)}) custom-call(f32[1,1,3200,256]{3,2,1,0:T(8,128)} %err.3, f32[1,320,1280]{2,1,0:T(8,128)} %params.1, ...), custom_call_target="tpu_custom_call", output_to_operand_aliasing={{4}: (8, {})} | custom-call | tf_op jit(solution)/shard_map/gradient/pallas_call | solution.py:351
  9.1 0.0 collective-permute-done.refs_0_.refs_1_
  9.1 0.2 delta_rows.1
  9.3 3.9 %collective-permute-start.1 = (f32[136,256]{1,0:T(8,128)S(1)}, f32[136,256]{1,0:T(8,128)S(1)}, u32[]{:S(2)}, u32[]{:S(2)}) collective-permute-start(f32[136,256]{1,0:T(8,128)S(1)} %get-tuple-element.49), channel_id=1, source_target_pairs={{0,30},{2,4},{4,2},{6,8},{8,6},{10,12},{12,10},{14,16},{16,14},{18... | collective-permute-start | bytes 417800 | tf_op jit(solution)/shard_map/ppermute | solution.py:542
  13.1 0.0 collective-permute-start.2
  13.1 0.0 copy-done.1
  13.1 3.0 %own_updates.1 = (f32[1,1,3200,256]{3,2,1,0:T(8,128)}, f32[1,320,1280]{2,1,0:T(8,128)}, f32[320,1280]{1,0:T(8,128)S(1)}, f32[320,1280]{1,0:T(8,128)S(1)}) custom-call(f32[1,320,1280]{2,1,0:T(8,128)S(1)} %get-tuple-element.37.p_v, f32[1,320,1280]{2,1,0:T(8,128)S(1)} %copy-done, f32[1,320,1280]{2,1,0:T(8,128)S(1)} %copy-done.1, ...), custom_call_target="tpu_custom_call" | custom-call | tf_op jit(solution)/shard_map/own_updates/pallas_call | solution.py:465
  16.2 0.0 collective-permute-done.2.second
  16.2 0.3 %collective-permute-done.1.first = f32[136,256]{1,0:T(8,128)S(1)} collective-permute-done((f32[136,256]{1,0:T(8,128)S(1)}, f32[136,256]{1,0:T(8,128)S(1)}, u32[]{:S(2)}, u32[]{:S(2)}) %collective-permute-start.1) | collective-permute-done | bytes 139296 | tf_op jit(solution)/shard_map/ppermute | solution.py:542
  16.5 2.1 %neighbours.1 = (f32[1,320,1280]{2,1,0:T(8,128)}, f32[1,320,1280]{2,1,0:T(8,128)}) custom-call(f32[320,1280]{1,0:T(8,128)S(1)} %get-tuple-element.46.mixed_pre, f32[320,1280]{1,0:T(8,128)S(1)} %get-tuple-element.47.params_pre, bf16[1600,256]{1,0:T(8,128)(2,1)S(1)} %get-tuple-element.48.spread, f32[136,256]{1,0:T(8,128)S(1)} %collective-permute-done.1.first, ...), custom_call_target="tpu_custom_call" | custom-call | tf_op jit(solution)/shard_map/neighbours/pallas_call | solution.py:511
Async XLA Ops:
  3.4 3.1 %copy-start = (f32[1,320,1280]{2,1,0:T(8,128)S(1)}, f32[1,320,1280]{2,1,0:T(8,128)}, u32[]{:S(2)}) copy-start(f32[1,320,1280]{2,1,0:T(8,128)} %e_v.3) | copy-start | bytes 4915204
  4.6 4.5 %collective-permute-start = (f32[64,256]{1,0:T(8,128)S(1)}, f32[64,256]{1,0:T(8,128)S(1)}, u32[]{:S(2)}, u32[]{:S(2)}) collective-permute-start(f32[64,256]{1,0:T(8,128)S(1)} %get-tuple-element.43), channel_id=1, source_target_pairs={{0,1},{1,0},{2,3},{3,2},{4,5},{5,4},{6,7},{7,6},{8,9},{9,8},{10,11... | collective-permute-start | bytes 196616 | tf_op jit(solution)/shard_map/ppermute | solution.py:570
  6.5 6.7 %copy-start.1 = (f32[1,320,1280]{2,1,0:T(8,128)S(1)}, f32[1,320,1280]{2,1,0:T(8,128)}, u32[]{:S(2)}) copy-start(f32[1,320,1280]{2,1,0:T(8,128)} %m_v.1) | copy-start | bytes 4915204
  9.3 7.2 %collective-permute-start.1 = (f32[136,256]{1,0:T(8,128)S(1)}, f32[136,256]{1,0:T(8,128)S(1)}, u32[]{:S(2)}, u32[]{:S(2)}) collective-permute-start(f32[136,256]{1,0:T(8,128)S(1)} %get-tuple-element.49), channel_id=1, source_target_pairs={{0,30},{2,4},{4,2},{6,8},{8,6},{10,12},{12,10},{14,16},{16,14},{18... | collective-permute-start | bytes 417800 | tf_op jit(solution)/shard_map/ppermute | solution.py:542
  13.1 3.1 %collective-permute-start.2 = (f32[128,256]{1,0:T(8,128)S(1)}, f32[128,256]{1,0:T(8,128)S(1)}, u32[]{:S(2)}, u32[]{:S(2)}) collective-permute-start(f32[128,256]{1,0:T(8,128)S(1)} %get-tuple-element.44.delta), channel_id=1, source_target_pairs={{0,2},{2,0},{4,6},{6,4},{8,10},{10,8},{12,14},{14,12},{16,18},{18,... | collective-permute-start | bytes 393224 | tf_op jit(solution)/shard_map/ppermute | solution.py:543

commit v6 on v5

--- a/solution.py
+++ b/solution.py
@@ -196,7 +196,11 @@
 
 
 def early_tiles(me, silo):
-    return jnp.where((me == 0) & (silo < 2), 2, 0)
+    return jnp.where((me == 0) & (silo < 2), 1, 0)
+
+
+def tiles_by_then(silo, count, tiles):
+    return jnp.where(silo == 1, tiles, count)
 
 
 def sum_kernel(shards, per_row, scale, grad_rows, err_rows, act_v, cot_v, *outs):
@@ -225,7 +229,7 @@
         in_specs=[IN_VMEM] * 4,
         out_specs=[IN_VMEM] * shards,
         out_shape=[pltpu.VMEM(shape, F32)] * (shards - 1)
-        + [pltpu.VMEM((shape[1] // 128, owner_tiles(shards, cot_v.shape[1]) * TILE * per_row, 128), F32)],
+        + [pltpu.VMEM((shape[1] // 128, cot_v.shape[1] * per_row, 128), F32)],
         compiler_params=pltpu.CompilerParams(vmem_limit_bytes=8 * MIB),
         cost_estimate=pl.CostEstimate(flops=10**10, bytes_accessed=3 * 10**7, transcendentals=0),
     )(grad_rows, err_rows, act_v, cot_v)
@@ -303,15 +307,18 @@
     other_memory = load(range(count, tiles), 3 + halves)
 
     def store(place, carry):
-        for where, piece in pieces(tile_gradient(cot_v, act_v, scale, start + place), place, per_row, halves):
+        grad = tile_gradient(cot_v, act_v, scale, lax.rem(start + place, tiles))
+        for where, piece in pieces(grad, place, per_row, halves):
             grad_v[where] = piece
         return carry
 
-    lax.fori_loop(early_tiles(me, lax.axis_index("silo")), count, store, 0)
+    silo = lax.axis_index("silo")
+    lax.fori_loop(early_tiles(me, silo), tiles_by_then(silo, count, tiles), store, 0)
     for copy in small + own_memory:
         copy.wait()
+    done = count * step
     for half in range(halves):
-        err_v[half, : count * step, :] = err_v[half, : count * step, :] + grad_v[half]
+        err_v[half, :done, :] = err_v[half, :done, :] + grad_v[half, :done, :]
         err_v[half, tiles * step :, :] = jnp.zeros((8, 128), F32)
 
     def take(slot, carry):
@@ -388,13 +395,14 @@
         in_specs=[IN_VMEM] * (2 + len(arrived)),
         out_specs=[IN_VMEM] * 2,
         out_shape=[pltpu.VMEM((base.shape[0] + 8, base.shape[1]), F32), pltpu.VMEM(base.shape, F32)],
+        cost_estimate=pl.CostEstimate(flops=10**10, bytes_accessed=3 * 10**7, transcendentals=0),
         compiler_params=pltpu.CompilerParams(vmem_limit_bytes=8 * MIB),
     )(base, match, *arrived)
 
 
 def own_kernel(
     shards, per_row, scale,
-    p_v, e_v, m_v, err_v, act_v, cot_v, row_table, kept_hot, own_hot, delta, *refs
+    p_v, e_v, m_v, err_v, grad_v, act_v, cot_v, row_table, kept_hot, own_hot, delta, *refs
 ):
     kept = refs[:shards]
     err_out, est_out, mixed_pre, params_pre, table_s, rest_v, est_v, sems = refs[shards:]
@@ -431,7 +439,15 @@
             rest_v[where] = err_v[there] + piece
         return carry
 
-    lax.fori_loop(0, tiles - count, store, 0)
+    by_then = tiles_by_then(lax.axis_index("silo"), count, tiles)
+
+    @pl.when(by_then == tiles)
+    def _():
+        for half in range(halves):
+            rows = slice(count * step, tiles * step)
+            rest_v[half, : (tiles - count) * step, :] = err_v[half, rows, :] + grad_v[half, rows, :]
+
+    lax.fori_loop(0, tiles - by_then, store, 0)
     small.wait()
     clear_rows(rest_v, table_s, shards, shards)
     store_memory(rest_v, count, range(count, tiles))
@@ -457,7 +473,7 @@
 
 
 def own_updates(
-    shards, per_row, scale, err_shape, params, estimate, mixed, err_v, act_v, cot_v, row_table, kept_hot, own_hot, delta, kept
+    shards, per_row, scale, err_shape, params, estimate, mixed, err_v, grad_v, act_v, cot_v, row_table, kept_hot, own_hot, delta, kept
 ):
     owned = mixed.shape[1:]
     halves = err_v.shape[0]
@@ -465,7 +481,7 @@
     return pl.pallas_call(
         functools.partial(own_kernel, shards, per_row, scale),
         name="own_updates",
-        in_specs=[IN_VMEM] * (10 + shards),
+        in_specs=[IN_VMEM] * (11 + shards),
         out_specs=[ANY, ANY, IN_VMEM, IN_VMEM],
         out_shape=[
             pltpu.HBM(err_shape, F32),
@@ -480,7 +496,7 @@
             pltpu.SemaphoreType.DMA((1 + halves + per_row,)),
         ],
         compiler_params=pltpu.CompilerParams(vmem_limit_bytes=16 * MIB),
-    )(params, estimate, mixed, err_v, act_v, cot_v, row_table, kept_hot, own_hot, delta, *kept)
+    )(params, estimate, mixed, err_v, grad_v, act_v, cot_v, row_table, kept_hot, own_hot, delta, *kept)
 
 
 def final_kernel(per_row, mixed_pre, params_pre, spread, first, second, mixed_out, params_out, m_v, p_v, sems):
@@ -571,14 +587,14 @@
         for shift, rows in enumerate(outgoing, 1)
     ]
     estimate, mixed = (pltpu.with_memory_space_constraint(array, pltpu.VMEM) for array in (estimate, mixed))
-    mine, base, err_v, params, _ = gradient(
+    mine, base, err_v, params, grad_v = gradient(
         shards, per_row, scale, error_memory, params, estimate, own_match, act_v, cot_v, row_table, g_table, grad_v
     )
     delta, again = delta_rows(base, match, arrived)
     first, second = exchange(delta, again, silos)
     error_out, estimate_out, mixed_pre, params_pre = own_updates(
         shards, per_row, scale, error_memory.shape, params, estimate, mixed,
-        err_v, act_v, cot_v, row_table, kept_hot, own_hot, again, [mine, *arrived],
+        err_v, grad_v, act_v, cot_v, row_table, kept_hot, own_hot, again, [mine, *arrived],
     )
     mixed_out, params_out = final(per_row, mixed.shape, mixed_pre, params_pre, spread, first, second)
     return params_out, estimate_out, mixed_out, error_out

time: 18.7 us -> 18.7 us (level)
  Pallas kernels: 11.8 us -> 11.2 us
  starting transfers between devices: 5.76 us -> 6.35 us
    pallas_call x1, Pallas kernels: 1.14 us -> 0.58 us  [outgoing_rows(): pl.pallas_call(functools.partial(sum_kernel, shards, per_row, scale), nam...]
    ppermute x1, starting transfers between devices: 1.89 us -> 2.45 us  [body(): lax.ppermute(rows, 'shard', [(r, (r + shift) % shards) for r in range(sha...]
where the time goes in v6:
time: 18.7 us; the launch traced here: 18.5 us
  Pallas kernels  11.2 us (60%)
  starting transfers between devices  6.35 us (34%)
  between operations  0.7 us (4%)
  waiting for transfers between devices  0.3 us (2%)
    ppermute x1, starting transfers between devices, exchange(): far = lax.ppermute(rows, 'silo', routes[0])  3.89 us
    pallas_call x1, Pallas kernels, own_updates(): pl.pallas_call(functools.partial(own_kernel, shards, per_row, scale), nam...  3.03 us
    pallas_call x1, Pallas kernels, moving_rows(): pl.pallas_call(functools.partial(rows_kernel, shards, silos, own_blocks,...  2.78 us
    pallas_call x1, Pallas kernels, gradient(): pl.pallas_call(functools.partial(gradient_kernel, shards, per_row, scale)...  2.54 us
    ppermute x1, starting transfers between devices, body(): lax.ppermute(rows, 'shard', [(r, (r + shift) % shards) for r in range(sha...  2.45 us
    pallas_call x1, Pallas kernels, final(): pl.pallas_call(functools.partial(final_kernel, per_row), name='neighbours...  2.07 us
    pallas_call x1, Pallas kernels, outgoing_rows(): pl.pallas_call(functools.partial(sum_kernel, shards, per_row, scale), nam...  0.58 us
  transfers between devices with their start and end apart: 3, of which 1 were waited for; matrix products, arithmetic and copies ran while one was open for 0% of the time, Pallas kernels for 30%

profile of v6, /device:TPU:0, one launch (start us, length us, event | category | flops | bytes accessed | tf_op | source)
XLA Modules:
  0.0 18.5 jit_solution(11506868327024662680)
XLA Ops:
  0.6 2.8 %moving_rows.1 = (f32[64,256]{1,0:T(8,128)S(1)}, f32[64,256]{1,0:T(8,128)S(1)}, bf16[1024,1280]{1,0:T(8,128)(2,1)S(1)}, bf16[1024,640]{1,0:T(8,128)(2,1)S(1)}, b...) custom-call(s32[1,2,2,64]{3,2,1,0:T(2,128)} %lists.1, ...), custom_call_target="tpu_custom_call" | custom-call | tf_op jit(solution)/shard_map/moving_rows/pallas_call | solution.py:169
  3.4 0.0 copy-start
  3.4 0.6 %outgoing_rows.1 = (f32[64,256]{1,0:T(8,128)S(1)}, f32[2,3200,128]{2,1,0:T(8,128)S(1)}) custom-call(f32[64,256]{1,0:T(8,128)S(1)} %get-tuple-element.35.grad_rows, f32[64,256]{1,0:T(8,128)S(1)} %get-tuple-element.36.err_rows, bf16[1024,1280]{1,0:T(8,128)(2,1)S(1)} %get-tuple-element.31.act_v, bf16[1024,640]{1,0:T(8,128)(2,1)S(1)} %get-tuple-element.32.cot_v), custom_call_target="tpu_custom_call" | custom-call | flops 10000000000 | bytes 30000000 | tf_op jit(solution)/shard_map/outgoing_rows/pallas_call | solution.py:226
  4.0 2.5 %collective-permute-start = (f32[64,256]{1,0:T(8,128)S(1)}, f32[64,256]{1,0:T(8,128)S(1)}, u32[]{:S(2)}, u32[]{:S(2)}) collective-permute-start(f32[64,256]{1,0:T(8,128)S(1)} %get-tuple-element.45), channel_id=1, source_target_pairs={{0,1},{1,0},{2,3},{3,2},{4,5},{5,4},{6,7},{7,6},{8,9},{9,8},{10,11... | collective-permute-start | bytes 196616 | tf_op jit(solution)/shard_map/ppermute | solution.py:586
  6.5 0.0 copy-done
  6.5 2.5 %gradient.1 = (f32[64,256]{1,0:T(8,128)S(1)}, f32[128,256]{1,0:T(8,128)S(1)}, f32[2,3208,128]{2,1,0:T(8,128)S(1)}, f32[1,320,1280]{2,1,0:T(8,128)S(1)}, f32[2,3200,128]{2,1,0:T(8,128)S(1)}) custom-call(f32[1,1,3200,256]{3,2,1,0:T(8,128)} %err.3, f32[1,320,1280]{2,1,0:T(8,128)} %params.1, ...), custom_call_target="tpu_custom_call", output_to_operand_aliasing={{4}: (8, {})} | custom-call | tf_op jit(solution)/shard_map/gradient/pallas_call | solution.py:358
  9.0 0.0 collective-permute-done.refs_0_.refs_1_
  9.0 0.0 copy-start.1
  9.0 0.2 delta_rows.1
  9.2 3.9 %collective-permute-start.1 = (f32[136,256]{1,0:T(8,128)S(1)}, f32[136,256]{1,0:T(8,128)S(1)}, u32[]{:S(2)}, u32[]{:S(2)}) collective-permute-start(f32[136,256]{1,0:T(8,128)S(1)} %get-tuple-element.51), channel_id=1, source_target_pairs={{0,30},{2,4},{4,2},{6,8},{8,6},{10,12},{12,10},{14,16},{16,14},{18... | collective-permute-start | bytes 417800 | tf_op jit(solution)/shard_map/ppermute | solution.py:558
  13.1 0.0 collective-permute-start.2
  13.1 0.0 copy-done.1
  13.1 3.0 %own_updates.1 = (f32[1,1,3200,256]{3,2,1,0:T(8,128)}, f32[1,320,1280]{2,1,0:T(8,128)}, f32[320,1280]{1,0:T(8,128)S(1)}, f32[320,1280]{1,0:T(8,128)S(1)}) custom-call(f32[1,320,1280]{2,1,0:T(8,128)S(1)} %get-tuple-element.38.p_v, f32[1,320,1280]{2,1,0:T(8,128)S(1)} %copy-done, f32[1,320,1280]{2,1,0:T(8,128)S(1)} %copy-done.1, ...), custom_call_target="tpu_custom_call" | custom-call | tf_op jit(solution)/shard_map/own_updates/pallas_call | solution.py:481
  16.1 0.0 collective-permute-done.2.second
  16.1 0.3 %collective-permute-done.1.first = f32[136,256]{1,0:T(8,128)S(1)} collective-permute-done((f32[136,256]{1,0:T(8,128)S(1)}, f32[136,256]{1,0:T(8,128)S(1)}, u32[]{:S(2)}, u32[]{:S(2)}) %collective-permute-start.1) | collective-permute-done | bytes 139296 | tf_op jit(solution)/shard_map/ppermute | solution.py:558
  16.4 2.1 %neighbours.1 = (f32[1,320,1280]{2,1,0:T(8,128)}, f32[1,320,1280]{2,1,0:T(8,128)}) custom-call(f32[320,1280]{1,0:T(8,128)S(1)} %get-tuple-element.48.mixed_pre, f32[320,1280]{1,0:T(8,128)S(1)} %get-tuple-element.49.params_pre, bf16[1600,256]{1,0:T(8,128)(2,1)S(1)} %get-tuple-element.50.spread, f32[136,256]{1,0:T(8,128)S(1)} %collective-permute-done.1.first, ...), custom_call_target="tpu_custom_call" | custom-call | tf_op jit(solution)/shard_map/neighbours/pallas_call | solution.py:527
Async XLA Ops:
  3.4 3.1 %copy-start = (f32[1,320,1280]{2,1,0:T(8,128)S(1)}, f32[1,320,1280]{2,1,0:T(8,128)}, u32[]{:S(2)}) copy-start(f32[1,320,1280]{2,1,0:T(8,128)} %e_v.3) | copy-start | bytes 4915204
  4.0 5.0 %collective-permute-start = (f32[64,256]{1,0:T(8,128)S(1)}, f32[64,256]{1,0:T(8,128)S(1)}, u32[]{:S(2)}, u32[]{:S(2)}) collective-permute-start(f32[64,256]{1,0:T(8,128)S(1)} %get-tuple-element.45), channel_id=1, source_target_pairs={{0,1},{1,0},{2,3},{3,2},{4,5},{5,4},{6,7},{7,6},{8,9},{9,8},{10,11... | collective-permute-start | bytes 196616 | tf_op jit(solution)/shard_map/ppermute | solution.py:586
  9.0 4.1 %copy-start.1 = (f32[1,320,1280]{2,1,0:T(8,128)S(1)}, f32[1,320,1280]{2,1,0:T(8,128)}, u32[]{:S(2)}) copy-start(f32[1,320,1280]{2,1,0:T(8,128)} %m_v.1) | copy-start | bytes 4915204
  9.2 7.2 %collective-permute-start.1 = (f32[136,256]{1,0:T(8,128)S(1)}, f32[136,256]{1,0:T(8,128)S(1)}, u32[]{:S(2)}, u32[]{:S(2)}) collective-permute-start(f32[136,256]{1,0:T(8,128)S(1)} %get-tuple-element.51), channel_id=1, source_target_pairs={{0,30},{2,4},{4,2},{6,8},{8,6},{10,12},{12,10},{14,16},{16,14},{18... | collective-permute-start | bytes 417800 | tf_op jit(solution)/shard_map/ppermute | solution.py:558
  13.1 3.1 %collective-permute-start.2 = (f32[128,256]{1,0:T(8,128)S(1)}, f32[128,256]{1,0:T(8,128)S(1)}, u32[]{:S(2)}, u32[]{:S(2)}) collective-permute-start(f32[128,256]{1,0:T(8,128)S(1)} %get-tuple-element.46.delta), channel_id=1, source_target_pairs={{0,2},{2,0},{4,6},{6,4},{8,10},{10,8},{12,14},{14,12},{16,18},{18,... | collective-permute-start | bytes 393224 | tf_op jit(solution)/shard_map/ppermute | solution.py:559

commit v7 on v6

--- a/solution.py
+++ b/solution.py
@@ -31,6 +31,12 @@
 def split(rows):
     high = rows.astype(BF16)
     return jnp.concatenate([high, (rows - high.astype(F32)).astype(BF16)], axis=0)
+
+
+def exact_pick(choice, rows):
+    high = rows.astype(BF16)
+    rest = rows - high.astype(F32)
+    return dot(choice, high) + pick(choice, split(rest))
 
 
 def pick(choice, rows):
@@ -229,7 +235,7 @@
         in_specs=[IN_VMEM] * 4,
         out_specs=[IN_VMEM] * shards,
         out_shape=[pltpu.VMEM(shape, F32)] * (shards - 1)
-        + [pltpu.VMEM((shape[1] // 128, cot_v.shape[1] * per_row, 128), F32)],
+        + [pltpu.VMEM((shape[1] // 128, cot_v.shape[1] * per_row + 8, 128), F32)],
         compiler_params=pltpu.CompilerParams(vmem_limit_bytes=8 * MIB),
         cost_estimate=pl.CostEstimate(flops=10**10, bytes_accessed=3 * 10**7, transcendentals=0),
     )(grad_rows, err_rows, act_v, cot_v)
@@ -453,12 +459,11 @@
     store_memory(rest_v, count, range(count, tiles))
 
     kept_parts = split(jnp.concatenate([rows[...] for rows in kept], axis=0))
-    delta_parts = split(delta[...])
     for part in range(per_row):
         lanes = slice(part * width, (part + 1) * width)
         blocks = slice(part * out_rows, (part + 1) * out_rows)
         grad = pick(kept_hot[blocks, :], kept_parts)
-        change = pick(own_hot[blocks, :], delta_parts)
+        change = exact_pick(own_hot[blocks, :], delta[...])
         half_step = p_v[0, :, lanes] - LEARN_RATE * grad
         est = e_v[0, :, lanes] + change
         mix = m_v[0, :, lanes] + MIX_WEIGHT * change

time: 18.7 us -> 18.7 us (level)
  waiting for transfers between devices: 0.3 us -> 0.01 us
  Pallas kernels: 11.2 us -> 11.4 us
    pallas_call x1, Pallas kernels: 3.03 us -> 3.33 us  [own_updates(): pl.pallas_call(functools.partial(own_kernel, shards, per_row, scale), nam...]
    ppermute x1, waiting for transfers between devices: 0.29 us -> 0.01 us  [exchange(): far = lax.ppermute(rows, 'silo', routes[0])]
  transfers between devices with their start and end apart: 3 -> 3, of which waited for: 1 -> 0; matrix products, arithmetic and copies ran while one was open for 0% -> 0% of each run, Pallas kernels for 30% -> 32%
where the time goes in v7:
time: 18.7 us; the launch traced here: 18.6 us
  Pallas kernels  11.4 us (61%)
  starting transfers between devices  6.39 us (34%)
  between operations  0.71 us (4%)
    ppermute x1, starting transfers between devices, exchange(): far = lax.ppermute(rows, 'silo', routes[0])  3.94 us
    pallas_call x1, Pallas kernels, own_updates(): pl.pallas_call(functools.partial(own_kernel, shards, per_row, scale), nam...  3.33 us
    pallas_call x1, Pallas kernels, moving_rows(): pl.pallas_call(functools.partial(rows_kernel, shards, silos, own_blocks,...  2.78 us
    pallas_call x1, Pallas kernels, gradient(): pl.pallas_call(functools.partial(gradient_kernel, shards, per_row, scale)...  2.54 us
    ppermute x1, starting transfers between devices, body(): lax.ppermute(rows, 'shard', [(r, (r + shift) % shards) for r in range(sha...  2.45 us
    pallas_call x1, Pallas kernels, final(): pl.pallas_call(functools.partial(final_kernel, per_row), name='neighbours...  2.06 us
    pallas_call x1, Pallas kernels, outgoing_rows(): pl.pallas_call(functools.partial(sum_kernel, shards, per_row, scale), nam...  0.58 us
  transfers between devices with their start and end apart: 3, of which 0 were waited for; matrix products, arithmetic and copies ran while one was open for 0% of the time, Pallas kernels for 32%

profile of v7, /device:TPU:0, one launch (start us, length us, event | category | flops | bytes accessed | tf_op | source)
XLA Modules:
  0.0 18.6 jit_solution(9726690523332359667)
XLA Ops:
  0.6 2.8 %moving_rows.1 = (f32[64,256]{1,0:T(8,128)S(1)}, f32[64,256]{1,0:T(8,128)S(1)}, bf16[1024,1280]{1,0:T(8,128)(2,1)S(1)}, bf16[1024,640]{1,0:T(8,128)(2,1)S(1)}, b...) custom-call(s32[1,2,2,64]{3,2,1,0:T(2,128)} %lists.1, ...), custom_call_target="tpu_custom_call" | custom-call | tf_op jit(solution)/shard_map/moving_rows/pallas_call | solution.py:175
  3.4 0.0 copy-start
  3.4 0.6 %outgoing_rows.1 = (f32[64,256]{1,0:T(8,128)S(1)}, f32[2,3208,128]{2,1,0:T(8,128)S(1)}) custom-call(f32[64,256]{1,0:T(8,128)S(1)} %get-tuple-element.35.grad_rows, f32[64,256]{1,0:T(8,128)S(1)} %get-tuple-element.36.err_rows, bf16[1024,1280]{1,0:T(8,128)(2,1)S(1)} %get-tuple-element.31.act_v, bf16[1024,640]{1,0:T(8,128)(2,1)S(1)} %get-tuple-element.32.cot_v), custom_call_target="tpu_custom_call" | custom-call | flops 10000000000 | bytes 30000000 | tf_op jit(solution)/shard_map/outgoing_rows/pallas_call | solution.py:232
  4.0 2.5 %collective-permute-start = (f32[64,256]{1,0:T(8,128)S(1)}, f32[64,256]{1,0:T(8,128)S(1)}, u32[]{:S(2)}, u32[]{:S(2)}) collective-permute-start(f32[64,256]{1,0:T(8,128)S(1)} %get-tuple-element.45), channel_id=1, source_target_pairs={{0,1},{1,0},{2,3},{3,2},{4,5},{5,4},{6,7},{7,6},{8,9},{9,8},{10,11... | collective-permute-start | bytes 196616 | tf_op jit(solution)/shard_map/ppermute | solution.py:591
  6.5 0.0 copy-done
  6.5 2.5 %gradient.1 = (f32[64,256]{1,0:T(8,128)S(1)}, f32[128,256]{1,0:T(8,128)S(1)}, f32[2,3208,128]{2,1,0:T(8,128)S(1)}, f32[1,320,1280]{2,1,0:T(8,128)S(1)}, f32[2,3208,128]{2,1,0:T(8,128)S(1)}) custom-call(f32[1,1,3200,256]{3,2,1,0:T(8,128)} %err.3, f32[1,320,1280]{2,1,0:T(8,128)} %params.1, ...), custom_call_target="tpu_custom_call", output_to_operand_aliasing={{4}: (8, {})} | custom-call | tf_op jit(solution)/shard_map/gradient/pallas_call | solution.py:364
  9.0 0.0 collective-permute-done.refs_0_.refs_1_
  9.0 0.0 copy-start.1
  9.0 0.2 delta_rows.1
  9.2 3.9 %collective-permute-start.1 = (f32[136,256]{1,0:T(8,128)S(1)}, f32[136,256]{1,0:T(8,128)S(1)}, u32[]{:S(2)}, u32[]{:S(2)}) collective-permute-start(f32[136,256]{1,0:T(8,128)S(1)} %get-tuple-element.51), channel_id=1, source_target_pairs={{0,30},{2,4},{4,2},{6,8},{8,6},{10,12},{12,10},{14,16},{16,14},{18... | collective-permute-start | bytes 417800 | tf_op jit(solution)/shard_map/ppermute | solution.py:563
  13.1 0.0 collective-permute-start.2
  13.1 0.0 copy-done.1
  13.1 3.3 %own_updates.1 = (f32[1,1,3200,256]{3,2,1,0:T(8,128)}, f32[1,320,1280]{2,1,0:T(8,128)}, f32[320,1280]{1,0:T(8,128)S(1)}, f32[320,1280]{1,0:T(8,128)S(1)}) custom-call(f32[1,320,1280]{2,1,0:T(8,128)S(1)} %get-tuple-element.38.p_v, f32[1,320,1280]{2,1,0:T(8,128)S(1)} %copy-done, f32[1,320,1280]{2,1,0:T(8,128)S(1)} %copy-done.1, ...), custom_call_target="tpu_custom_call" | custom-call | tf_op jit(solution)/shard_map/own_updates/pallas_call | solution.py:486
  16.5 0.0 collective-permute-done.2.second
  16.5 0.0 collective-permute-done.1.first
  16.5 2.1 %neighbours.1 = (f32[1,320,1280]{2,1,0:T(8,128)}, f32[1,320,1280]{2,1,0:T(8,128)}) custom-call(f32[320,1280]{1,0:T(8,128)S(1)} %get-tuple-element.48.mixed_pre, f32[320,1280]{1,0:T(8,128)S(1)} %get-tuple-element.49.params_pre, bf16[1600,256]{1,0:T(8,128)(2,1)S(1)} %get-tuple-element.50.spread, f32[136,256]{1,0:T(8,128)S(1)} %collective-permute-done.1.first, ...), custom_call_target="tpu_custom_call" | custom-call | tf_op jit(solution)/shard_map/neighbours/pallas_call | solution.py:532
Async XLA Ops:
  3.4 3.1 %copy-start = (f32[1,320,1280]{2,1,0:T(8,128)S(1)}, f32[1,320,1280]{2,1,0:T(8,128)}, u32[]{:S(2)}) copy-start(f32[1,320,1280]{2,1,0:T(8,128)} %e_v.3) | copy-start | bytes 4915204
  4.0 5.0 %collective-permute-start = (f32[64,256]{1,0:T(8,128)S(1)}, f32[64,256]{1,0:T(8,128)S(1)}, u32[]{:S(2)}, u32[]{:S(2)}) collective-permute-start(f32[64,256]{1,0:T(8,128)S(1)} %get-tuple-element.45), channel_id=1, source_target_pairs={{0,1},{1,0},{2,3},{3,2},{4,5},{5,4},{6,7},{7,6},{8,9},{9,8},{10,11... | collective-permute-start | bytes 196616 | tf_op jit(solution)/shard_map/ppermute | solution.py:591
  9.0 4.1 %copy-start.1 = (f32[1,320,1280]{2,1,0:T(8,128)S(1)}, f32[1,320,1280]{2,1,0:T(8,128)}, u32[]{:S(2)}) copy-start(f32[1,320,1280]{2,1,0:T(8,128)} %m_v.1) | copy-start | bytes 4915204
  9.2 7.3 %collective-permute-start.1 = (f32[136,256]{1,0:T(8,128)S(1)}, f32[136,256]{1,0:T(8,128)S(1)}, u32[]{:S(2)}, u32[]{:S(2)}) collective-permute-start(f32[136,256]{1,0:T(8,128)S(1)} %get-tuple-element.51), channel_id=1, source_target_pairs={{0,30},{2,4},{4,2},{6,8},{8,6},{10,12},{12,10},{14,16},{16,14},{18... | collective-permute-start | bytes 417800 | tf_op jit(solution)/shard_map/ppermute | solution.py:563
  13.1 3.3 %collective-permute-start.2 = (f32[128,256]{1,0:T(8,128)S(1)}, f32[128,256]{1,0:T(8,128)S(1)}, u32[]{:S(2)}, u32[]{:S(2)}) collective-permute-start(f32[128,256]{1,0:T(8,128)S(1)} %get-tuple-element.46.delta), channel_id=1, source_target_pairs={{0,2},{2,0},{4,6},{6,4},{8,10},{10,8},{12,14},{14,12},{16,18},{18,... | collective-permute-start | bytes 393224 | tf_op jit(solution)/shard_map/ppermute | solution.py:564

commit v8 on v6

--- a/solution.py
+++ b/solution.py
@@ -136,12 +136,12 @@
     chunks = per_row * width // 128
     row = divide(g_v[silo], per_row)
     place = (g_v[silo] - row * per_row) * (width // 128 * out_rows) + row
-    sent = lax.broadcasted_iota(I32, (1, g_slots), 1) < gc_s[silo]
-    g_table[...] = jnp.where(sent, place, chunks * out_rows)
+    sent_row = lax.broadcasted_iota(I32, (1, g_slots), 1) < gc_s[silo]
+    g_table[...] = jnp.where(sent_row, place, chunks * out_rows)
     first, second = neighbours(silo, silos)
     for ids, into in (
         (jnp.concatenate(senders, axis=1), kept_hot),
-        (g_v[silo], own_hot),
+        (jnp.where(sent_row, g_v[silo], -1), own_hot),
         (jnp.concatenate([g_v[first], g_v[second]], axis=1), spread),
     ):
         for part in range(per_row):
@@ -229,7 +229,7 @@
         in_specs=[IN_VMEM] * 4,
         out_specs=[IN_VMEM] * shards,
         out_shape=[pltpu.VMEM(shape, F32)] * (shards - 1)
-        + [pltpu.VMEM((shape[1] // 128, cot_v.shape[1] * per_row, 128), F32)],
+        + [pltpu.VMEM((shape[1] // 128, cot_v.shape[1] * per_row + 8, 128), F32)],
         compiler_params=pltpu.CompilerParams(vmem_limit_bytes=8 * MIB),
         cost_estimate=pl.CostEstimate(flops=10**10, bytes_accessed=3 * 10**7, transcendentals=0),
     )(grad_rows, err_rows, act_v, cot_v)
@@ -402,12 +402,12 @@
 
 def own_kernel(
     shards, per_row, scale,
-    p_v, e_v, m_v, err_v, grad_v, act_v, cot_v, row_table, kept_hot, own_hot, delta, *refs
+    p_v, e_v, m_v, err_v, grad_v, act_v, cot_v, row_table, kept_hot, own_hot, _, *refs
 ):
     kept = refs[:shards]
     err_out, est_out, mixed_pre, params_pre, table_s, rest_v, est_v, sems = refs[shards:]
     me = lax.axis_index("shard")
-    width = delta.shape[1]
+    width = kept[0].shape[1]
     halves = err_v.shape[0]
     out_rows = p_v.shape[1]
     step = TILE * per_row
@@ -453,13 +453,14 @@
     store_memory(rest_v, count, range(count, tiles))
 
     kept_parts = split(jnp.concatenate([rows[...] for rows in kept], axis=0))
-    delta_parts = split(delta[...])
+    ones = jnp.ones((own_hot.shape[1], width), BF16)
     for part in range(per_row):
         lanes = slice(part * width, (part + 1) * width)
         blocks = slice(part * out_rows, (part + 1) * out_rows)
         grad = pick(kept_hot[blocks, :], kept_parts)
-        change = pick(own_hot[blocks, :], delta_parts)
         half_step = p_v[0, :, lanes] - LEARN_RATE * grad
+        gossiped = dot(own_hot[blocks, :], ones) > 0.0
+        change = jnp.where(gossiped, half_step - e_v[0, :, lanes], 0.0)
         est = e_v[0, :, lanes] + change
         mix = m_v[0, :, lanes] + MIX_WEIGHT * change
         est_v[:, lanes] = est

time: 18.7 us -> 18.7 us (level)
  transfers between devices with their start and end apart: 3 -> 3, of which waited for: 1 -> 1; matrix products, arithmetic and copies ran while one was open for 0% -> 0% of each run, Pallas kernels for 30% -> 31%
where the time goes in v8:
time: 18.7 us; the launch traced here: 18.5 us
  Pallas kernels  11.3 us (60%)
  starting transfers between devices  6.4 us (34%)
  between operations  0.7 us (4%)
    ppermute x1, starting transfers between devices, exchange(): far = lax.ppermute(rows, 'silo', routes[0])  3.95 us
    pallas_call x1, Pallas kernels, own_updates(): pl.pallas_call(functools.partial(own_kernel, shards, per_row, scale), nam...  3.15 us
    pallas_call x1, Pallas kernels, moving_rows(): pl.pallas_call(functools.partial(rows_kernel, shards, silos, own_blocks,...  2.78 us
    pallas_call x1, Pallas kernels, gradient(): pl.pallas_call(functools.partial(gradient_kernel, shards, per_row, scale)...  2.54 us
    ppermute x1, starting transfers between devices, body(): lax.ppermute(rows, 'shard', [(r, (r + shift) % shards) for r in range(sha...  2.44 us
    pallas_call x1, Pallas kernels, final(): pl.pallas_call(functools.partial(final_kernel, per_row), name='neighbours...  2.06 us
    pallas_call x1, Pallas kernels, outgoing_rows(): pl.pallas_call(functools.partial(sum_kernel, shards, per_row, scale), nam...  0.59 us
  transfers between devices with their start and end apart: 3, of which 1 were waited for; matrix products, arithmetic and copies ran while one was open for 0% of the time, Pallas kernels for 31%

profile of v8, /device:TPU:0, one launch (start us, length us, event | category | flops | bytes accessed | tf_op | source)
XLA Modules:
  0.0 18.5 jit_solution(6339806932512858466)
XLA Ops:
  0.6 2.8 %moving_rows.1 = (f32[64,256]{1,0:T(8,128)S(1)}, f32[64,256]{1,0:T(8,128)S(1)}, bf16[1024,1280]{1,0:T(8,128)(2,1)S(1)}, bf16[1024,640]{1,0:T(8,128)(2,1)S(1)}, b...) custom-call(s32[1,2,2,64]{3,2,1,0:T(2,128)} %lists.1, ...), custom_call_target="tpu_custom_call" | custom-call | tf_op jit(solution)/shard_map/moving_rows/pallas_call | solution.py:169
  3.4 0.0 copy-start
  3.4 0.6 %outgoing_rows.1 = (f32[64,256]{1,0:T(8,128)S(1)}, f32[2,3208,128]{2,1,0:T(8,128)S(1)}) custom-call(f32[64,256]{1,0:T(8,128)S(1)} %get-tuple-element.35.grad_rows, f32[64,256]{1,0:T(8,128)S(1)} %get-tuple-element.36.err_rows, bf16[1024,1280]{1,0:T(8,128)(2,1)S(1)} %get-tuple-element.31.act_v, bf16[1024,640]{1,0:T(8,128)(2,1)S(1)} %get-tuple-element.32.cot_v), custom_call_target="tpu_custom_call" | custom-call | flops 10000000000 | bytes 30000000 | tf_op jit(solution)/shard_map/outgoing_rows/pallas_call | solution.py:226
  4.0 2.4 %collective-permute-start = (f32[64,256]{1,0:T(8,128)S(1)}, f32[64,256]{1,0:T(8,128)S(1)}, u32[]{:S(2)}, u32[]{:S(2)}) collective-permute-start(f32[64,256]{1,0:T(8,128)S(1)} %get-tuple-element.45), channel_id=1, source_target_pairs={{0,1},{1,0},{2,3},{3,2},{4,5},{5,4},{6,7},{7,6},{8,9},{9,8},{10,11... | collective-permute-start | bytes 196616 | tf_op jit(solution)/shard_map/ppermute | solution.py:587
  6.5 0.0 copy-done
  6.5 2.5 %gradient.1 = (f32[64,256]{1,0:T(8,128)S(1)}, f32[128,256]{1,0:T(8,128)S(1)}, f32[2,3208,128]{2,1,0:T(8,128)S(1)}, f32[1,320,1280]{2,1,0:T(8,128)S(1)}, f32[2,3208,128]{2,1,0:T(8,128)S(1)}) custom-call(f32[1,1,3200,256]{3,2,1,0:T(8,128)} %err.3, f32[1,320,1280]{2,1,0:T(8,128)} %params.1, ...), custom_call_target="tpu_custom_call", output_to_operand_aliasing={{4}: (8, {})} | custom-call | tf_op jit(solution)/shard_map/gradient/pallas_call | solution.py:358
  9.0 0.0 collective-permute-done.refs_0_.refs_1_
  9.0 0.0 copy-start.1
  9.0 0.2 delta_rows.1
  9.2 4.0 %collective-permute-start.1 = (f32[136,256]{1,0:T(8,128)S(1)}, f32[136,256]{1,0:T(8,128)S(1)}, u32[]{:S(2)}, u32[]{:S(2)}) collective-permute-start(f32[136,256]{1,0:T(8,128)S(1)} %get-tuple-element.51), channel_id=1, source_target_pairs={{0,30},{2,4},{4,2},{6,8},{8,6},{10,12},{12,10},{14,16},{16,14},{18... | collective-permute-start | bytes 417800 | tf_op jit(solution)/shard_map/ppermute | solution.py:559
  13.2 0.0 collective-permute-start.2
  13.2 0.0 copy-done.1
  13.2 3.2 %own_updates.1 = (f32[1,1,3200,256]{3,2,1,0:T(8,128)}, f32[1,320,1280]{2,1,0:T(8,128)}, f32[320,1280]{1,0:T(8,128)S(1)}, f32[320,1280]{1,0:T(8,128)S(1)}) custom-call(f32[1,320,1280]{2,1,0:T(8,128)S(1)} %get-tuple-element.38.p_v, f32[1,320,1280]{2,1,0:T(8,128)S(1)} %copy-done, f32[1,320,1280]{2,1,0:T(8,128)S(1)} %copy-done.1, ...), custom_call_target="tpu_custom_call" | custom-call | tf_op jit(solution)/shard_map/own_updates/pallas_call | solution.py:482
  16.3 0.0 collective-permute-done.2.second
  16.3 0.1 collective-permute-done.1.first
  16.4 2.1 %neighbours.1 = (f32[1,320,1280]{2,1,0:T(8,128)}, f32[1,320,1280]{2,1,0:T(8,128)}) custom-call(f32[320,1280]{1,0:T(8,128)S(1)} %get-tuple-element.48.mixed_pre, f32[320,1280]{1,0:T(8,128)S(1)} %get-tuple-element.49.params_pre, bf16[1600,256]{1,0:T(8,128)(2,1)S(1)} %get-tuple-element.50.spread, f32[136,256]{1,0:T(8,128)S(1)} %collective-permute-done.1.first, ...), custom_call_target="tpu_custom_call" | custom-call | tf_op jit(solution)/shard_map/neighbours/pallas_call | solution.py:528
Async XLA Ops:
  3.4 3.1 %copy-start = (f32[1,320,1280]{2,1,0:T(8,128)S(1)}, f32[1,320,1280]{2,1,0:T(8,128)}, u32[]{:S(2)}) copy-start(f32[1,320,1280]{2,1,0:T(8,128)} %e_v.3) | copy-start | bytes 4915204
  4.0 5.0 %collective-permute-start = (f32[64,256]{1,0:T(8,128)S(1)}, f32[64,256]{1,0:T(8,128)S(1)}, u32[]{:S(2)}, u32[]{:S(2)}) collective-permute-start(f32[64,256]{1,0:T(8,128)S(1)} %get-tuple-element.45), channel_id=1, source_target_pairs={{0,1},{1,0},{2,3},{3,2},{4,5},{5,4},{6,7},{7,6},{8,9},{9,8},{10,11... | collective-permute-start | bytes 196616 | tf_op jit(solution)/shard_map/ppermute | solution.py:587
  9.0 4.1 %copy-start.1 = (f32[1,320,1280]{2,1,0:T(8,128)S(1)}, f32[1,320,1280]{2,1,0:T(8,128)}, u32[]{:S(2)}) copy-start(f32[1,320,1280]{2,1,0:T(8,128)} %m_v.1) | copy-start | bytes 4915204
  9.2 7.2 %collective-permute-start.1 = (f32[136,256]{1,0:T(8,128)S(1)}, f32[136,256]{1,0:T(8,128)S(1)}, u32[]{:S(2)}, u32[]{:S(2)}) collective-permute-start(f32[136,256]{1,0:T(8,128)S(1)} %get-tuple-element.51), channel_id=1, source_target_pairs={{0,30},{2,4},{4,2},{6,8},{8,6},{10,12},{12,10},{14,16},{16,14},{18... | collective-permute-start | bytes 417800 | tf_op jit(solution)/shard_map/ppermute | solution.py:559
  13.2 3.2 %collective-permute-start.2 = (f32[128,256]{1,0:T(8,128)S(1)}, f32[128,256]{1,0:T(8,128)S(1)}, u32[]{:S(2)}, u32[]{:S(2)}) collective-permute-start(f32[128,256]{1,0:T(8,128)S(1)} %get-tuple-element.46._), channel_id=1, source_target_pairs={{0,2},{2,0},{4,6},{6,4},{8,10},{10,8},{12,14},{14,12},{16,18},{18,... | collective-permute-start | bytes 393224 | tf_op jit(solution)/shard_map/ppermute | solution.py:560

commit v9 on v8

--- a/solution.py
+++ b/solution.py
@@ -229,7 +229,7 @@
         in_specs=[IN_VMEM] * 4,
         out_specs=[IN_VMEM] * shards,
         out_shape=[pltpu.VMEM(shape, F32)] * (shards - 1)
-        + [pltpu.VMEM((shape[1] // 128, cot_v.shape[1] * per_row + 8, 128), F32)],
+        + [pltpu.VMEM((shape[1] // 128, TILE * per_row + 8, 128), F32)],
         compiler_params=pltpu.CompilerParams(vmem_limit_bytes=8 * MIB),
         cost_estimate=pl.CostEstimate(flops=10**10, bytes_accessed=3 * 10**7, transcendentals=0),
     )(grad_rows, err_rows, act_v, cot_v)
@@ -277,7 +277,7 @@
 
 def gradient_kernel(
     shards, per_row, scale,
-    err, params, e_v, own_match, act_v, cot_v, row_table, g_table, _,
+    err, params, e_v, own_match, act_v, cot_v, row_table, g_table, early_v,
     mine, base, err_v, p_v, grad_v, table_s, g_s, rows_v, drift_v, sems,
 ):
     me = lax.axis_index("shard")
@@ -317,8 +317,19 @@
     for copy in small + own_memory:
         copy.wait()
     done = count * step
+
+    @pl.when(early_tiles(me, silo) > 0)
+    def _():
+        for half in range(halves):
+            err_v[half, :step, :] = err_v[half, :step, :] + early_v[half, :step, :]
+
+    @pl.when(early_tiles(me, silo) == 0)
+    def _():
+        for half in range(halves):
+            err_v[half, :step, :] = err_v[half, :step, :] + grad_v[half, :step, :]
+
     for half in range(halves):
-        err_v[half, :done, :] = err_v[half, :done, :] + grad_v[half, :done, :]
+        err_v[half, step:done, :] = err_v[half, step:done, :] + grad_v[half, step:done, :]
         err_v[half, tiles * step :, :] = jnp.zeros((8, 128), F32)
 
     def take(slot, carry):
@@ -349,7 +360,7 @@
         copy.wait()
 
 
-def gradient(shards, per_row, scale, err, params, estimate, own_match, act_v, cot_v, row_table, g_table, grad_v):
+def gradient(shards, per_row, scale, err, params, estimate, own_match, act_v, cot_v, row_table, g_table, early_v):
     slots = row_table.shape[1]
     g_slots = own_match.shape[0]
     nblocks, width = err.shape[2:]
@@ -365,9 +376,8 @@
             pltpu.VMEM((g_slots, width), F32),
             pltpu.VMEM((halves, nblocks + 8, 128), F32),
             pltpu.VMEM(params.shape, F32),
-            pltpu.VMEM(grad_v.shape, F32),
+            pltpu.VMEM((halves, nblocks + 8, 128), F32),
         ],
-        input_output_aliases={8: 4},
         scratch_shapes=[
             pltpu.SMEM(row_table.shape, I32),
             pltpu.SMEM(g_table.shape, I32),
@@ -376,7 +386,7 @@
             pltpu.SemaphoreType.DMA((3 + 2 * halves,)),
         ],
         compiler_params=pltpu.CompilerParams(vmem_limit_bytes=16 * MIB),
-    )(err, params, estimate, own_match, act_v, cot_v, row_table, g_table, grad_v)
+    )(err, params, estimate, own_match, act_v, cot_v, row_table, g_table, early_v)
 
 
 def delta_kernel(base, match, *refs):
@@ -582,14 +592,14 @@
         shards, silos, own_blocks, per_row, scale,
         kept_blocks, kept_counts, gossip_blocks, gossip_counts, activ, cotangent, error_memory,
     )
-    *outgoing, grad_v = outgoing_rows(shards, per_row, scale, grad_rows, err_rows, act_v, cot_v)
+    *outgoing, early_v = outgoing_rows(shards, per_row, scale, grad_rows, err_rows, act_v, cot_v)
     arrived = [
         lax.ppermute(rows, "shard", [(r, (r + shift) % shards) for r in range(shards)])
         for shift, rows in enumerate(outgoing, 1)
     ]
     estimate, mixed = (pltpu.with_memory_space_constraint(array, pltpu.VMEM) for array in (estimate, mixed))
     mine, base, err_v, params, grad_v = gradient(
-        shards, per_row, scale, error_memory, params, estimate, own_match, act_v, cot_v, row_table, g_table, grad_v
+        shards, per_row, scale, error_memory, params, estimate, own_match, act_v, cot_v, row_table, g_table, early_v
     )
     delta, again = delta_rows(base, match, arrived)
     first, second = exchange(delta, again, silos)

time: 18.7 us -> 18.6 us (level)
  transfers between devices with their start and end apart: 3 -> 3, of which waited for: 1 -> 1; matrix products, arithmetic and copies ran while one was open for 0% -> 0% of each run, Pallas kernels for 31% -> 30%
where the time goes in v9:
time: 18.6 us; the launch traced here: 18.5 us
  Pallas kernels  11.2 us (60%)
  starting transfers between devices  6.4 us (34%)
  between operations  0.7 us (4%)
    ppermute x1, starting transfers between devices, exchange(): far = lax.ppermute(rows, 'silo', routes[0])  3.95 us
    pallas_call x1, Pallas kernels, own_updates(): pl.pallas_call(functools.partial(own_kernel, shards, per_row, scale), nam...  3.15 us
    pallas_call x1, Pallas kernels, moving_rows(): pl.pallas_call(functools.partial(rows_kernel, shards, silos, own_blocks,...  2.78 us
    pallas_call x1, Pallas kernels, gradient(): pl.pallas_call(functools.partial(gradient_kernel, shards, per_row, scale)...  2.49 us
    ppermute x1, starting transfers between devices, body(): lax.ppermute(rows, 'shard', [(r, (r + shift) % shards) for r in range(sha...  2.46 us
    pallas_call x1, Pallas kernels, final(): pl.pallas_call(functools.partial(final_kernel, per_row), name='neighbours...  2.05 us
    pallas_call x1, Pallas kernels, outgoing_rows(): pl.pallas_call(functools.partial(sum_kernel, shards, per_row, scale), nam...  0.58 us
  transfers between devices with their start and end apart: 3, of which 1 were waited for; matrix products, arithmetic and copies ran while one was open for 0% of the time, Pallas kernels for 30%

profile of v9, /device:TPU:0, one launch (start us, length us, event | category | flops | bytes accessed | tf_op | source)
XLA Modules:
  0.0 18.5 jit_solution(10076800277277026668)
XLA Ops:
  0.6 2.8 %moving_rows.1 = (f32[64,256]{1,0:T(8,128)S(1)}, f32[64,256]{1,0:T(8,128)S(1)}, bf16[1024,1280]{1,0:T(8,128)(2,1)S(1)}, bf16[1024,640]{1,0:T(8,128)(2,1)S(1)}, b...) custom-call(s32[1,2,2,64]{3,2,1,0:T(2,128)} %lists.1, ...), custom_call_target="tpu_custom_call" | custom-call | tf_op jit(solution)/shard_map/moving_rows/pallas_call | solution.py:169
  3.4 0.0 copy-start
  3.4 0.6 %outgoing_rows.1 = (f32[64,256]{1,0:T(8,128)S(1)}, f32[2,648,128]{2,1,0:T(8,128)S(1)}) custom-call(f32[64,256]{1,0:T(8,128)S(1)} %get-tuple-element.35.grad_rows, f32[64,256]{1,0:T(8,128)S(1)} %get-tuple-element.36.err_rows, bf16[1024,1280]{1,0:T(8,128)(2,1)S(1)} %get-tuple-element.31.act_v, bf16[1024,640]{1,0:T(8,128)(2,1)S(1)} %get-tuple-element.32.cot_v), custom_call_target="tpu_custom_call" | custom-call | flops 10000000000 | bytes 30000000 | tf_op jit(solution)/shard_map/outgoing_rows/pallas_call | solution.py:226
  4.0 2.5 %collective-permute-start = (f32[64,256]{1,0:T(8,128)S(1)}, f32[64,256]{1,0:T(8,128)S(1)}, u32[]{:S(2)}, u32[]{:S(2)}) collective-permute-start(f32[64,256]{1,0:T(8,128)S(1)} %get-tuple-element.45), channel_id=1, source_target_pairs={{0,1},{1,0},{2,3},{3,2},{4,5},{5,4},{6,7},{7,6},{8,9},{9,8},{10,11... | collective-permute-start | bytes 196616 | tf_op jit(solution)/shard_map/ppermute | solution.py:597
  6.5 0.0 copy-done
  6.5 2.5 %gradient.1 = (f32[64,256]{1,0:T(8,128)S(1)}, f32[128,256]{1,0:T(8,128)S(1)}, f32[2,3208,128]{2,1,0:T(8,128)S(1)}, f32[1,320,1280]{2,1,0:T(8,128)S(1)}, f32[2,3208,128]{2,1,0:T(8,128)S(1)}) custom-call(f32[1,1,3200,256]{3,2,1,0:T(8,128)} %err.3, f32[1,320,1280]{2,1,0:T(8,128)} %params.1, f32[1,320,1280]{2,1,0:T(8,128)S(1)} %copy-done, ...), custom_call_target="tpu_custom_call" | custom-call | tf_op jit(solution)/shard_map/gradient/pallas_call | solution.py:369
  9.0 0.0 collective-permute-done.refs_0_.refs_1_
  9.0 0.0 copy-start.1
  9.0 0.2 delta_rows.1
  9.2 3.9 %collective-permute-start.1 = (f32[136,256]{1,0:T(8,128)S(1)}, f32[136,256]{1,0:T(8,128)S(1)}, u32[]{:S(2)}, u32[]{:S(2)}) collective-permute-start(f32[136,256]{1,0:T(8,128)S(1)} %get-tuple-element.51), channel_id=1, source_target_pairs={{0,30},{2,4},{4,2},{6,8},{8,6},{10,12},{12,10},{14,16},{16,14},{18... | collective-permute-start | bytes 417800 | tf_op jit(solution)/shard_map/ppermute | solution.py:569
  13.1 0.0 collective-permute-start.2
  13.1 0.0 copy-done.1
  13.1 3.1 %own_updates.1 = (f32[1,1,3200,256]{3,2,1,0:T(8,128)}, f32[1,320,1280]{2,1,0:T(8,128)}, f32[320,1280]{1,0:T(8,128)S(1)}, f32[320,1280]{1,0:T(8,128)S(1)}) custom-call(f32[1,320,1280]{2,1,0:T(8,128)S(1)} %get-tuple-element.38.p_v, f32[1,320,1280]{2,1,0:T(8,128)S(1)} %copy-done, f32[1,320,1280]{2,1,0:T(8,128)S(1)} %copy-done.1, ...), custom_call_target="tpu_custom_call" | custom-call | tf_op jit(solution)/shard_map/own_updates/pallas_call | solution.py:492
  16.3 0.0 collective-permute-done.2.second
  16.3 0.1 collective-permute-done.1.first
  16.4 2.1 %neighbours.1 = (f32[1,320,1280]{2,1,0:T(8,128)}, f32[1,320,1280]{2,1,0:T(8,128)}) custom-call(f32[320,1280]{1,0:T(8,128)S(1)} %get-tuple-element.48.mixed_pre, f32[320,1280]{1,0:T(8,128)S(1)} %get-tuple-element.49.params_pre, bf16[1600,256]{1,0:T(8,128)(2,1)S(1)} %get-tuple-element.50.spread, f32[136,256]{1,0:T(8,128)S(1)} %collective-permute-done.1.first, ...), custom_call_target="tpu_custom_call" | custom-call | tf_op jit(solution)/shard_map/neighbours/pallas_call | solution.py:538
Async XLA Ops:
  3.4 3.1 %copy-start = (f32[1,320,1280]{2,1,0:T(8,128)S(1)}, f32[1,320,1280]{2,1,0:T(8,128)}, u32[]{:S(2)}) copy-start(f32[1,320,1280]{2,1,0:T(8,128)} %e_v.3) | copy-start | bytes 4915204
  4.0 5.0 %collective-permute-start = (f32[64,256]{1,0:T(8,128)S(1)}, f32[64,256]{1,0:T(8,128)S(1)}, u32[]{:S(2)}, u32[]{:S(2)}) collective-permute-start(f32[64,256]{1,0:T(8,128)S(1)} %get-tuple-element.45), channel_id=1, source_target_pairs={{0,1},{1,0},{2,3},{3,2},{4,5},{5,4},{6,7},{7,6},{8,9},{9,8},{10,11... | collective-permute-start | bytes 196616 | tf_op jit(solution)/shard_map/ppermute | solution.py:597
  9.0 4.1 %copy-start.1 = (f32[1,320,1280]{2,1,0:T(8,128)S(1)}, f32[1,320,1280]{2,1,0:T(8,128)}, u32[]{:S(2)}) copy-start(f32[1,320,1280]{2,1,0:T(8,128)} %m_v.1) | copy-start | bytes 4915204
  9.2 7.2 %collective-permute-start.1 = (f32[136,256]{1,0:T(8,128)S(1)}, f32[136,256]{1,0:T(8,128)S(1)}, u32[]{:S(2)}, u32[]{:S(2)}) collective-permute-start(f32[136,256]{1,0:T(8,128)S(1)} %get-tuple-element.51), channel_id=1, source_target_pairs={{0,30},{2,4},{4,2},{6,8},{8,6},{10,12},{12,10},{14,16},{16,14},{18... | collective-permute-start | bytes 417800 | tf_op jit(solution)/shard_map/ppermute | solution.py:569
  13.1 3.2 %collective-permute-start.2 = (f32[128,256]{1,0:T(8,128)S(1)}, f32[128,256]{1,0:T(8,128)S(1)}, u32[]{:S(2)}, u32[]{:S(2)}) collective-permute-start(f32[128,256]{1,0:T(8,128)S(1)} %get-tuple-element.46._), channel_id=1, source_target_pairs={{0,2},{2,0},{4,6},{6,4},{8,10},{10,8},{12,14},{14,12},{16,18},{18,... | collective-permute-start | bytes 393224 | tf_op jit(solution)/shard_map/ppermute | solution.py:570

commit v10 on v9

--- a/solution.py
+++ b/solution.py
@@ -83,9 +83,7 @@
     ]
     for copy in [*small, cot_copy, *act_copies]:
         copy.start()
-    for copy in small:
-        copy.wait()
-
+    small[0].wait()
     columns, fills = [], []
     for shift in range(1, shards):
         owner = lax.rem(me + shift, shards)
@@ -97,6 +95,10 @@
             return carry
 
         lax.fori_loop(0, slots, fetch, 0, unroll=slots)
+    for copy in small[1:]:
+        copy.wait()
+    for shift in range(1, shards):
+        owner = lax.rem(me + shift, shards)
         row = lists_v[me, pl.ds(owner, 1), :] + owner * own_blocks
         columns.append(as_column(row))
         slot_ids = lax.broadcasted_iota(I32, (slots, 1), 0)

time: 18.6 us -> 18.7 us (level)
  no operation moved by 1% of the time
where the time goes in v10:
time: 18.7 us; the launch traced here: 18.5 us
  Pallas kernels  11.3 us (60%)
  starting transfers between devices  6.41 us (34%)
  between operations  0.7 us (4%)
    ppermute x1, starting transfers between devices, exchange(): far = lax.ppermute(rows, 'silo', routes[0])  3.95 us
    pallas_call x1, Pallas kernels, own_updates(): pl.pallas_call(functools.partial(own_kernel, shards, per_row, scale), nam...  3.15 us
    pallas_call x1, Pallas kernels, moving_rows(): pl.pallas_call(functools.partial(rows_kernel, shards, silos, own_blocks,...  2.83 us
    pallas_call x1, Pallas kernels, gradient(): pl.pallas_call(functools.partial(gradient_kernel, shards, per_row, scale)...  2.49 us
    ppermute x1, starting transfers between devices, body(): lax.ppermute(rows, 'shard', [(r, (r + shift) % shards) for r in range(sha...  2.46 us
    pallas_call x1, Pallas kernels, final(): pl.pallas_call(functools.partial(final_kernel, per_row), name='neighbours...  2.06 us
    pallas_call x1, Pallas kernels, outgoing_rows(): pl.pallas_call(functools.partial(sum_kernel, shards, per_row, scale), nam...  0.57 us
  transfers between devices with their start and end apart: 3, of which 1 were waited for; matrix products, arithmetic and copies ran while one was open for 0% of the time, Pallas kernels for 30%

profile of v10, /device:TPU:0, one launch (start us, length us, event | category | flops | bytes accessed | tf_op | source)
XLA Modules:
  0.0 18.5 jit_solution(12692376060700365959)
XLA Ops:
  0.6 2.8 %moving_rows.1 = (f32[64,256]{1,0:T(8,128)S(1)}, f32[64,256]{1,0:T(8,128)S(1)}, bf16[1024,1280]{1,0:T(8,128)(2,1)S(1)}, bf16[1024,640]{1,0:T(8,128)(2,1)S(1)}, b...) custom-call(s32[1,2,2,64]{3,2,1,0:T(2,128)} %lists.1, ...), custom_call_target="tpu_custom_call" | custom-call | tf_op jit(solution)/shard_map/moving_rows/pallas_call | solution.py:171
  3.5 0.0 copy-start
  3.5 0.6 %outgoing_rows.1 = (f32[64,256]{1,0:T(8,128)S(1)}, f32[2,648,128]{2,1,0:T(8,128)S(1)}) custom-call(f32[64,256]{1,0:T(8,128)S(1)} %get-tuple-element.35.grad_rows, f32[64,256]{1,0:T(8,128)S(1)} %get-tuple-element.36.err_rows, bf16[1024,1280]{1,0:T(8,128)(2,1)S(1)} %get-tuple-element.31.act_v, bf16[1024,640]{1,0:T(8,128)(2,1)S(1)} %get-tuple-element.32.cot_v), custom_call_target="tpu_custom_call" | custom-call | flops 10000000000 | bytes 30000000 | tf_op jit(solution)/shard_map/outgoing_rows/pallas_call | solution.py:228
  4.1 2.5 %collective-permute-start = (f32[64,256]{1,0:T(8,128)S(1)}, f32[64,256]{1,0:T(8,128)S(1)}, u32[]{:S(2)}, u32[]{:S(2)}) collective-permute-start(f32[64,256]{1,0:T(8,128)S(1)} %get-tuple-element.45), channel_id=1, source_target_pairs={{0,1},{1,0},{2,3},{3,2},{4,5},{5,4},{6,7},{7,6},{8,9},{9,8},{10,11... | collective-permute-start | bytes 196616 | tf_op jit(solution)/shard_map/ppermute | solution.py:599
  6.5 0.0 copy-done
  6.5 2.5 %gradient.1 = (f32[64,256]{1,0:T(8,128)S(1)}, f32[128,256]{1,0:T(8,128)S(1)}, f32[2,3208,128]{2,1,0:T(8,128)S(1)}, f32[1,320,1280]{2,1,0:T(8,128)S(1)}, f32[2,3208,128]{2,1,0:T(8,128)S(1)}) custom-call(f32[1,1,3200,256]{3,2,1,0:T(8,128)} %err.3, f32[1,320,1280]{2,1,0:T(8,128)} %params.1, f32[1,320,1280]{2,1,0:T(8,128)S(1)} %copy-done, ...), custom_call_target="tpu_custom_call" | custom-call | tf_op jit(solution)/shard_map/gradient/pallas_call | solution.py:371
  9.0 0.0 collective-permute-done.refs_0_.refs_1_
  9.0 0.0 copy-start.1
  9.0 0.2 delta_rows.1
  9.2 3.9 %collective-permute-start.1 = (f32[136,256]{1,0:T(8,128)S(1)}, f32[136,256]{1,0:T(8,128)S(1)}, u32[]{:S(2)}, u32[]{:S(2)}) collective-permute-start(f32[136,256]{1,0:T(8,128)S(1)} %get-tuple-element.51), channel_id=1, source_target_pairs={{0,30},{2,4},{4,2},{6,8},{8,6},{10,12},{12,10},{14,16},{16,14},{18... | collective-permute-start | bytes 417800 | tf_op jit(solution)/shard_map/ppermute | solution.py:571
  13.2 0.0 collective-permute-start.2
  13.2 0.0 copy-done.1
  13.2 3.1 %own_updates.1 = (f32[1,1,3200,256]{3,2,1,0:T(8,128)}, f32[1,320,1280]{2,1,0:T(8,128)}, f32[320,1280]{1,0:T(8,128)S(1)}, f32[320,1280]{1,0:T(8,128)S(1)}) custom-call(f32[1,320,1280]{2,1,0:T(8,128)S(1)} %get-tuple-element.38.p_v, f32[1,320,1280]{2,1,0:T(8,128)S(1)} %copy-done, f32[1,320,1280]{2,1,0:T(8,128)S(1)} %copy-done.1, ...), custom_call_target="tpu_custom_call" | custom-call | tf_op jit(solution)/shard_map/own_updates/pallas_call | solution.py:494
  16.3 0.0 collective-permute-done.2.second
  16.3 0.1 collective-permute-done.1.first
  16.4 2.1 %neighbours.1 = (f32[1,320,1280]{2,1,0:T(8,128)}, f32[1,320,1280]{2,1,0:T(8,128)}) custom-call(f32[320,1280]{1,0:T(8,128)S(1)} %get-tuple-element.48.mixed_pre, f32[320,1280]{1,0:T(8,128)S(1)} %get-tuple-element.49.params_pre, bf16[1600,256]{1,0:T(8,128)(2,1)S(1)} %get-tuple-element.50.spread, f32[136,256]{1,0:T(8,128)S(1)} %collective-permute-done.1.first, ...), custom_call_target="tpu_custom_call" | custom-call | tf_op jit(solution)/shard_map/neighbours/pallas_call | solution.py:540
Async XLA Ops:
  3.5 3.1 %copy-start = (f32[1,320,1280]{2,1,0:T(8,128)S(1)}, f32[1,320,1280]{2,1,0:T(8,128)}, u32[]{:S(2)}) copy-start(f32[1,320,1280]{2,1,0:T(8,128)} %e_v.3) | copy-start | bytes 4915204
  4.1 5.0 %collective-permute-start = (f32[64,256]{1,0:T(8,128)S(1)}, f32[64,256]{1,0:T(8,128)S(1)}, u32[]{:S(2)}, u32[]{:S(2)}) collective-permute-start(f32[64,256]{1,0:T(8,128)S(1)} %get-tuple-element.45), channel_id=1, source_target_pairs={{0,1},{1,0},{2,3},{3,2},{4,5},{5,4},{6,7},{7,6},{8,9},{9,8},{10,11... | collective-permute-start | bytes 196616 | tf_op jit(solution)/shard_map/ppermute | solution.py:599
  9.0 4.1 %copy-start.1 = (f32[1,320,1280]{2,1,0:T(8,128)S(1)}, f32[1,320,1280]{2,1,0:T(8,128)}, u32[]{:S(2)}) copy-start(f32[1,320,1280]{2,1,0:T(8,128)} %m_v.1) | copy-start | bytes 4915204
  9.2 7.2 %collective-permute-start.1 = (f32[136,256]{1,0:T(8,128)S(1)}, f32[136,256]{1,0:T(8,128)S(1)}, u32[]{:S(2)}, u32[]{:S(2)}) collective-permute-start(f32[136,256]{1,0:T(8,128)S(1)} %get-tuple-element.51), channel_id=1, source_target_pairs={{0,30},{2,4},{4,2},{6,8},{8,6},{10,12},{12,10},{14,16},{16,14},{18... | collective-permute-start | bytes 417800 | tf_op jit(solution)/shard_map/ppermute | solution.py:571
  13.2 3.2 %collective-permute-start.2 = (f32[128,256]{1,0:T(8,128)S(1)}, f32[128,256]{1,0:T(8,128)S(1)}, u32[]{:S(2)}, u32[]{:S(2)}) collective-permute-start(f32[128,256]{1,0:T(8,128)S(1)} %get-tuple-element.46._), channel_id=1, source_target_pairs={{0,2},{2,0},{4,6},{6,4},{8,10},{10,8},{12,14},{14,12},{16,18},{18,... | collective-permute-start | bytes 393224 | tf_op jit(solution)/shard_map/ppermute | solution.py:572
